TPU v7x, 32 devices: a whole 2x2x4 slice. The times are simulated.
32 devices in a mesh: dp: 8 (over z, x), tensor: 4 (over y, core).
Axes of the slice: x: 2, y: 2, z: 4, core: 2. Of those that a mesh axis runs over, the one named last changes fastest.
Arguments:
- states_in: float32 [8192, 1536], P(('dp', 'tensor')), may hold values from -6 to 6
- documents: int32 [8192], P('dp'), may hold values from 0 to 2, as said below
- attnorm_one: float32 [1536], P('dp'), may hold values from 0.1 to 1.9
- query_one: float32 [1536, 1536], P('dp', 'tensor'), may hold values from -0.15625 to 0.15625
- key_one: float32 [1536, 768], P('dp', 'tensor'), may hold values from -0.15625 to 0.15625
- value_one: float32 [1536, 768], P('dp', 'tensor'), may hold values from -0.15625 to 0.15625
- output_one: float32 [1536, 1536], P('tensor', 'dp'), may hold values from -1.75 to 1.75
- mlpnorm_one: float32 [1536], P('dp'), may hold values from 0.1 to 1.9
- gate_one: float32 [1536, 4096], P('dp', 'tensor'), may hold values from -0.15625 to 0.15625
- up_one: float32 [1536, 4096], P('dp', 'tensor'), may hold values from -0.15625 to 0.15625
- down_one: float32 [4096, 1536], P('tensor', 'dp'), may hold values from -0.125 to 0.125
- attnorm_two: float32 [1536], P('dp'), may hold values from 0.1 to 1.9
- query_two: float32 [1536, 1536], P('dp', 'tensor'), may hold values from -0.15625 to 0.15625
- key_two: float32 [1536, 768], P('dp', 'tensor'), may hold values from -0.15625 to 0.15625
- value_two: float32 [1536, 768], P('dp', 'tensor'), may hold values from -0.15625 to 0.15625
- output_two: float32 [1536, 1536], P('tensor', 'dp'), may hold values from -1.75 to 1.75
- mlpnorm_two: float32 [1536], P('dp'), may hold values from 0.1 to 1.9
- gate_two: float32 [1536, 4096], P('dp', 'tensor'), may hold values from -0.15625 to 0.15625
- up_two: float32 [1536, 4096], P('dp', 'tensor'), may hold values from -0.15625 to 0.15625
- down_two: float32 [4096, 1536], P('tensor', 'dp'), may hold values from -0.09375 to 0.09375
- cotangent: float32 [8192, 1536], P(('dp', 'tensor')), may hold values from -6 to 6
Outputs:
- states_out: float32 [8192, 1536], P(('dp', 'tensor'))
- grad_input: float32 [8192, 1536], P(('dp', 'tensor'))
- dattnorm_one: float32 [1536], P('dp')
- dquery_one: float32 [1536, 1536], P('dp', 'tensor')
- dkey_one: float32 [1536, 768], P('dp', 'tensor')
- dvalue_one: float32 [1536, 768], P('dp', 'tensor')
- doutput_one: float32 [1536, 1536], P('tensor', 'dp')
- dmlpnorm_one: float32 [1536], P('dp')
- dgate_one: float32 [1536, 4096], P('dp', 'tensor')
- dup_one: float32 [1536, 4096], P('dp', 'tensor')
- ddown_one: float32 [4096, 1536], P('tensor', 'dp')
- dattnorm_two: float32 [1536], P('dp')
- dquery_two: float32 [1536, 1536], P('dp', 'tensor')
- dkey_two: float32 [1536, 768], P('dp', 'tensor')
- dvalue_two: float32 [1536, 768], P('dp', 'tensor')
- doutput_two: float32 [1536, 1536], P('tensor', 'dp')
- dmlpnorm_two: float32 [1536], P('dp')
- dgate_two: float32 [1536, 4096], P('dp', 'tensor')
- dup_two: float32 [1536, 4096], P('dp', 'tensor')
- ddown_two: float32 [4096, 1536], P('tensor', 'dp')
Inputs may be any that keep to these rules, and one draw needn't show every extreme that they name: In each aligned run of 1024 tokens the document numbers are 0, 1, 2 in order, never falling; documents 0 and 2 each have 1 to 127 tokens.
All inputs are finite; a program needn't handle non-finite values.
Results may differ from a plain program's by a relative error of at most 0.035.
Values may be sent and summed in bfloat16 or wider, within the bound.
A program may use at most 256 MiB of HBM per device.

v0:
```python
import math

import jax
import jax.numpy as jnp
from jax import lax
from jax.sharding import PartitionSpec as P

HEAD_DIM = 96
BLOCK = 256


epsilon = 1e-05
rope_base = 100000.0
masked_value = -1e30


def dot_rows(left, right):
    return lax.dot_general(
        left, right, (((0,), (0,)), ((), ())), preferred_element_type=jnp.float32
    )


def dot_cols(left, right):
    return lax.dot_general(
        left, right, (((1,), (1,)), ((), ())), preferred_element_type=jnp.float32
    )


def normalize(values):
    factor = lax.rsqrt(jnp.mean(values * values, axis=-1, keepdims=True) + epsilon)
    return (values * factor, factor)


def norm_back(grad_norm, normed, factor):
    return factor * (grad_norm - normed * jnp.mean(grad_norm * normed, axis=-1, keepdims=True))


def layout(documents):
    length = documents.shape[0]
    places = jnp.arange(length, dtype=jnp.int32)
    change = jnp.concatenate([jnp.ones((1,), dtype=jnp.bool_), documents[1:] != documents[:-1]])
    starts = lax.cummax(jnp.where(change, places, 0), axis=0)
    offset = places - starts
    half_dim = HEAD_DIM // 2
    freqs = jnp.exp(
        jnp.arange(half_dim, dtype=jnp.float32) * (-2.0 * math.log(rope_base) / HEAD_DIM)
    )
    angles = offset.astype(jnp.float32)[:, None] * freqs[None, :]
    return (offset // BLOCK, jnp.cos(angles), jnp.sin(angles))


def rotate(values, cosine, sine):
    half_dim = values.shape[-1] // 2
    front_half = values[..., :half_dim]
    back_half = values[..., half_dim:]
    cos_b = cosine[:, None, :]
    sin_b = sine[:, None, :]
    return jnp.concatenate(
        [front_half * cos_b - back_half * sin_b, back_half * cos_b + front_half * sin_b], axis=-1
    )


def rotate_back(values, cosine, sine):
    half_dim = values.shape[-1] // 2
    front_half = values[..., :half_dim]
    back_half = values[..., half_dim:]
    cos_b = cosine[:, None, :]
    sin_b = sine[:, None, :]
    return jnp.concatenate(
        [front_half * cos_b + back_half * sin_b, back_half * cos_b - front_half * sin_b], axis=-1
    )


def block_mask(documents, blocks, start, count):
    doc_rows = documents[start : start + count]
    blk_rows = blocks[start : start + count]
    return (doc_rows[:, None] == documents[None, :]) & (blocks[None, :] <= blk_rows[:, None])


def scores_of(query_block, keys, allowed):
    raw = jnp.einsum(
        "qngd,knd->ngqk", query_block, keys, preferred_element_type=jnp.float32
    ) / math.sqrt(HEAD_DIM)
    return jnp.where(allowed[None, None], raw, masked_value)


def attend(queries, keys, values, documents, blocks):
    length = queries.shape[0]
    span = min(512, length)
    outputs = []
    totals = []
    for start in range(0, length, span):
        scores = scores_of(
            queries[start : start + span], keys, block_mask(documents, blocks, start, span)
        )
        row_max = jnp.max(scores, axis=-1, keepdims=True)
        exponent = jnp.exp(scores - row_max)
        summed = jnp.sum(exponent, axis=-1, keepdims=True)
        prob_low = (exponent / summed).astype(jnp.bfloat16)
        outputs.append(
            jnp.einsum(
                "ngqk,knd->qngd", prob_low, values, preferred_element_type=jnp.float32
            ).astype(jnp.bfloat16)
        )
        totals.append(row_max + jnp.log(summed))
    return (jnp.concatenate(outputs, axis=0), totals)


def attend_back(grad_out, queries, keys, values, totals, documents, blocks):
    length = queries.shape[0]
    span = min(512, length)
    grad_keys = jnp.zeros(keys.shape, jnp.float32)
    grad_values = jnp.zeros(values.shape, jnp.float32)
    grad_queries = []
    for turn_index, start in enumerate(range(0, length, span)):
        query_block = queries[start : start + span]
        scores = scores_of(query_block, keys, block_mask(documents, blocks, start, span))
        prob_full = jnp.exp(scores - totals[turn_index])
        prob_low = prob_full.astype(jnp.bfloat16)
        grad_block = grad_out[start : start + span]
        grad_values = grad_values + jnp.einsum(
            "ngqk,qngd->knd", prob_low, grad_block, preferred_element_type=jnp.float32
        )
        grad_prob = jnp.einsum(
            "qngd,knd->ngqk", grad_block, values, preferred_element_type=jnp.float32
        )
        inner = jnp.sum(prob_full * grad_prob, axis=-1, keepdims=True)
        grad_score = (prob_full * (grad_prob - inner)).astype(jnp.bfloat16)
        grad_queries.append(
            jnp.einsum("ngqk,knd->qngd", grad_score, keys, preferred_element_type=jnp.float32)
            / math.sqrt(HEAD_DIM)
        )
        grad_keys = grad_keys + jnp.einsum(
            "ngqk,qngd->knd", grad_score, query_block, preferred_element_type=jnp.float32
        ) / math.sqrt(HEAD_DIM)
    return (jnp.concatenate(grad_queries, axis=0), grad_keys, grad_values)


def fetch_attn(shards):
    low_gain = shards[0].astype(jnp.bfloat16)
    low_query = shards[1].astype(jnp.bfloat16)
    low_key = shards[2].astype(jnp.bfloat16)
    low_value = shards[3].astype(jnp.bfloat16)
    low_output = shards[4].astype(jnp.bfloat16)
    return (
        lax.all_gather(low_gain, "dp", axis=0, tiled=True),
        lax.all_gather(low_query, "dp", axis=0, tiled=True),
        lax.all_gather(low_key, "dp", axis=0, tiled=True),
        lax.all_gather(low_value, "dp", axis=0, tiled=True),
        lax.all_gather(low_output, "dp", axis=1, tiled=True),
    )


def fetch_mlp(shards):
    low_gain = shards[0].astype(jnp.bfloat16)
    low_gate = shards[1].astype(jnp.bfloat16)
    low_up = shards[2].astype(jnp.bfloat16)
    low_down = shards[3].astype(jnp.bfloat16)
    return (
        lax.all_gather(low_gain, "dp", axis=0, tiled=True),
        lax.all_gather(low_gate, "dp", axis=0, tiled=True),
        lax.all_gather(low_up, "dp", axis=0, tiled=True),
        lax.all_gather(low_down, "dp", axis=1, tiled=True),
    )


def again_attn(shards):
    low_gain = shards[0].astype(jnp.bfloat16)
    low_query = shards[1].astype(jnp.bfloat16)
    low_key = shards[2].astype(jnp.bfloat16)
    low_value = shards[3].astype(jnp.bfloat16)
    low_output = shards[4].astype(jnp.bfloat16)
    return (
        lax.all_gather(low_gain, "dp", axis=0, tiled=True),
        lax.all_gather(low_query, "dp", axis=0, tiled=True),
        lax.all_gather(low_key, "dp", axis=0, tiled=True),
        lax.all_gather(low_value, "dp", axis=0, tiled=True),
        lax.all_gather(low_output, "dp", axis=1, tiled=True),
    )


def again_mlp(shards):
    low_gain = shards[0].astype(jnp.bfloat16)
    low_gate = shards[1].astype(jnp.bfloat16)
    low_up = shards[2].astype(jnp.bfloat16)
    low_down = shards[3].astype(jnp.bfloat16)
    return (
        lax.all_gather(low_gain, "dp", axis=0, tiled=True),
        lax.all_gather(low_gate, "dp", axis=0, tiled=True),
        lax.all_gather(low_up, "dp", axis=0, tiled=True),
        lax.all_gather(low_down, "dp", axis=1, tiled=True),
    )


def to_group(tok_rows):
    return lax.all_gather(tok_rows, "tensor", axis=0, tiled=True)


def from_group(partial_sum):
    return lax.psum_scatter(
        partial_sum.astype(jnp.bfloat16), "tensor", scatter_dimension=0, tiled=True
    ).astype(jnp.float32)


def grads_to_group(tok_rows):
    return lax.all_gather(tok_rows, "tensor", axis=0, tiled=True)


def grads_from_group(partial_sum):
    return lax.psum_scatter(
        partial_sum.astype(jnp.bfloat16), "tensor", scatter_dimension=0, tiled=True
    ).astype(jnp.float32)


def layer_forward(tok_rows, attn_w, mlp_w, documents, blocks, cosine, sine):
    gain_attn, w_query, w_key, w_value, w_output = attn_w
    gain_mlp, w_gate, w_up, w_down = mlp_w
    heads_here = w_query.shape[1] // HEAD_DIM
    kv_here = w_key.shape[1] // HEAD_DIM
    normed_attn, factor_attn = normalize(tok_rows)
    gathered = to_group((normed_attn * gain_attn.astype(jnp.float32)).astype(jnp.bfloat16))
    length = gathered.shape[0]
    q_lin = jnp.dot(gathered, w_query, preferred_element_type=jnp.float32).reshape(
        length, heads_here, HEAD_DIM
    )
    k_lin = jnp.dot(gathered, w_key, preferred_element_type=jnp.float32).reshape(
        length, kv_here, HEAD_DIM
    )
    v_lin = jnp.dot(gathered, w_value, preferred_element_type=jnp.float32)
    queries = (
        rotate(q_lin, cosine, sine)
        .astype(jnp.bfloat16)
        .reshape(length, kv_here, heads_here // kv_here, HEAD_DIM)
    )
    keys = rotate(k_lin, cosine, sine).astype(jnp.bfloat16)
    values = v_lin.astype(jnp.bfloat16).reshape(length, kv_here, HEAD_DIM)
    mixed, totals = attend(queries, keys, values, documents, blocks)
    mixed_flat = mixed.reshape(length, heads_here * HEAD_DIM)
    middle = tok_rows + from_group(
        jnp.dot(mixed_flat, w_output, preferred_element_type=jnp.float32)
    )
    normed_mlp, factor_mlp = normalize(middle)
    gathered_mlp = to_group((normed_mlp * gain_mlp.astype(jnp.float32)).astype(jnp.bfloat16))
    gate_pre = jnp.dot(gathered_mlp, w_gate, preferred_element_type=jnp.float32)
    up_pre = jnp.dot(gathered_mlp, w_up, preferred_element_type=jnp.float32)
    hidden = (jax.nn.silu(gate_pre) * up_pre).astype(jnp.bfloat16)
    result = middle + from_group(jnp.dot(hidden, w_down, preferred_element_type=jnp.float32))
    saved = (
        normed_attn,
        factor_attn,
        gathered,
        queries,
        keys,
        values,
        totals,
        mixed_flat,
        normed_mlp,
        factor_mlp,
        gathered_mlp,
        gate_pre,
        up_pre,
        hidden,
    )
    return (result, saved)


def layer_backward(grad_rows, saved, attn_w, mlp_w, documents, blocks, cosine, sine):
    (
        normed_attn,
        factor_attn,
        gathered,
        queries,
        keys,
        values,
        totals,
        mixed_flat,
        normed_mlp,
        factor_mlp,
        gathered_mlp,
        gate_pre,
        up_pre,
        hidden,
    ) = saved
    gain_attn, w_query, w_key, w_value, w_output = attn_w
    gain_mlp, w_gate, w_up, w_down = mlp_w
    length = gathered.shape[0]
    heads_here = w_query.shape[1] // HEAD_DIM
    kv_here = w_key.shape[1] // HEAD_DIM
    grad_mlp = grads_to_group(grad_rows.astype(jnp.bfloat16))
    grad_down = dot_rows(hidden, grad_mlp)
    grad_hidden = dot_cols(grad_mlp, w_down)
    sigmoid_g = jax.nn.sigmoid(gate_pre)
    grad_gate_pre = (
        grad_hidden * up_pre * sigmoid_g * (1.0 + gate_pre * (1.0 - sigmoid_g))
    ).astype(jnp.bfloat16)
    grad_up_pre = (grad_hidden * gate_pre * sigmoid_g).astype(jnp.bfloat16)
    grad_gate = dot_rows(gathered_mlp, grad_gate_pre)
    grad_up = dot_rows(gathered_mlp, grad_up_pre)
    grad_in_mlp = grads_from_group(dot_cols(grad_gate_pre, w_gate) + dot_cols(grad_up_pre, w_up))
    grad_gain_mlp = jnp.sum(grad_in_mlp * normed_mlp, axis=0)
    grad_middle = grad_rows + norm_back(
        grad_in_mlp * gain_mlp.astype(jnp.float32), normed_mlp, factor_mlp
    )
    mlp_grads = (grad_gain_mlp, grad_gate, grad_up, grad_down)
    mlp_grads = (
        lax.psum_scatter(
            grad_gain_mlp.astype(jnp.bfloat16), "dp", scatter_dimension=0, tiled=True
        ).astype(jnp.float32),
        lax.psum_scatter(
            grad_gate.astype(jnp.bfloat16), "dp", scatter_dimension=0, tiled=True
        ).astype(jnp.float32),
        lax.psum_scatter(
            grad_up.astype(jnp.bfloat16), "dp", scatter_dimension=0, tiled=True
        ).astype(jnp.float32),
        lax.psum_scatter(
            grad_down.astype(jnp.bfloat16), "dp", scatter_dimension=1, tiled=True
        ).astype(jnp.float32),
    )
    grad_att = grads_to_group(grad_middle.astype(jnp.bfloat16))
    grad_output = dot_rows(mixed_flat, grad_att)
    grad_mixed = (
        dot_cols(grad_att, w_output)
        .astype(jnp.bfloat16)
        .reshape(length, kv_here, heads_here // kv_here, HEAD_DIM)
    )
    grad_queries, grad_keys, grad_values = attend_back(
        grad_mixed, queries, keys, values, totals, documents, blocks
    )
    grad_q_lin = (
        rotate_back(grad_queries.reshape(length, heads_here, HEAD_DIM), cosine, sine)
        .astype(jnp.bfloat16)
        .reshape(length, heads_here * HEAD_DIM)
    )
    grad_k_lin = (
        rotate_back(grad_keys, cosine, sine)
        .astype(jnp.bfloat16)
        .reshape(length, kv_here * HEAD_DIM)
    )
    grad_v_lin = grad_values.astype(jnp.bfloat16).reshape(length, kv_here * HEAD_DIM)
    grad_query = dot_rows(gathered, grad_q_lin)
    grad_key = dot_rows(gathered, grad_k_lin)
    grad_value = dot_rows(gathered, grad_v_lin)
    grad_normed = (
        dot_cols(grad_q_lin, w_query) + dot_cols(grad_k_lin, w_key) + dot_cols(grad_v_lin, w_value)
    )
    grad_in_attn = grads_from_group(grad_normed)
    grad_gain_attn = jnp.sum(grad_in_attn * normed_attn, axis=0)
    grad_states = grad_middle + norm_back(
        grad_in_attn * gain_attn.astype(jnp.float32), normed_attn, factor_attn
    )
    attn_grads = (grad_gain_attn, grad_query, grad_key, grad_value, grad_output)
    attn_grads = (
        lax.psum_scatter(
            grad_gain_attn.astype(jnp.bfloat16), "dp", scatter_dimension=0, tiled=True
        ).astype(jnp.float32),
        lax.psum_scatter(
            grad_query.astype(jnp.bfloat16), "dp", scatter_dimension=0, tiled=True
        ).astype(jnp.float32),
        lax.psum_scatter(
            grad_key.astype(jnp.bfloat16), "dp", scatter_dimension=0, tiled=True
        ).astype(jnp.float32),
        lax.psum_scatter(
            grad_value.astype(jnp.bfloat16), "dp", scatter_dimension=0, tiled=True
        ).astype(jnp.float32),
        lax.psum_scatter(
            grad_output.astype(jnp.bfloat16), "dp", scatter_dimension=1, tiled=True
        ).astype(jnp.float32),
    )
    return (grad_states, attn_grads, mlp_grads)


def body(
    states_in,
    documents,
    attnorm_one,
    query_one,
    key_one,
    value_one,
    output_one,
    mlpnorm_one,
    gate_one,
    up_one,
    down_one,
    attnorm_two,
    query_two,
    key_two,
    value_two,
    output_two,
    mlpnorm_two,
    gate_two,
    up_two,
    down_two,
    cotangent,
):
    attn_shards = [
        (attnorm_one, query_one, key_one, value_one, output_one),
        (attnorm_two, query_two, key_two, value_two, output_two),
    ]
    mlp_shards = [
        (mlpnorm_one, gate_one, up_one, down_one),
        (mlpnorm_two, gate_two, up_two, down_two),
    ]
    blocks, cosine, sine = layout(documents)
    states = states_in
    kept_weights = []
    kept_saved = []
    for level in range(2):
        attn_w = fetch_attn(attn_shards[level])
        mlp_w = fetch_mlp(mlp_shards[level])
        states, saved = layer_forward(states, attn_w, mlp_w, documents, blocks, cosine, sine)
        kept_weights.append((attn_w, mlp_w))
        kept_saved.append(saved)
    grad_states = cotangent
    attn_parts = [None, None]
    mlp_parts = [None, None]
    for level in (1, 0):
        attn_w = again_attn(attn_shards[level])
        mlp_w = again_mlp(mlp_shards[level])
        grad_states, attn_grads, mlp_grads = layer_backward(
            grad_states, kept_saved[level], attn_w, mlp_w, documents, blocks, cosine, sine
        )
        attn_parts[level] = attn_grads
        mlp_parts[level] = mlp_grads
    gains = lax.psum(
        (attn_parts[0][0], mlp_parts[0][0], attn_parts[1][0], mlp_parts[1][0]), "tensor"
    )
    return (
        states,
        grad_states,
        gains[0],
        attn_parts[0][1],
        attn_parts[0][2],
        attn_parts[0][3],
        attn_parts[0][4],
        gains[1],
        mlp_parts[0][1],
        mlp_parts[0][2],
        mlp_parts[0][3],
        gains[2],
        attn_parts[1][1],
        attn_parts[1][2],
        attn_parts[1][3],
        attn_parts[1][4],
        gains[3],
        mlp_parts[1][1],
        mlp_parts[1][2],
        mlp_parts[1][3],
    )


def solution(mesh):
    placed = (
        P(("dp", "tensor"), None),
        P("dp"),
        P("dp"),
        P("dp", "tensor"),
        P("dp", "tensor"),
        P("dp", "tensor"),
        P("tensor", "dp"),
        P("dp"),
        P("dp", "tensor"),
        P("dp", "tensor"),
        P("tensor", "dp"),
        P("dp"),
        P("dp", "tensor"),
        P("dp", "tensor"),
        P("dp", "tensor"),
        P("tensor", "dp"),
        P("dp"),
        P("dp", "tensor"),
        P("dp", "tensor"),
        P("tensor", "dp"),
        P(("dp", "tensor"), None),
    )
    return jax.shard_map(
        body,
        mesh=mesh,
        in_specs=placed,
        out_specs=(
            P(("dp", "tensor"), None),
            P(("dp", "tensor"), None),
            P("dp"),
            P("dp", "tensor"),
            P("dp", "tensor"),
            P("dp", "tensor"),
            P("tensor", "dp"),
            P("dp"),
            P("dp", "tensor"),
            P("dp", "tensor"),
            P("tensor", "dp"),
            P("dp"),
            P("dp", "tensor"),
            P("dp", "tensor"),
            P("dp", "tensor"),
            P("tensor", "dp"),
            P("dp"),
            P("dp", "tensor"),
            P("dp", "tensor"),
            P("tensor", "dp"),
        ),
        check_vma=False,
    )
```

profile of v0, /device:TPU:28, one launch (start us, length us, event | category | flops | bytes accessed | tf_op | source)
XLA Modules:
  0.0 2301.0 jit_solution(13517813019197658901)
XLA Ops:
  14.7 32.5 %all-reduce.10 = (bf16[1536]{0:T(1024)(128)(2,1)}, bf16[1536]{0:T(1024)(128)(2,1)S(1)}, bf16[1536]{0:T(1024)(128)(2,1)S(1)}, bf16[1536]{0:T(1024)(128)(2,1)S(1)}) all-reduce(bf16[1536]{0:T(1024)(128)(2,1)S(1)} %dynamic-update-slice.3, bf16[1536]{0:T(1024)(128)(2,1)S(1)} %dynamic-update-slice.1, ...), channel_id=1, replica_groups=mesh['dp'=8,'tensor'=4] {'dp'}, use_global_device_ids=true, to_apply=%add.3 | all-reduce | flops 6144 | bytes 24576
  52.7 36.7 %all_gather.98 = bf16[1536,192]{1,0:T(8,128)(2,1)} all-gather(bf16[192,192]{1,0:T(8,128)(2,1)S(1)} %convert_element_type.404), channel_id=1, replica_groups=mesh['dp'=8,'tensor'=4] {'dp'}, dimensions={0}, use_global_device_ids=true | all-gather | bytes 663552 | tf_op jit(solution)/shard_map/all_gather | solution.py:149
  89.4 34.2 %all_gather.99 = bf16[1536,192]{1,0:T(8,128)(2,1)} all-gather(bf16[192,192]{1,0:T(8,128)(2,1)S(1)} %convert_element_type.406), channel_id=1, replica_groups=mesh['dp'=8,'tensor'=4] {'dp'}, dimensions={0}, use_global_device_ids=true | all-gather | bytes 663552 | tf_op jit(solution)/shard_map/all_gather | solution.py:148
  177.5 35.2 %reduce-scatter.23.cloned.1.call-done = bf16[256,1536]{1,0:T(8,128)(2,1)} async-done(((bf16[1024,1536]{1,0:T(8,128)(2,1)}), bf16[256,1536]{1,0:T(8,128)(2,1)}) %reduce-scatter.23.cloned.1.call-update) | async-done | bytes 786448 | tf_op jit(solution)/shard_map/reduce_scatter | solution.py:200
  218.8 56.7 %all-gather.27.cloned.1.call-done = bf16[1536,1024]{1,0:T(8,128)(2,1)} async-done(((bf16[192,1024]{1,0:T(8,128)(2,1)}), bf16[1536,1024]{1,0:T(8,128)(2,1)}) %all-gather.27.cloned.1.call-update) | async-done | bytes 3145744 | tf_op jit(solution)/shard_map/all_gather | solution.py:161
  313.6 54.7 %all-gather.29.cloned.1.call-done = bf16[1536,1024]{1,0:T(8,128)(2,1)} async-done(((bf16[192,1024]{1,0:T(8,128)(2,1)}), bf16[1536,1024]{1,0:T(8,128)(2,1)}) %all-gather.29.cloned.1.call-update) | async-done | bytes 3145744 | tf_op jit(solution)/shard_map/all_gather | solution.py:162
  378.6 51.8 %all-gather.31.cloned.1.call-done = bf16[1024,1536]{0,1:T(8,128)(2,1)} async-done(((bf16[1024,192]{0,1:T(8,128)(2,1)}), bf16[1024,1536]{0,1:T(8,128)(2,1)}) %all-gather.31.cloned.1.call-update) | async-done | bytes 3145744 | tf_op jit(solution)/shard_map/all_gather | solution.py:163
  438.0 37.2 %reduce-scatter.25.cloned.1.call-done = bf16[256,1536]{1,0:T(8,128)(2,1)} async-done(((bf16[1024,1536]{1,0:T(8,128)(2,1)}), bf16[256,1536]{1,0:T(8,128)(2,1)}) %reduce-scatter.25.cloned.1.call-update) | async-done | bytes 786448 | tf_op jit(solution)/shard_map/reduce_scatter | solution.py:200
  511.1 33.2 %all_gather.110 = bf16[1536,192]{1,0:T(8,128)(2,1)S(1)} all-gather(bf16[192,192]{1,0:T(8,128)(2,1)S(1)} %convert_element_type.432), channel_id=1, replica_groups=mesh['dp'=8,'tensor'=4] {'dp'}, dimensions={0}, use_global_device_ids=true | all-gather | bytes 663552 | tf_op jit(solution)/shard_map/all_gather | solution.py:148
  603.7 35.2 %reduce-scatter.27.cloned.1.call-done = bf16[256,1536]{1,0:T(8,128)(2,1)} async-done(((bf16[1024,1536]{1,0:T(8,128)(2,1)}), bf16[256,1536]{1,0:T(8,128)(2,1)}) %reduce-scatter.27.cloned.1.call-update) | async-done | bytes 786448 | tf_op jit(solution)/shard_map/reduce_scatter | solution.py:200
  648.3 53.4 %all-gather.43.cloned.1.call-done = bf16[1536,1024]{1,0:T(8,128)(2,1)} async-done(((bf16[192,1024]{1,0:T(8,128)(2,1)}), bf16[1536,1024]{1,0:T(8,128)(2,1)}) %all-gather.43.cloned.1.call-update) | async-done | bytes 3145744 | tf_op jit(solution)/shard_map/all_gather | solution.py:162
  739.7 54.6 %all-gather.41.cloned.1.call-done = bf16[1536,1024]{1,0:T(8,128)(2,1)} async-done(((bf16[192,1024]{1,0:T(8,128)(2,1)}), bf16[1536,1024]{1,0:T(8,128)(2,1)}) %all-gather.41.cloned.1.call-update) | async-done | bytes 3145744 | tf_op jit(solution)/shard_map/all_gather | solution.py:161
  824.0 62.3 %all-gather.45.cloned.1.call-done = bf16[1024,1536]{0,1:T(8,128)(2,1)} async-done(((bf16[1024,192]{0,1:T(8,128)(2,1)}), bf16[1024,1536]{0,1:T(8,128)(2,1)}) %all-gather.45.cloned.1.call-update) | async-done | bytes 3145744 | tf_op jit(solution)/shard_map/all_gather | solution.py:163
  906.8 37.2 %reduce-scatter.31.cloned.1.call-done = bf16[256,1536]{1,0:T(8,128)(2,1)} async-done(((bf16[1024,1536]{1,0:T(8,128)(2,1)}), bf16[256,1536]{1,0:T(8,128)(2,1)}) %reduce-scatter.31.cloned.1.call-update) | async-done | bytes 786448 | tf_op jit(solution)/shard_map/reduce_scatter | solution.py:210
  1022.6 30.3 %reduce-scatter.33.cloned.1.call-done = bf16[256,1536]{1,0:T(8,128)(2,1)} async-done(((bf16[1024,1536]{1,0:T(8,128)(2,1)}), bf16[256,1536]{1,0:T(8,128)(2,1)}) %reduce-scatter.33.cloned.1.call-update) | async-done | bytes 786448 | tf_op jit(solution)/shard_map/reduce_scatter | solution.py:210
  1055.2 38.4 %reduce-scatter.29.cloned.1.call-done = bf16[256,1536]{1,0:T(8,128)(2,1)} async-done(((bf16[1024,1536]{1,0:T(8,128)(2,1)}), bf16[256,1536]{1,0:T(8,128)(2,1)}) %reduce-scatter.29.cloned.1.call-update) | async-done | bytes 786448 | tf_op jit(solution)/shard_map/reduce_scatter | solution.py:200
  1145.5 38.0 %reduce-scatter.35.cloned.1.call-done = bf16[256,1536]{1,0:T(8,128)(2,1)} async-done(((bf16[1024,1536]{1,0:T(8,128)(2,1)}), bf16[256,1536]{1,0:T(8,128)(2,1)}) %reduce-scatter.35.cloned.1.call-update) | async-done | bytes 786448 | tf_op jit(solution)/shard_map/reduce_scatter | solution.py:210
  1335.6 35.2 %reduce-scatter.63.cloned.1.call-done = bf16[192,1024]{1,0:T(8,128)(2,1)} async-done(((bf16[1536,1024]{1,0:T(8,128)(2,1)}), bf16[192,1024]{1,0:T(8,128)(2,1)}) %reduce-scatter.63.cloned.1.call-update) | async-done | bytes 393232 | tf_op jit(solution)/shard_map/reduce_scatter | solution.py:312
  1372.8 75.4 %reduce-scatter.61.cloned.1.call-done = bf16[192,1024]{1,0:T(8,128)(2,1)} async-done(((bf16[1536,1024]{1,0:T(8,128)(2,1)}), bf16[192,1024]{1,0:T(8,128)(2,1)}) %reduce-scatter.61.cloned.1.call-update) | async-done | bytes 393232 | tf_op jit(solution)/shard_map/reduce_scatter | solution.py:309
  1450.2 64.7 %reduce-scatter.57.cloned.1.call-done = bf16[192,192]{1,0:T(8,128)(2,1)} async-done(((bf16[1536,192]{1,0:T(8,128)(2,1)}), bf16[192,192]{1,0:T(8,128)(2,1)}) %reduce-scatter.57.cloned.1.call-update) | async-done | bytes 73744 | tf_op jit(solution)/shard_map/reduce_scatter | solution.py:362
  1516.4 63.6 %reduce-scatter.55.cloned.1.call-done = bf16[192,192]{1,0:T(8,128)(2,1)} async-done(((bf16[1536,192]{1,0:T(8,128)(2,1)}), bf16[192,192]{1,0:T(8,128)(2,1)}) %reduce-scatter.55.cloned.1.call-update) | async-done | bytes 73744 | tf_op jit(solution)/shard_map/reduce_scatter | solution.py:359
  1581.6 65.2 %reduce-scatter.59.cloned.1.call-done = bf16[384,192]{0,1:T(8,128)(2,1)} async-done(((bf16[384,1536]{0,1:T(8,128)(2,1)}), bf16[384,192]{0,1:T(8,128)(2,1)}) %reduce-scatter.59.cloned.1.call-update) | async-done | bytes 147472 | tf_op jit(solution)/shard_map/reduce_scatter | solution.py:365
  1648.5 65.2 %reduce-scatter.53.cloned.1.call-done = bf16[192,384]{1,0:T(8,128)(2,1)} async-done(((bf16[1536,384]{1,0:T(8,128)(2,1)}), bf16[192,384]{1,0:T(8,128)(2,1)}) %reduce-scatter.53.cloned.1.call-update) | async-done | bytes 147472 | tf_op jit(solution)/shard_map/reduce_scatter | solution.py:356
  1715.3 74.8 %reduce-scatter.51.cloned.1.call-done = bf16[1024,192]{0,1:T(8,128)(2,1)} async-done(((bf16[1024,1536]{0,1:T(8,128)(2,1)}), bf16[1024,192]{0,1:T(8,128)(2,1)}) %reduce-scatter.51.cloned.1.call-update) | async-done | bytes 393232 | tf_op jit(solution)/shard_map/reduce_scatter | solution.py:315
  1792.1 75.8 %reduce-scatter.49.cloned.1.call-done = bf16[192,1024]{1,0:T(8,128)(2,1)} async-done(((bf16[1536,1024]{1,0:T(8,128)(2,1)}), bf16[192,1024]{1,0:T(8,128)(2,1)}) %reduce-scatter.49.cloned.1.call-update) | async-done | bytes 393232 | tf_op jit(solution)/shard_map/reduce_scatter | solution.py:312
  1869.8 75.7 %reduce-scatter.47.cloned.1.call-done = bf16[192,1024]{1,0:T(8,128)(2,1)} async-done(((bf16[1536,1024]{1,0:T(8,128)(2,1)}), bf16[192,1024]{1,0:T(8,128)(2,1)}) %reduce-scatter.47.cloned.1.call-update) | async-done | bytes 393232 | tf_op jit(solution)/shard_map/reduce_scatter | solution.py:309
  1947.4 63.9 %reduce-scatter.43.cloned.1.call-done = bf16[192,192]{1,0:T(8,128)(2,1)} async-done(((bf16[1536,192]{1,0:T(8,128)(2,1)}), bf16[192,192]{1,0:T(8,128)(2,1)}) %reduce-scatter.43.cloned.1.call-update) | async-done | bytes 73744 | tf_op jit(solution)/shard_map/reduce_scatter | solution.py:362
  2012.9 63.1 %reduce-scatter.41.cloned.1.call-done = bf16[192,192]{1,0:T(8,128)(2,1)} async-done(((bf16[1536,192]{1,0:T(8,128)(2,1)}), bf16[192,192]{1,0:T(8,128)(2,1)}) %reduce-scatter.41.cloned.1.call-update) | async-done | bytes 73744 | tf_op jit(solution)/shard_map/reduce_scatter | solution.py:359
  2077.6 65.1 %reduce-scatter.45.cloned.1.call-done = bf16[384,192]{0,1:T(8,128)(2,1)} async-done(((bf16[384,1536]{0,1:T(8,128)(2,1)}), bf16[384,192]{0,1:T(8,128)(2,1)}) %reduce-scatter.45.cloned.1.call-update) | async-done | bytes 147472 | tf_op jit(solution)/shard_map/reduce_scatter | solution.py:365
  2144.4 65.1 %reduce-scatter.39.cloned.1.call-done = bf16[192,384]{1,0:T(8,128)(2,1)} async-done(((bf16[1536,384]{1,0:T(8,128)(2,1)}), bf16[192,384]{1,0:T(8,128)(2,1)}) %reduce-scatter.39.cloned.1.call-update) | async-done | bytes 147472 | tf_op jit(solution)/shard_map/reduce_scatter | solution.py:356
  2211.1 38.4 %reduce-scatter.37.cloned.1.call-done = bf16[256,1536]{1,0:T(8,128)(2,1)} async-done(((bf16[1024,1536]{1,0:T(8,128)(2,1)}), bf16[256,1536]{1,0:T(8,128)(2,1)}) %reduce-scatter.37.cloned.1.call-update) | async-done | bytes 786448 | tf_op jit(solution)/shard_map/reduce_scatter | solution.py:210
  2251.2 32.5 %all-reduce.9 = (bf16[1536]{0:T(1024)(128)(2,1)S(1)}, bf16[1536]{0:T(1024)(128)(2,1)S(1)}, bf16[1536]{0:T(1024)(128)(2,1)S(1)}, bf16[1536]{0:T(1024)(128)(2,1)S(1)}) all-reduce(bf16[1536]{0:T(1024)(128)(2,1)S(1)} %get-tuple-element.26, bf16[1536]{0:T(1024)(128)(2,1)S(1)} %copy-done.113, ...), channel_id=10, replica_groups=mesh['dp'=8,'tensor'=4] {'dp'}, use_global_device_ids=true, to_apply=%region_31.32.clone | all-reduce | flops 6144 | bytes 24576
  (547 shorter events, 637.8 us)
Async XLA Ops:
  7.2 119.4 %all-gather.19.cloned.1.call-start = ((), (), s32[]{:S(2)}) async-start(), calls=%async_computation.22 | async-start | bytes 3932160 | tf_op jit(solution)/shard_map/all_gather | solution.py:196
  51.1 119.0 %all-gather.23.cloned.1.call-start = ((), (), s32[]{:S(2)}) async-start(), calls=%async_computation.24 | async-start | bytes 1327104 | tf_op jit(solution)/shard_map/all_gather | solution.py:150
  51.8 160.8 %reduce-scatter.23.cloned.1.call-start = ((), (), s32[]{:S(2)}) async-start(), calls=%async_computation.25 | async-start | bytes 3932160 | tf_op jit(solution)/shard_map/reduce_scatter | solution.py:200
  177.4 127.9 %all-gather.25.cloned.1.call-start = ((), (), s32[]{:S(2)}) async-start(), calls=%async_computation.26 | async-start | bytes 3932160 | tf_op jit(solution)/shard_map/all_gather | solution.py:196
  217.0 151.2 %all-gather.29.cloned.1.call-start = ((), (), s32[]{:S(2)}) async-start(), calls=%async_computation.28 | async-start | bytes 3538944 | tf_op jit(solution)/shard_map/all_gather | solution.py:162
  217.9 212.5 %all-gather.31.cloned.1.call-start = ((), (), s32[]{:S(2)}) async-start(), calls=%async_computation.29 | async-start | bytes 3538944 | tf_op jit(solution)/shard_map/all_gather | solution.py:163
  218.8 256.4 %reduce-scatter.25.cloned.1.call-start = ((), (), s32[]{:S(2)}) async-start(), calls=%async_computation.30 | async-start | bytes 3932160 | tf_op jit(solution)/shard_map/reduce_scatter | solution.py:200
  437.9 106.4 %all-gather.33.cloned.1.call-start = ((), (), s32[]{:S(2)}) async-start(), calls=%async_computation.31 | async-start | bytes 3932160 | tf_op jit(solution)/shard_map/all_gather | solution.py:196
  479.8 117.1 %all-gather.37.cloned.1.call-start = ((), (), s32[]{:S(2)}) async-start(), calls=%async_computation.33 | async-start | bytes 1327104 | tf_op jit(solution)/shard_map/all_gather | solution.py:150
  481.5 157.4 %reduce-scatter.27.cloned.1.call-start = ((), (), s32[]{:S(2)}) async-start(), calls=%async_computation.34 | async-start | bytes 3932160 | tf_op jit(solution)/shard_map/reduce_scatter | solution.py:200
  603.6 127.9 %all-gather.39.cloned.1.call-start = ((), (), s32[]{:S(2)}) async-start(), calls=%async_computation.35 | async-start | bytes 3932160 | tf_op jit(solution)/shard_map/all_gather | solution.py:196
  643.2 151.1 %all-gather.41.cloned.1.call-start = ((), (), s32[]{:S(2)}) async-start(), calls=%async_computation.36 | async-start | bytes 3538944 | tf_op jit(solution)/shard_map/all_gather | solution.py:161
  645.2 178.8 %all-gather.47.cloned.1.call-start = ((), (), s32[]{:S(2)}) async-start(), calls=%async_computation.40 | async-start | bytes 3932160 | tf_op jit(solution)/shard_map/all_gather | solution.py:206
  646.2 240.1 %all-gather.45.cloned.1.call-start = ((), (), s32[]{:S(2)}) async-start(), calls=%async_computation.38 | async-start | bytes 3538944 | tf_op jit(solution)/shard_map/all_gather | solution.py:163
  648.3 295.7 %reduce-scatter.31.cloned.1.call-start = ((), (), s32[]{:S(2)}) async-start(), calls=%async_computation.41 | async-start | bytes 3932160 | tf_op jit(solution)/shard_map/reduce_scatter | solution.py:210
  1022.5 104.5 %all-gather.51.cloned.1.call-start = ((), (), s32[]{:S(2)}) async-start(), calls=%async_computation.44 | async-start | bytes 3932160 | tf_op jit(solution)/shard_map/all_gather | solution.py:206
  1145.5 109.5 %all-gather.53.cloned.1.call-start = ((), (), s32[]{:S(2)}) async-start(), calls=%async_computation.46 | async-start | bytes 3932160 | tf_op jit(solution)/shard_map/all_gather | solution.py:206
  1187.6 146.0 %reduce-scatter.65.cloned.1.call-start = ((), (), s32[]{:S(2)}) async-start(), calls=%async_computation.61 | async-start | bytes 3538944 | tf_op jit(solution)/shard_map/reduce_scatter | solution.py:315
  1195.6 175.3 %reduce-scatter.63.cloned.1.call-start = ((), (), s32[]{:S(2)}) async-start(), calls=%async_computation.60 | async-start | bytes 3538944 | tf_op jit(solution)/shard_map/reduce_scatter | solution.py:312
  1204.0 244.2 %reduce-scatter.61.cloned.1.call-start = ((), (), s32[]{:S(2)}) async-start(), calls=%async_computation.59 | async-start | bytes 3538944 | tf_op jit(solution)/shard_map/reduce_scatter | solution.py:309
  1211.8 303.1 %reduce-scatter.57.cloned.1.call-start = ((), (), s32[]{:S(2)}) async-start(), calls=%async_computation.57 | async-start | bytes 884736 | tf_op jit(solution)/shard_map/reduce_scatter | solution.py:362
  1215.7 364.3 %reduce-scatter.55.cloned.1.call-start = ((), (), s32[]{:S(2)}) async-start(), calls=%async_computation.56 | async-start | bytes 884736 | tf_op jit(solution)/shard_map/reduce_scatter | solution.py:359
  1219.6 427.2 %reduce-scatter.59.cloned.1.call-start = ((), (), s32[]{:S(2)}) async-start(), calls=%async_computation.58 | async-start | bytes 1327104 | tf_op jit(solution)/shard_map/reduce_scatter | solution.py:365
  1224.9 488.7 %reduce-scatter.53.cloned.1.call-start = ((), (), s32[]{:S(2)}) async-start(), calls=%async_computation.55 | async-start | bytes 1327104 | tf_op jit(solution)/shard_map/reduce_scatter | solution.py:356
  1230.0 560.1 %reduce-scatter.51.cloned.1.call-start = ((), (), s32[]{:S(2)}) async-start(), calls=%async_computation.54 | async-start | bytes 3538944 | tf_op jit(solution)/shard_map/reduce_scatter | solution.py:315
  1237.7 630.2 %reduce-scatter.49.cloned.1.call-start = ((), (), s32[]{:S(2)}) async-start(), calls=%async_computation.53 | async-start | bytes 3538944 | tf_op jit(solution)/shard_map/reduce_scatter | solution.py:312
  1245.5 700.0 %reduce-scatter.47.cloned.1.call-start = ((), (), s32[]{:S(2)}) async-start(), calls=%async_computation.52 | async-start | bytes 3538944 | tf_op jit(solution)/shard_map/reduce_scatter | solution.py:309
  1253.6 757.7 %reduce-scatter.43.cloned.1.call-start = ((), (), s32[]{:S(2)}) async-start(), calls=%async_computation.50 | async-start | bytes 884736 | tf_op jit(solution)/shard_map/reduce_scatter | solution.py:362
  1289.7 786.3 %reduce-scatter.41.cloned.1.call-start = ((), (), s32[]{:S(2)}) async-start(), calls=%async_computation.49 | async-start | bytes 884736 | tf_op jit(solution)/shard_map/reduce_scatter | solution.py:359
  1310.6 832.2 %reduce-scatter.45.cloned.1.call-start = ((), (), s32[]{:S(2)}) async-start(), calls=%async_computation.51 | async-start | bytes 1327104 | tf_op jit(solution)/shard_map/reduce_scatter | solution.py:365
  1315.7 893.7 %reduce-scatter.39.cloned.1.call-start = ((), (), s32[]{:S(2)}) async-start(), calls=%async_computation.48 | async-start | bytes 1327104 | tf_op jit(solution)/shard_map/reduce_scatter | solution.py:356
  1325.5 923.9 %reduce-scatter.37.cloned.1.call-start = ((), (), s32[]{:S(2)}) async-start(), calls=%async_computation.47 | async-start | bytes 3932160 | tf_op jit(solution)/shard_map/reduce_scatter | solution.py:210
  (141 other events, 7576.4 us)
Sparse Core Ops, SparseCore 0:
  82.7 44.8 all-gather.20
  130.3 39.8 all-gather.22
  175.6 37.0 reduce-scatter.22
  215.5 59.9 all-gather.26
  308.2 59.9 all-gather.28
  371.2 59.0 all-gather.30
  438.1 37.0 reduce-scatter.24
  509.5 44.8 all-gather.34
  557.0 39.8 all-gather.36
  601.8 37.0 reduce-scatter.26
  641.7 59.9 all-gather.42
  734.3 59.9 all-gather.40
  826.3 59.9 all-gather.44
  906.9 37.0 reduce-scatter.30
  1014.9 37.9 reduce-scatter.32
  1055.6 37.9 reduce-scatter.28
  1145.6 37.9 reduce-scatter.34
  1220.2 73.4 reduce-scatter.64
  1297.5 73.2 reduce-scatter.62
  1374.8 73.3 reduce-scatter.60
  1452.4 62.3 reduce-scatter.56
  1518.5 61.4 reduce-scatter.54
  1583.8 62.9 reduce-scatter.58
  1650.6 63.0 reduce-scatter.52
  1717.5 72.5 reduce-scatter.50
  1794.1 73.6 reduce-scatter.48
  1871.9 73.5 reduce-scatter.46
  1949.0 62.2 reduce-scatter.42
  2014.5 61.4 reduce-scatter.40
  2079.8 62.9 reduce-scatter.44
  2146.3 63.0 reduce-scatter.38
  2212.1 37.2 reduce-scatter.36
  (8 shorter events, 226.0 us)
where the time goes:
time: 2310 us; the launch traced here: 2300 us
  waiting for transfers between devices  1660 us (72%)
  matrix products  278 us (12%)
  blocking collectives  205 us (9%)
  other arithmetic  108 us (5%)
  local copies, waits for them, and re-layouts  28.5 us (1%)
    reduce_scatter x2, waiting for transfers between devices, layer_backward(): lax.psum_scatter(grad_gate.astype(jnp.bfloat16), 'dp', scatter_dimension=...  151 us
    reduce_scatter x4, waiting for transfers between devices, from_group(): lax.psum_scatter(partial_sum.astype(jnp.bfloat16), 'tensor', scatter_dime...  146 us
    reduce_scatter x4, waiting for transfers between devices, grads_from_group(): lax.psum_scatter(partial_sum.astype(jnp.bfloat16), 'tensor', scatter_dime...  144 us
    reduce_scatter x2, waiting for transfers between devices, layer_backward(): lax.psum_scatter(grad_output.astype(jnp.bfloat16), 'dp', scatter_dimensio...  130 us
    reduce_scatter x2, waiting for transfers between devices, layer_backward(): lax.psum_scatter(grad_query.astype(jnp.bfloat16), 'dp', scatter_dimension...  130 us
    reduce_scatter x2, waiting for transfers between devices, layer_backward(): lax.psum_scatter(grad_value.astype(jnp.bfloat16), 'dp', scatter_dimension...  129 us
    reduce_scatter x2, waiting for transfers between devices, layer_backward(): lax.psum_scatter(grad_key.astype(jnp.bfloat16), 'dp', scatter_dimension=0...  127 us
    all_gather x2, waiting for transfers between devices, fetch_mlp(): lax.all_gather(low_down, 'dp', axis=1, tiled=True)  114 us
  transfers between devices with their start and end apart: 40, of which 35 were waited for; matrix products, arithmetic and copies ran while one was open for 12% of the time, Pallas kernels for 0%

commit v1 on v0

v1 whole, which is shorter than its diff:
```python
import functools
import math

import jax
import jax.numpy as jnp
import numpy as np
from jax import lax
from jax.experimental import pallas as pl
from jax.experimental.pallas import tpu as pltpu
from jax.sharding import PartitionSpec as P

HEAD_DIM = 96
HALF = HEAD_DIM // 2
BLOCK = 256
PAD = 128
GAIN_ROWS = 16
LIMIT = 60 * 1024 * 1024

epsilon = 1e-05
rope_base = 100000.0
masked_value = -1e30
scale = 1.0 / math.sqrt(HEAD_DIM)

BF = jnp.bfloat16
F32 = jnp.float32
MESH = pl.DeviceIdType.MESH
ANY = pl.BlockSpec(memory_space=pl.ANY)
VM = pl.BlockSpec(memory_space=pltpu.VMEM)


def nn(left, right):
    return lax.dot_general(left, right, (((1,), (0,)), ((), ())), preferred_element_type=F32)


def nt(left, right):
    return lax.dot_general(left, right, (((1,), (1,)), ((), ())), preferred_element_type=F32)


def tn(left, right):
    return lax.dot_general(left, right, (((0,), (0,)), ((), ())), preferred_element_type=F32)


def tile(index, size):
    return pl.ds(pl.multiple_of(index * size, size), size)


def each(count, body):
    def step(index, carry):
        body(index)
        return carry

    lax.fori_loop(0, count, step, 0)


class Group:
    def __init__(self):
        self.me = lax.axis_index("tensor")
        self.core_bit = lax.rem(self.me, 2)
        self.chip = self.me // 2
        self.core = self.me + 1 - 2 * self.core_bit
        self.other = lax.rem(self.me + 2, 4)

    def greet(self):
        barrier = pltpu.get_barrier_semaphore()
        for near in (self.core, self.other):
            pl.semaphore_signal(barrier, inc=1, device_id={"tensor": near}, device_id_type=MESH)
        pl.semaphore_wait(barrier, 2)

    def remote(self, source, target, send, recv, device):
        return pltpu.make_async_remote_copy(
            src_ref=source,
            dst_ref=target,
            send_sem=send,
            recv_sem=recv,
            device_id={"tensor": device},
            device_id_type=MESH,
        )


class Gather:
    def __init__(self, group, full, send, recv):
        self.group, self.full, self.send, self.recv = group, full, send, recv
        half = full.shape[1] // 2
        mine = full.at[group.me]
        self.to_core = group.remote(mine, mine, send.at[0], recv.at[0], group.core)
        self.to_other = []
        self.onward = []
        for part in range(2):
            piece = full.at[group.me, pl.ds(part * half, half)]
            self.to_other.append(
                group.remote(piece, piece, send.at[1 + part], recv.at[1 + part], group.other)
            )
            piece = full.at[group.other, pl.ds(part * half, half)]
            self.onward.append(
                group.remote(piece, piece, send.at[3 + part], recv.at[3 + part], group.core)
            )

    def start(self):
        for copy in self.to_other:
            copy.start()
        self.to_core.start()

    def wait_chip(self):
        self.to_core.wait_recv()

    def forward(self):
        for here, there in zip(self.to_other, self.onward):
            here.wait_recv()
            there.start()

    def wait_other(self):
        for copy in self.onward:
            copy.wait_recv()

    def finish(self):
        self.to_core.wait_send()
        for copy in self.to_other + self.onward:
            copy.wait_send()


class Scatter:
    def __init__(self, group, parts, near, away, landed, send, recv):
        self.group, self.parts, self.near = group, parts, near
        self.away, self.landed = away, landed
        self.to_core = [
            group.remote(
                parts.at[turn, 1 - group.core_bit], near.at[turn], send.at[turn], recv.at[turn], group.core
            )
            for turn in range(2)
        ]
        half = away.shape[0] // 2
        self.to_other = [
            group.remote(
                away.at[pl.ds(part * half, half)],
                landed.at[pl.ds(part * half, half)],
                send.at[2 + part],
                recv.at[2 + part],
                group.other,
            )
            for part in range(2)
        ]

    def rows_of(self, turn):
        return 1 - self.group.chip if turn == 0 else self.group.chip

    def send_core(self, turn):
        self.to_core[turn].start()

    def send_away(self):
        self.to_core[0].wait_recv()
        half = self.away.shape[0] // 2
        for part in range(2):

            def add(index):
                rows = pl.ds(pl.multiple_of(part * half + index * 32, 32), 32)
                total = self.parts[0, self.group.core_bit, rows, :].astype(F32) + self.near[
                    0, rows, :
                ].astype(F32)
                self.away[rows, :] = total.astype(BF)

            each(half // 32, add)
            self.to_other[part].start()

    def wait(self):
        self.to_core[1].wait_recv()
        for copy in self.to_other:
            copy.wait_recv()

    def total(self, rows):
        return (
            self.parts[1, self.group.core_bit, rows, :].astype(F32)
            + self.near[1, rows, :].astype(F32)
            + self.landed[rows, :].astype(F32)
        )

    def finish(self):
        for copy in self.to_core + self.to_other:
            copy.wait_send()


def comm_scratch(rows, width):
    return [
        pltpu.VMEM((4, rows, width), BF),
        pltpu.VMEM((2, 2, rows, width), BF),
        pltpu.VMEM((2, rows, width), BF),
        pltpu.VMEM((rows, width), BF),
        pltpu.VMEM((rows, width), BF),
        pltpu.SemaphoreType.DMA((5,)),
        pltpu.SemaphoreType.DMA((5,)),
        pltpu.SemaphoreType.DMA((4,)),
        pltpu.SemaphoreType.DMA((4,)),
    ]


def source_block(index, n_dp):
    mine = lax.axis_index("dp")
    high, low = mine // 2, lax.rem(mine, 2)
    shift, side = index // 2, lax.rem(index, 2)
    count = n_dp // 2
    return lax.rem(high + count - shift, count) * 2 + lax.rem(low + side, 2)


def target_block(index, n_dp):
    mine = lax.axis_index("dp")
    high, low = mine // 2, lax.rem(mine, 2)
    shift, side = index // 2, lax.rem(index, 2)
    count = n_dp // 2
    return lax.rem(high + shift, count) * 2 + lax.rem(low + side, 2)


class Weights:
    def __init__(self, shards, held, sems, low_gains=None, gain_sems=None):
        n_dp = len(shards)
        depth = held.shape[0] // n_dp
        self.copies = []
        for index, shard in enumerate(shards):
            block = source_block(index, n_dp)
            rows = pl.ds(pl.multiple_of(block * depth, GAIN_ROWS), depth)
            self.copies.append(
                pltpu.make_async_copy(shard.at[pl.ds(0, depth)], held.at[rows], sems.at[index])
            )
            if low_gains is not None:
                self.copies.append(
                    pltpu.make_async_copy(
                        shard.at[pl.ds(depth, GAIN_ROWS), pl.ds(0, low_gains.shape[2])],
                        low_gains.at[block],
                        gain_sems.at[index],
                    )
                )

    def start(self):
        for copy in self.copies:
            copy.start()

    def wait(self):
        for copy in self.copies:
            copy.wait()


def spread(block, depth, lanes, width):
    row = lax.broadcasted_iota(jnp.int32, (lanes, width), 0)
    column = lax.broadcasted_iota(jnp.int32, (lanes, width), 1)
    hit = (column - row == block * depth) & (row < depth)
    return jnp.where(hit, 1.0, 0.0).astype(BF)


def turn_half(values):
    return pltpu.roll(values, PAD // 2, 1)


def out_columns(group, scatter, turn, left_rows, right_tile, columns):
    product = nt(left_rows, right_tile)
    rows = product.shape[0] // 2
    scatter.parts[turn, 0, :, columns] = product[:rows].astype(BF)
    scatter.parts[turn, 1, :, columns] = product[rows:].astype(BF)


def attn_forward_kernel(n_dp, depth, *refs):
    x_ref, cos_ref, sin_ref, span_ref, place_ref = refs[:5]
    shards = refs[5 : 5 + n_dp]
    refs = refs[5 + n_dp :]
    mid_ref, gains_ref, a_out, qkv_out, o_out = refs[:5]
    p_outs = refs[5:9]
    (full, parts, near, away, landed, g_send, g_recv, s_send, s_recv) = refs[9:18]
    (held, low_gains, padded, qkv, mixed, compact, p0, p1, p2, p3, w_sems, gain_sems, out_sems) = refs[18:]
    probs = (p0, p1, p2, p3)
    rows, width = x_ref.shape
    length = 4 * rows
    group = Group()
    weights = Weights(shards, held, w_sems, low_gains, gain_sems)
    weights.start()
    weights.wait()
    gains_ref[...] = jnp.zeros_like(gains_ref)

    def gather_gain(block):
        gains_ref[...] += nn(
            low_gains[block], spread(block, depth, low_gains.shape[2], width)
        )

    each(n_dp, gather_gain)
    gather = Gather(group, full, g_send, g_recv)
    scatter = Scatter(group, parts, near, away, landed, s_send, s_recv)
    gain = gains_ref[0:1, :]

    def norm(index):
        part = tile(index, 32)
        values = x_ref[part, :]
        factor = lax.rsqrt(jnp.mean(values * values, axis=-1, keepdims=True) + epsilon)
        full[group.me, part, :] = (values * factor * gain).astype(BF)

    each(rows // 32, norm)
    group.greet()
    gather.start()
    place = place_ref[...]
    heads = place.shape[1] // PAD
    compact_width = place.shape[0]
    head_width = place.shape[1]

    def pad(index):
        part = tile(index, 256)
        padded[part, 0:head_width] = nn(held[part, 0:compact_width], place).astype(BF)
        padded[part, head_width : 2 * head_width] = nn(
            held[part, compact_width : 2 * compact_width], place
        ).astype(BF)

    each(width // 256, pad)

    def project(chip):
        left = full[pl.ds(2 * chip, 2)].reshape(2 * rows, width)
        where = tile(chip, 2 * rows)
        cosine, sine = cos_ref[where, :], sin_ref[where, :]

        def turned(index):
            columns = tile(index, 2 * PAD)
            product = nn(left, padded[:, columns])
            for half in range(2):
                u = product[:, half * PAD : (half + 1) * PAD]
                qkv[where, tile(2 * index + half, PAD)] = (u * cosine + turn_half(u) * sine).astype(BF)

        each(3 * heads // 4, turned)
        columns = pl.ds(3 * heads // 2 * PAD, heads // 2 * PAD)
        qkv[where, columns] = nn(left, padded[:, columns]).astype(BF)

    gather.wait_chip()
    project(group.chip)
    gather.forward()
    gather.wait_other()
    project(1 - group.chip)
    copies = [
        pltpu.make_async_copy(full, a_out, out_sems.at[0]),
        pltpu.make_async_copy(qkv, qkv_out, out_sems.at[1]),
    ]
    for copy in copies:
        copy.start()
    kv_at = heads * PAD
    value_at = kv_at + heads // 2 * PAD
    for turn, prob in enumerate(probs):
        reach = prob.shape[2]
        where = pl.ds(turn * rows, rows)

        def attend(head):
            query = qkv[where, tile(head, PAD)]
            key = qkv[0:reach, pl.ds(pl.multiple_of(kv_at + head // 2 * PAD, PAD), PAD)]
            value = qkv[0:reach, pl.ds(pl.multiple_of(value_at + head // 2 * PAD, PAD), PAD)]
            scores = nt(query, key) * scale
            place_of = lax.broadcasted_iota(jnp.int32, scores.shape, 1)
            first = span_ref[where, 0:1]
            last = span_ref[where, 1:2]
            scores = jnp.where((place_of >= first) & (place_of < last), scores, masked_value)
            exponent = jnp.exp(scores - jnp.max(scores, axis=-1, keepdims=True))
            summed = jnp.sum(exponent, axis=-1, keepdims=True)
            low = (exponent * (1.0 / summed)).astype(BF)
            prob[head] = low
            mixed[where, tile(head, PAD)] = nn(low, value).astype(BF)

        each(heads, attend)
        copy = pltpu.make_async_copy(prob, p_outs[turn], out_sems.at[2 + turn])
        copy.start()
        copies.append(copy)
        compact[where, :] = nt(mixed[where, :], place).astype(BF)
    copy = pltpu.make_async_copy(compact, o_out, out_sems.at[6])
    copy.start()
    copies.append(copy)
    for turn in range(2):
        left = compact[tile(scatter.rows_of(turn), 2 * rows), :]

        def part_of(index):
            columns = tile(index, 256)
            out_columns(group, scatter, turn, left, held[columns, 2 * compact_width :], columns)

        each(width // 256, part_of)
        scatter.send_core(turn)
        if turn == 0:
            scatter.send_away()
    scatter.wait()

    def close(index):
        part = tile(index, 32)
        mid_ref[part, :] = x_ref[part, :] + scatter.total(part)

    each(rows // 32, close)
    gather.finish()
    scatter.finish()
    for copy in copies:
        copy.wait()


def mlp_forward_kernel(n_dp, *refs):
    mid_ref, gains_ref = refs[:2]
    shards = refs[2 : 2 + n_dp]
    refs = refs[2 + n_dp :]
    y_ref, m_out, gu_out, hid_out = refs[:4]
    (full, parts, near, away, landed, g_send, g_recv, s_send, s_recv) = refs[4:13]
    held, gu, hid, w_sems, out_sems = refs[13:]
    rows, width = mid_ref.shape
    units = hid.shape[1]
    group = Group()
    weights = Weights(shards, held, w_sems)
    weights.start()
    gather = Gather(group, full, g_send, g_recv)
    scatter = Scatter(group, parts, near, away, landed, s_send, s_recv)
    gain = gains_ref[1:2, :]

    def norm(index):
        part = tile(index, 32)
        values = mid_ref[part, :]
        factor = lax.rsqrt(jnp.mean(values * values, axis=-1, keepdims=True) + epsilon)
        full[group.me, part, :] = (values * factor * gain).astype(BF)

    each(rows // 32, norm)
    group.greet()
    gather.start()
    weights.wait()

    def expand(chip):
        left = full[pl.ds(2 * chip, 2)].reshape(2 * rows, width)
        where = tile(chip, 2 * rows)

        def unit(index):
            columns = tile(index, 256)
            further = pl.ds(pl.multiple_of(units + index * 256, 256), 256)
            gate = nn(left, held[:, columns])
            up = nn(left, held[:, further])
            hid[where, columns] = (gate / (1.0 + jnp.exp(-gate)) * up).astype(BF)
            gu[where, columns] = gate.astype(BF)
            gu[where, further] = up.astype(BF)

        each(units // 256, unit)

    gather.wait_chip()
    expand(group.chip)
    gather.forward()
    gather.wait_other()
    expand(1 - group.chip)
    copies = [
        pltpu.make_async_copy(full, m_out, out_sems.at[0]),
        pltpu.make_async_copy(gu, gu_out, out_sems.at[1]),
        pltpu.make_async_copy(hid, hid_out, out_sems.at[2]),
    ]
    for copy in copies:
        copy.start()
    for turn in range(2):
        left = hid[tile(scatter.rows_of(turn), 2 * rows), :]

        def part_of(index):
            columns = tile(index, 256)
            out_columns(group, scatter, turn, left, held[columns, 2 * units :], columns)

        each(width // 256, part_of)
        scatter.send_core(turn)
        if turn == 0:
            scatter.send_away()
    scatter.wait()

    def close(index):
        part = tile(index, 32)
        y_ref[part, :] = mid_ref[part, :] + scatter.total(part)

    each(rows // 32, close)
    gather.finish()
    scatter.finish()
    for copy in copies:
        copy.wait()


def flip(source, target, slot, rows, width):
    def block(index):
        columns = tile(index, 256)
        target[columns, slot * rows : (slot + 1) * rows] = source[slot, :, columns].T

    each(width // 256, block)


def close_back(scatter, grad_ref, state_ref, gain, grad_out, dgain):
    rows = state_ref.shape[0]
    dgain[...] = jnp.zeros_like(dgain)

    def close(index):
        part = tile(index, 32)
        values = state_ref[part, :]
        factor = lax.rsqrt(jnp.mean(values * values, axis=-1, keepdims=True) + epsilon)
        normed = values * factor
        grad_in = scatter.total(part)
        dgain[...] += jnp.sum((grad_in * normed).reshape(4, 8, -1), axis=0)
        grad_norm = grad_in * gain
        inner = jnp.mean(grad_norm * normed, axis=-1, keepdims=True)
        grad_out[part, :] = grad_ref[part, :] + factor * (grad_norm - normed * inner)

    each(rows // 32, close)


def mlp_backward_kernel(n_dp, depth, *refs):
    grad_ref, mid_ref, gains_ref, m_in, gu_in, hid_in = refs[:6]
    shards = refs[6 : 6 + n_dp]
    refs = refs[6 + n_dp :]
    out_ref, dgain_ref = refs[:2]
    g_outs = refs[2 : 2 + n_dp]
    refs = refs[2 + n_dp :]
    (full, parts, near, away, landed, g_send, g_recv, s_send, s_recv) = refs[:9]
    held, m_full, flipped, gu, hid, grad_gu, grads, w_sems, in_sems, out_sems = refs[9:]
    rows, width = mid_ref.shape
    units = hid.shape[1]
    group = Group()
    weights = Weights(shards, held, w_sems)
    fetches = [
        pltpu.make_async_copy(m_in, m_full, in_sems.at[0]),
        pltpu.make_async_copy(gu_in, gu, in_sems.at[1]),
        pltpu.make_async_copy(hid_in, hid, in_sems.at[2]),
    ]
    gather = Gather(group, full, g_send, g_recv)
    scatter = Scatter(group, parts, near, away, landed, s_send, s_recv)
    fetches[0].start()
    weights.start()
    fetches[1].start()
    fetches[2].start()
    full[group.me] = grad_ref[...].astype(BF)
    group.greet()
    gather.start()
    fetches[0].wait()
    for slot in range(4):
        flip(m_full, flipped, slot, rows, width)
    weights.wait()
    for copy in fetches[1:]:
        copy.wait()

    def inward(chip):
        left = full[pl.ds(2 * chip, 2)].reshape(2 * rows, width)
        where = tile(chip, 2 * rows)

        def unit(index):
            columns = tile(index, 256)
            further = pl.ds(pl.multiple_of(units + index * 256, 256), 256)
            last = pl.ds(pl.multiple_of(2 * units + index * 256, 256), 256)
            grad = nn(left, held[:, last])
            gate = gu[where, columns].astype(F32)
            up = gu[where, further].astype(F32)
            sig = 1.0 / (1.0 + jnp.exp(-gate))
            grad_gu[where, columns] = (grad * up * sig * (1.0 + gate * (1.0 - sig))).astype(BF)
            grad_gu[where, further] = (grad * gate * sig).astype(BF)

        each(units // 256, unit)

    gather.wait_chip()
    inward(group.chip)
    gather.forward()
    gather.wait_other()
    inward(1 - group.chip)
    for turn in range(2):
        where = tile(scatter.rows_of(turn), 2 * rows)

        def part_of(index):
            columns = tile(index, 256)
            out_columns(group, scatter, turn, grad_gu[where, :], held[columns, 0 : 2 * units], columns)

        each(width // 256, part_of)
        scatter.send_core(turn)
        if turn == 0:
            scatter.send_away()
    def grad_of(order, first, count, right):
        block = target_block(order, n_dp)
        left = flipped[pl.ds(pl.multiple_of(block * depth, GAIN_ROWS), depth), :]

        def some(index):
            columns = pl.ds(pl.multiple_of(first + index * 512, 512), 512)
            grads[order, :, columns] = nn(left, right[:, tile(index, 512)]).astype(BF)

        each(count // 512, some)

    each(n_dp, lambda order: grad_of(order, 0, 2 * units, grad_gu))
    for slot in range(4):
        flip(full, flipped, slot, rows, width)
    each(n_dp, lambda order: grad_of(order, 2 * units, units, hid))
    copies = []
    for order in range(n_dp):
        copy = pltpu.make_async_copy(grads.at[order], g_outs[order], out_sems.at[order])
        copy.start()
        copies.append(copy)
    scatter.wait()
    close_back(scatter, grad_ref, mid_ref, gains_ref[1:2, :], out_ref, dgain_ref)
    gather.finish()
    scatter.finish()
    for copy in copies:
        copy.wait()


def attn_backward_kernel(n_dp, depth, *refs):
    grad_ref, x_ref, gains_ref, dmlp_ref, cos_ref, sin_ref, place_ref, a_in, qkv_in, o_in = refs[:10]
    p_ins = refs[10:14]
    shards = refs[14 : 14 + n_dp]
    refs = refs[14 + n_dp :]
    out_ref = refs[0]
    g_outs = refs[1 : 1 + n_dp]
    refs = refs[1 + n_dp :]
    (full, parts, near, away, landed, g_send, g_recv, s_send, s_recv) = refs[:9]
    held, a_full, flipped, qkv, compact, p0, p1, p2, p3 = refs[9:18]
    (grad_mixed, grad_q, grad_kv, grad_k, grad_v, grad_low, grads, dgain, w_sems, in_sems, out_sems) = refs[18:]
    probs = (p0, p1, p2, p3)
    rows, width = x_ref.shape
    length = 4 * rows
    group = Group()
    weights = Weights(shards, held, w_sems)
    fetches = [
        pltpu.make_async_copy(a_in, a_full, in_sems.at[0]),
        pltpu.make_async_copy(qkv_in, qkv, in_sems.at[1]),
        pltpu.make_async_copy(o_in, compact, in_sems.at[2]),
    ] + [pltpu.make_async_copy(p_ins[i], probs[i], in_sems.at[3 + i]) for i in range(4)]
    gather = Gather(group, full, g_send, g_recv)
    scatter = Scatter(group, parts, near, away, landed, s_send, s_recv)
    fetches[0].start()
    weights.start()
    for copy in fetches[1:]:
        copy.start()
    full[group.me] = grad_ref[...].astype(BF)
    group.greet()
    gather.start()
    fetches[0].wait()
    for slot in range(4):
        flip(a_full, flipped, slot, rows, width)
    weights.wait()
    for copy in fetches[1:]:
        copy.wait()
    place = place_ref[...]
    heads = place.shape[1] // PAD
    compact_width = place.shape[0]
    head_width = place.shape[1]

    def inward(chip):
        left = full[pl.ds(2 * chip, 2)].reshape(2 * rows, width)
        where = tile(chip, 2 * rows)
        grad = nn(left, held[:, 2 * compact_width :]).astype(BF)
        grad_mixed[where, :] = nn(grad, place).astype(BF)

    gather.wait_chip()
    inward(group.chip)
    gather.forward()
    gather.wait_other()
    inward(1 - group.chip)
    kv_at = heads * PAD
    value_at = kv_at + heads // 2 * PAD
    grad_k[...] = jnp.zeros_like(grad_k)
    grad_v[...] = jnp.zeros_like(grad_v)
    for turn, prob in enumerate(probs):
        reach = prob.shape[2]
        where = pl.ds(turn * rows, rows)
        cosine, sine = cos_ref[where, :], sin_ref[where, :]

        def attend(head):
            mine = tile(head, PAD)
            shared = tile(head // 2, PAD)
            query = qkv[where, mine]
            key = qkv[0:reach, pl.ds(pl.multiple_of(kv_at + head // 2 * PAD, PAD), PAD)]
            value = qkv[0:reach, pl.ds(pl.multiple_of(value_at + head // 2 * PAD, PAD), PAD)]
            grad = grad_mixed[where, mine]
            low = prob[head]
            grad_prob = nt(grad, value)
            weight = low.astype(F32)
            inner = jnp.sum(weight * grad_prob, axis=-1, keepdims=True)
            grad_score = (weight * (grad_prob - inner)).astype(BF)
            u = nn(grad_score, key) * scale
            grad_q[where, mine] = (u * cosine - turn_half(u) * sine).astype(BF)
            grad_k[0:reach, shared] += tn(grad_score, query)
            grad_v[0:reach, shared] += tn(low, grad)

        each(heads, attend)
    for pair in range(heads // 2):
        columns = pl.ds(pair * PAD, PAD)
        u = grad_k[:, columns] * scale
        grad_kv[:, columns] = (u * cos_ref[...] - turn_half(u) * sin_ref[...]).astype(BF)
        grad_kv[:, pl.ds((heads // 2 + pair) * PAD, PAD)] = grad_v[:, columns].astype(BF)
    grad_low[:, 0:compact_width] = nt(grad_q[...], place).astype(BF)
    grad_low[:, compact_width : 2 * compact_width] = nt(grad_kv[...], place).astype(BF)
    for turn in range(2):
        where = tile(scatter.rows_of(turn), 2 * rows)

        def part_of(index):
            columns = tile(index, 256)
            out_columns(
                group, scatter, turn, grad_low[where, :], held[columns, 0 : 2 * compact_width], columns
            )

        each(width // 256, part_of)
        scatter.send_core(turn)
        if turn == 0:
            scatter.send_away()

    def grad_of(order, first, right):
        block = target_block(order, n_dp)
        left = flipped[pl.ds(pl.multiple_of(block * depth, GAIN_ROWS), depth), :]
        grads[order, 0:depth, first : first + right.shape[1]] = nn(left, right[...]).astype(BF)

    each(n_dp, lambda order: grad_of(order, 0, grad_low))
    for slot in range(4):
        flip(full, flipped, slot, rows, width)
    each(n_dp, lambda order: grad_of(order, 2 * compact_width, compact))
    scatter.wait()
    close_back(scatter, grad_ref, x_ref, gains_ref[0:1, :], out_ref, dgain)
    both = jnp.concatenate(
        [
            jnp.sum(dgain[...], axis=0, keepdims=True),
            jnp.sum(dmlp_ref[...], axis=0, keepdims=True),
            jnp.zeros((GAIN_ROWS - 2, width), F32),
        ],
        axis=0,
    ).astype(BF)

    def gain_rows(order):
        lanes = 256
        chosen = spread(target_block(order, n_dp), depth, lanes, width)
        grads[order, depth : depth + GAIN_ROWS, 0:lanes] = nt(both, chosen).astype(BF)
        grads[order, depth : depth + GAIN_ROWS, lanes:] = jnp.zeros(
            (GAIN_ROWS, grads.shape[2] - lanes), BF
        )

    each(n_dp, gain_rows)
    copies = []
    for order in range(n_dp):
        copy = pltpu.make_async_copy(grads.at[order], g_outs[order], out_sems.at[order])
        copy.start()
        copies.append(copy)
    gather.finish()
    scatter.finish()
    for copy in copies:
        copy.wait()


def shaped(shape, dtype):
    return jax.ShapeDtypeStruct(shape, dtype)


def dma(count):
    return pltpu.SemaphoreType.DMA((count,))


def reaches(rows):
    return [min((turn + 1) * rows + PAD, 4 * rows) for turn in range(4)]


def params(which):
    return pltpu.CompilerParams(collective_id=which, has_side_effects=True, vmem_limit_bytes=LIMIT)


def cost(flops, moved):
    return pl.CostEstimate(flops=flops, bytes_accessed=moved, transcendentals=0)


def attn_forward(states, tables, shards):
    cosine, sine, spans, place = tables
    n_dp = len(shards)
    rows, width = states.shape
    depth = width // n_dp
    columns = shards[0].shape[1]
    heads = place.shape[1] // PAD
    reach = reaches(rows)
    length = 4 * rows
    results = pl.pallas_call(
        functools.partial(attn_forward_kernel, n_dp, depth),
        out_shape=[
            shaped((rows, width), F32),
            shaped((GAIN_ROWS, width), F32),
            shaped((4, rows, width), BF),
            shaped((length, 2 * heads * PAD), BF),
            shaped((length, place.shape[0]), BF),
        ]
        + [shaped((heads, rows, r), BF) for r in reach],
        in_specs=[VM] * 5 + [ANY] * n_dp,
        out_specs=[VM, VM] + [ANY] * 7,
        scratch_shapes=comm_scratch(rows, width)
        + [
            pltpu.VMEM((width, columns), BF),
            pltpu.VMEM((n_dp, GAIN_ROWS, 256), BF),
            pltpu.VMEM((width, 2 * heads * PAD), BF),
            pltpu.VMEM((length, 2 * heads * PAD), BF),
            pltpu.VMEM((length, heads * PAD), BF),
            pltpu.VMEM((length, place.shape[0]), BF),
        ]
        + [pltpu.VMEM((heads, rows, r), BF) for r in reach]
        + [dma(n_dp), dma(n_dp), dma(7)],
        compiler_params=params(0),
        cost_estimate=cost(20_000_000_000, 60_000_000),
        name="attn_forward",
    )(states, cosine, sine, spans, place, *shards)
    return results[0], results[1], results[2:]


def mlp_forward(middle, gains, shards):
    n_dp = len(shards)
    rows, width = middle.shape
    columns = shards[0].shape[1]
    units = columns // 3
    length = 4 * rows
    results = pl.pallas_call(
        functools.partial(mlp_forward_kernel, n_dp),
        out_shape=[
            shaped((rows, width), F32),
            shaped((4, rows, width), BF),
            shaped((length, 2 * units), BF),
            shaped((length, units), BF),
        ],
        in_specs=[VM] * 2 + [ANY] * n_dp,
        out_specs=[VM] + [ANY] * 3,
        scratch_shapes=comm_scratch(rows, width)
        + [
            pltpu.VMEM((width, columns), BF),
            pltpu.VMEM((length, 2 * units), BF),
            pltpu.VMEM((length, units), BF),
            dma(n_dp),
            dma(3),
        ],
        compiler_params=params(1),
        cost_estimate=cost(20_000_000_000, 60_000_000),
        name="mlp_forward",
    )(middle, gains, *shards)
    return results[0], results[1:]


def mlp_backward(grad, middle, gains, saved, shards):
    n_dp = len(shards)
    rows, width = middle.shape
    depth = width // n_dp
    columns = shards[0].shape[1]
    units = columns // 3
    length = 4 * rows
    results = pl.pallas_call(
        functools.partial(mlp_backward_kernel, n_dp, depth),
        out_shape=[shaped((rows, width), F32), shaped((8, width), F32)]
        + [shaped((depth, columns), BF)] * n_dp,
        in_specs=[VM] * 3 + [ANY] * (3 + n_dp),
        out_specs=[VM] * 2 + [ANY] * n_dp,
        scratch_shapes=comm_scratch(rows, width)
        + [
            pltpu.VMEM((width, columns), BF),
            pltpu.VMEM((4, rows, width), BF),
            pltpu.VMEM((width, length), BF),
            pltpu.VMEM((length, 2 * units), BF),
            pltpu.VMEM((length, units), BF),
            pltpu.VMEM((length, 2 * units), BF),
            pltpu.VMEM((n_dp, depth, columns), BF),
            dma(n_dp),
            dma(3),
            dma(n_dp),
        ],
        compiler_params=params(2),
        cost_estimate=cost(30_000_000_000, 60_000_000),
        name="mlp_backward",
    )(grad, middle, gains, *saved, *shards)
    return results[0], results[1], results[2:]


def attn_backward(grad, states, gains, dgain_mlp, tables, saved, shards):
    cosine, sine, _, place = tables
    n_dp = len(shards)
    rows, width = states.shape
    depth = width // n_dp
    columns = shards[0].shape[1]
    heads = place.shape[1] // PAD
    reach = reaches(rows)
    length = 4 * rows
    results = pl.pallas_call(
        functools.partial(attn_backward_kernel, n_dp, depth),
        out_shape=[shaped((rows, width), F32)]
        + [shaped((depth + GAIN_ROWS, columns), BF)] * n_dp,
        in_specs=[VM] * 7 + [ANY] * (7 + n_dp),
        out_specs=[VM] + [ANY] * n_dp,
        scratch_shapes=comm_scratch(rows, width)
        + [
            pltpu.VMEM((width, columns), BF),
            pltpu.VMEM((4, rows, width), BF),
            pltpu.VMEM((width, length), BF),
            pltpu.VMEM((length, 2 * heads * PAD), BF),
            pltpu.VMEM((length, place.shape[0]), BF),
        ]
        + [pltpu.VMEM((heads, rows, r), BF) for r in reach]
        + [
            pltpu.VMEM((length, heads * PAD), BF),
            pltpu.VMEM((length, heads * PAD), BF),
            pltpu.VMEM((length, heads * PAD), BF),
            pltpu.VMEM((length, heads // 2 * PAD), F32),
            pltpu.VMEM((length, heads // 2 * PAD), F32),
            pltpu.VMEM((length, 2 * place.shape[0]), BF),
            pltpu.VMEM((n_dp, depth + GAIN_ROWS, columns), BF),
            pltpu.VMEM((8, width), F32),
            dma(n_dp),
            dma(7),
            dma(n_dp),
        ],
        compiler_params=params(3),
        cost_estimate=cost(30_000_000_000, 60_000_000),
        name="attn_backward",
    )(grad, states, gains, dgain_mlp, cosine, sine, place, *saved, *shards)
    return results[0], results[1:]


def tables_of(documents, heads):
    length = documents.shape[0]
    places = jnp.arange(length, dtype=jnp.int32)
    head = jnp.sum((documents == 0).astype(jnp.int32))
    body_end = jnp.sum((documents <= 1).astype(jnp.int32))
    starts = jnp.where(documents == 0, 0, jnp.where(documents == 1, head, body_end))
    ends = jnp.where(documents == 0, head, jnp.where(documents == 1, body_end, length))
    offset = places - starts
    last = jnp.minimum(starts + (offset // BLOCK + 1) * BLOCK, ends)
    spans = jnp.stack([starts, last], axis=1)
    freqs = jnp.exp(
        jnp.arange(HALF, dtype=F32) * (-2.0 * math.log(rope_base) / HEAD_DIM)
    )
    angles = offset.astype(F32)[:, None] * freqs[None, :]
    gap = ((0, 0), (0, PAD // 2 - HALF))
    cos_half = jnp.pad(jnp.cos(angles), gap)
    sin_half = jnp.pad(jnp.sin(angles), gap)
    cosine = jnp.concatenate([cos_half, cos_half], axis=1)
    sine = jnp.concatenate([-sin_half, sin_half], axis=1)
    place = np.zeros((heads * HEAD_DIM, heads * PAD), np.float32)
    for row in range(heads * HEAD_DIM):
        which, column = divmod(row, HEAD_DIM)
        place[row, which * PAD + column + (PAD // 2 - HALF if column >= HALF else 0)] = 1.0
    return cosine, sine, spans, jnp.asarray(place, BF)


def pack_attn(gain_attn, query, key, value, output, gain_mlp):
    weights = jnp.concatenate([query, key, value, output.T], axis=1).astype(BF)
    depth, columns = weights.shape
    gains = jnp.stack([gain_attn, gain_mlp]).astype(BF)
    gains = jnp.pad(gains, ((0, GAIN_ROWS - 2), (0, columns - depth)))
    return jnp.concatenate([weights, gains], axis=0)


def pack_mlp(gate, up, down):
    return jnp.concatenate([gate, up, down.T], axis=1).astype(BF)


def across(value, count, shift, side):
    pairs = [
        (high * 2 + low, (high + shift) % count * 2 + (low + side) % 2)
        for high in range(count)
        for low in range(2)
    ]
    return lax.ppermute(value, "dp", pairs)


def fetch(pack, n_dp):
    count = n_dp // 2
    along = [pack] + [across(pack, count, shift, 0) for shift in range(1, count)]
    blocks = []
    for block in along:
        blocks += [block, across(block, count, 0, 1)]
    return blocks


def reduce_blocks(blocks):
    n_dp = len(blocks)
    count = n_dp // 2
    total = None
    for shift in range(count):
        arrived = across(blocks[2 * shift + 1], count, 0, 1)
        chunk = blocks[2 * shift].astype(F32) + arrived.astype(F32)
        if shift:
            chunk = across(chunk.astype(BF), count, shift, 0).astype(F32)
        total = chunk if total is None else total + chunk
    return total


def body(n_dp, states_in, documents, *rest):
    cotangent = rest[-1]
    layers = [rest[0:9], rest[9:18]]
    heads = layers[0][1].shape[1] // HEAD_DIM
    tables = tables_of(documents, heads)
    attn_packs = [pack_attn(w[0], w[1], w[2], w[3], w[4], w[5]) for w in layers]
    mlp_packs = [pack_mlp(w[6], w[7], w[8]) for w in layers]
    states = states_in
    kept = []
    for level in range(2):
        attn_shards = fetch(attn_packs[level], n_dp)
        mlp_shards = fetch(mlp_packs[level], n_dp)
        middle, gains, attn_saved = attn_forward(states, tables, attn_shards)
        result, mlp_saved = mlp_forward(middle, gains, mlp_shards)
        kept.append((states, middle, gains, attn_saved, mlp_saved, attn_shards, mlp_shards))
        states = result
    grad = cotangent
    parts = [None, None]
    for level in (1, 0):
        before, middle, gains, attn_saved, mlp_saved, attn_shards, mlp_shards = kept[level]
        (a_full, qkv, mixed, *probs) = attn_saved
        grad_middle, dgain_mlp, mlp_blocks = mlp_backward(grad, middle, gains, mlp_saved, mlp_shards)
        mlp_total = reduce_blocks(mlp_blocks)
        grad, attn_blocks = attn_backward(
            grad_middle, before, gains, dgain_mlp, tables, (a_full, qkv, mixed, *probs), attn_shards
        )
        attn_total = reduce_blocks(attn_blocks)
        parts[level] = (attn_total, mlp_total)
    depth = parts[0][1].shape[0]
    columns = [w.shape[1] for w in layers[0][1:4]]
    units = layers[0][6].shape[1]
    gains = lax.psum(
        jnp.concatenate([parts[level][0][depth : depth + 2, 0:depth] for level in range(2)], axis=0),
        "tensor",
    )
    outs = [states, grad]
    for level in range(2):
        attn_total, mlp_total = parts[level]
        attn_total = attn_total[0:depth]
        first = columns[0]
        second = first + columns[1]
        third = second + columns[2]
        outs += [
            gains[2 * level],
            attn_total[:, 0:first],
            attn_total[:, first:second],
            attn_total[:, second:third],
            attn_total[:, third:].T,
            gains[2 * level + 1],
            mlp_total[:, 0:units],
            mlp_total[:, units : 2 * units],
            mlp_total[:, 2 * units :].T,
        ]
    return tuple(outs)


def solution(mesh):
    layer = (
        P("dp"),
        P("dp", "tensor"),
        P("dp", "tensor"),
        P("dp", "tensor"),
        P("tensor", "dp"),
        P("dp"),
        P("dp", "tensor"),
        P("dp", "tensor"),
        P("tensor", "dp"),
    )
    rows = P(("dp", "tensor"), None)
    return jax.shard_map(
        functools.partial(body, mesh.shape["dp"]),
        mesh=mesh,
        in_specs=(rows, P("dp"), *layer, *layer, rows),
        out_specs=(rows, rows, *layer, *layer),
        check_vma=False,
    )
```

time: 2310 us -> 1190 us (0.52)
  waiting for transfers between devices: 1660 us -> 513 us
  Pallas kernels: 0 us -> 507 us
  matrix products: 278 us -> 0 us
  blocking collectives: 205 us -> 6.08 us
  starting transfers between devices: 3.25 us -> 111 us
  other arithmetic: 108 us -> 24.3 us
    reduce_scatter x22 -> x0, waiting for transfers between devices: 1140 us -> none  [the longest x2 151 us: layer_backward(): lax.psum_scatter(grad_gate.astype(jnp.bfloat16), 'dp', scatter_dimension=...]
    all_gather x18 -> x0, waiting for transfers between devices: 518 us -> none  [the longest x2 114 us: fetch_mlp(): lax.all_gather(low_down, 'dp', axis=1, tiled=True)]
    ppermute x0 -> x56, waiting for transfers between devices: none -> 513 us  [across(): return lax.ppermute(value, 'dp', pairs)]
    pallas_call x0 -> x8, Pallas kernels: none -> 507 us  [the longest x2 138 us: attn_forward(): pl.pallas_call(functools.partial(attn_forward_kernel, n_dp, depth), out_s...]
    dot_general x66 -> x0, matrix products: 278 us -> none  [the longest x14 76.3 us: dot_rows(): lax.dot_general(left, right, (((0,), (0,)), ((), ())), preferred_element_...]
    all_gather x4 -> x0, blocking collectives: 133 us -> none  [the longest x2 67.4 us: fetch_attn(): lax.all_gather(low_key, 'dp', axis=0, tiled=True)]
    ppermute x0 -> x56, starting transfers between devices: none -> 111 us  [across(): return lax.ppermute(value, 'dp', pairs)]
    convert_element_type x53 -> x12, other arithmetic: 74.1 us -> 8.45 us  [reduce_blocks(): chunk = across(chunk.astype(BF), count, shift, 0).astype(F32)]
  transfers between devices with their start and end apart: 40 -> 56, of which waited for: 35 -> 25; matrix products, arithmetic and copies ran while one was open for 12% -> 2% of each run, Pallas kernels for 0% -> 16%
where the time goes in v1:
time: 1190 us; the launch traced here: 1180 us
  waiting for transfers between devices  513 us (43%)
  Pallas kernels  507 us (43%)
  starting transfers between devices  111 us (9%)
  other arithmetic  24.3 us (2%)
  local copies, waits for them, and re-layouts  14.9 us (1%)
    ppermute x56, waiting for transfers between devices, across(): return lax.ppermute(value, 'dp', pairs)  513 us
    pallas_call x2, Pallas kernels, attn_forward(): pl.pallas_call(functools.partial(attn_forward_kernel, n_dp, depth), out_s...  138 us
    pallas_call x2, Pallas kernels, attn_backward(): pl.pallas_call(functools.partial(attn_backward_kernel, n_dp, depth), out_...  138 us
    pallas_call x2, Pallas kernels, mlp_backward(): pl.pallas_call(functools.partial(mlp_backward_kernel, n_dp, depth), out_s...  126 us
    ppermute x56, starting transfers between devices, across(): return lax.ppermute(value, 'dp', pairs)  111 us
    pallas_call x2, Pallas kernels, mlp_forward(): pl.pallas_call(functools.partial(mlp_forward_kernel, n_dp), out_shape=[sh...  106 us
  transfers between devices with their start and end apart: 56, of which 25 were waited for; matrix products, arithmetic and copies ran while one was open for 2% of the time, Pallas kernels for 16%

profile of v1, /device:TPU:28, one launch (start us, length us, event | category | flops | bytes accessed | tf_op | source)
XLA Modules:
  0.0 1178.5 jit_solution(13197319473887088668)
XLA Ops:
  22.1 17.9 %collective-permute-start.3 = (bf16[208,1152]{1,0:T(8,128)(2,1)S(1)}, bf16[208,1152]{1,0:T(8,128)(2,1)S(1)}, u32[]{:S(2)}, u32[]{:S(2)}) collective-permute-start(bf16[208,1152]{1,0:T(8,128)(2,1)S(1)} %pad_maximum_fusion.4.refs_5_.refs_14_), channel_id=1, source_target_pairs={{0,16},{4,20},{8,24},{12,28},{16,0},{20,4},{24,8},{28,12},{1,17},{... | collective-permute-start | bytes 1437704 | tf_op jit(solution)/shard_map/ppermute | solution.py:937
  40.0 21.1 %collective-permute-done.17.refs_9_.refs_18_ = bf16[208,1152]{1,0:T(8,128)(2,1)} collective-permute-done((bf16[208,1152]{1,0:T(8,128)(2,1)}, bf16[208,1152]{1,0:T(8,128)(2,1)}, u32[]{:S(2)}, u32[]{:S(2)}) %collective-permute-start.17) | collective-permute-done | bytes 479264 | tf_op jit(solution)/shard_map/ppermute | solution.py:937
  62.6 11.5 collective-permute-start.12
  78.4 54.8 %collective-permute-done.3.refs_9_.refs_18_ = bf16[208,1152]{1,0:T(8,128)(2,1)S(1)} collective-permute-done((bf16[208,1152]{1,0:T(8,128)(2,1)S(1)}, bf16[208,1152]{1,0:T(8,128)(2,1)S(1)}, u32[]{:S(2)}, u32[]{:S(2)}) %collective-permute-start.3) | collective-permute-done | bytes 479264 | tf_op jit(solution)/shard_map/ppermute | solution.py:937
  137.7 9.5 collective-permute-done.refs_6_.refs_15_
  148.7 8.8 collective-permute-done.6.refs_12_.refs_21_
  182.0 69.0 %attn_forward.2 = (f32[256,1536]{1,0:T(8,128)}, f32[16,1536]{1,0:T(8,128)}, bf16[4,256,1536]{2,1,0:T(8,128)(2,1)}, bf16[1024,1024]{1,0:T(8,128)(2,1)}, bf16[1024...) custom-call(f32[256,1536]{1,0:T(8,128)} %refs_1_.1, ...), custom_call_target="tpu_custom_call" | custom-call | flops 20000000000 | bytes 60000000 | tf_op jit(solution)/shard_map/attn_forward/pallas_call | solution.py:755
  251.0 13.4 %collective-permute-start.26 = (bf16[192,3072]{1,0:T(8,128)(2,1)S(1)}, bf16[192,3072]{1,0:T(8,128)(2,1)}, u32[]{:S(2)}, u32[]{:S(2)}) collective-permute-start(bf16[192,3072]{1,0:T(8,128)(2,1)S(1)} %pad_maximum_fusion.1.refs_2_.refs_6_), channel_id=1, source_target_pairs={{0,24},{4,28},{8,0},{12,4},{16,8},{20,12},{24,16},{28,20},{1,25},{... | collective-permute-start | bytes 3538952 | tf_op jit(solution)/shard_map/ppermute | solution.py:937
  267.4 22.0 %collective-permute-done.9.refs_5_.refs_9_ = bf16[192,3072]{1,0:T(8,128)(2,1)} collective-permute-done((bf16[192,3072]{1,0:T(8,128)(2,1)}, bf16[192,3072]{1,0:T(8,128)(2,1)}, u32[]{:S(2)}, u32[]{:S(2)}) %collective-permute-start.9) | collective-permute-done | bytes 1179680 | tf_op jit(solution)/shard_map/ppermute | solution.py:937
  290.9 52.7 %mlp_forward.2 = (f32[256,1536]{1,0:T(8,128)}, bf16[4,256,1536]{2,1,0:T(8,128)(2,1)}, bf16[1024,2048]{1,0:T(8,128)(2,1)}, bf16[1024,1024]{1,0:T(8,128)(2,1)}) custom-call(f32[256,1536]{1,0:T(8,128)} %get-tuple-element.84.refs_0_.refs_1_, f32[16,1536]{1,0:T(8,128)} %get-tuple-element.85.refs_1_.refs_2_, bf16[192,3072]{1,0:T(8,128)(2,1)} %copy-done.8, ...), custom_call_target="tpu_custom_call" | custom-call | flops 20000000000 | bytes 60000000 | tf_op jit(solution)/shard_map/mlp_forward/pallas_call | solution.py:791
  347.8 69.4 %attn_forward.3 = (f32[256,1536]{1,0:T(8,128)}, f32[16,1536]{1,0:T(8,128)}, bf16[4,256,1536]{2,1,0:T(8,128)(2,1)}, bf16[1024,1024]{1,0:T(8,128)(2,1)}, bf16[1024...) custom-call(f32[256,1536]{1,0:T(8,128)} %get-tuple-element.86.refs_0, ...), custom_call_target="tpu_custom_call" | custom-call | flops 20000000000 | bytes 60000000 | tf_op jit(solution)/shard_map/attn_forward/pallas_call | solution.py:755
  423.3 23.2 %collective-permute-done.23.refs_5_.refs_9_ = bf16[192,3072]{1,0:T(8,128)(2,1)} collective-permute-done((bf16[192,3072]{1,0:T(8,128)(2,1)}, bf16[192,3072]{1,0:T(8,128)(2,1)}, u32[]{:S(2)}, u32[]{:S(2)}) %collective-permute-start.23) | collective-permute-done | bytes 1179680 | tf_op jit(solution)/shard_map/ppermute | solution.py:937
  446.5 52.9 %mlp_forward.3 = (f32[256,1536]{1,0:T(8,128)}, bf16[4,256,1536]{2,1,0:T(8,128)(2,1)}, bf16[1024,2048]{1,0:T(8,128)(2,1)}, bf16[1024,1024]{1,0:T(8,128)(2,1)}) custom-call(f32[256,1536]{1,0:T(8,128)} %get-tuple-element.87.refs_0_.refs_1_, f32[16,1536]{1,0:T(8,128)} %get-tuple-element.88.refs_1_.refs_2_, bf16[192,3072]{1,0:T(8,128)(2,1)} %copy-done.9, ...), custom_call_target="tpu_custom_call" | custom-call | flops 20000000000 | bytes 60000000 | tf_op jit(solution)/shard_map/mlp_forward/pallas_call | solution.py:791
  499.5 62.4 %mlp_backward.2 = (f32[256,1536]{1,0:T(8,128)}, f32[8,1536]{1,0:T(8,128)}, bf16[192,3072]{1,0:T(8,128)(2,1)}, bf16[192,3072]{1,0:T(8,128)(2,1)}, bf16[192,3072]{...) custom-call(f32[256,1536]{1,0:T(8,128)} %refs_0_.3, ...), custom_call_target="tpu_custom_call" | custom-call | flops 30000001024 | bytes 60000000 | tf_op jit(solution)/shard_map/mlp_backward/pallas_call | solution.py:823
  561.9 68.9 %attn_backward.2 = (f32[256,1536]{1,0:T(8,128)}, bf16[208,1152]{1,0:T(8,128)(2,1)}, bf16[208,1152]{1,0:T(8,128)(2,1)}, bf16[208,1152]{1,0:T(8,128)(2,1)}, bf16[2...) custom-call(f32[256,1536]{1,0:T(8,128)} %get-tuple-element.93.refs_0, ...), custom_call_target="tpu_custom_call" | custom-call | flops 30000001024 | bytes 60000000 | tf_op jit(solution)/shard_map/attn_backward/pallas_call | solution.py:858
  630.8 63.2 %mlp_backward.3 = (f32[256,1536]{1,0:T(8,128)}, f32[8,1536]{1,0:T(8,128)}, bf16[192,3072]{1,0:T(8,128)(2,1)}, bf16[192,3072]{1,0:T(8,128)(2,1)}, bf16[192,3072]{...) custom-call(f32[256,1536]{1,0:T(8,128)} %get-tuple-element.102.refs_, ...), custom_call_target="tpu_custom_call" | custom-call | flops 30000001024 | bytes 60000000 | tf_op jit(solution)/shard_map/mlp_backward/pallas_call | solution.py:823
  694.0 68.8 %attn_backward.3 = (f32[256,1536]{1,0:T(8,128)}, bf16[208,1152]{1,0:T(8,128)(2,1)}, bf16[208,1152]{1,0:T(8,128)(2,1)}, bf16[208,1152]{1,0:T(8,128)(2,1)}, bf16[2...) custom-call(f32[256,1536]{1,0:T(8,128)} %get-tuple-element.106.refs_, ...), custom_call_target="tpu_custom_call" | custom-call | flops 30000001024 | bytes 60000000 | tf_op jit(solution)/shard_map/attn_backward/pallas_call | solution.py:858
  767.5 9.5 collective-permute-done.29
  778.8 18.8 %collective-permute-done.31 = bf16[208,1152]{1,0:T(8,128)(2,1)S(1)} collective-permute-done((bf16[208,1152]{1,0:T(8,128)(2,1)}, bf16[208,1152]{1,0:T(8,128)(2,1)S(1)}, u32[]{:S(2)}, u32[]{:S(2)}) %collective-permute-start.31) | collective-permute-done | bytes 479264 | tf_op jit(solution)/shard_map/ppermute | solution.py:937
  798.2 9.6 collective-permute-done.33
  808.5 19.9 %collective-permute-done.36 = bf16[208,1152]{1,0:T(8,128)(2,1)S(1)} collective-permute-done((bf16[208,1152]{1,0:T(8,128)(2,1)S(1)}, bf16[208,1152]{1,0:T(8,128)(2,1)S(1)}, u32[]{:S(2)}, u32[]{:S(2)}) %collective-permute-start.36) | collective-permute-done | bytes 479264 | tf_op jit(solution)/shard_map/ppermute | solution.py:937
  828.5 10.1 collective-permute-done.38
  851.1 21.0 %collective-permute-done.32 = bf16[208,1152]{1,0:T(8,128)(2,1)S(1)} collective-permute-done((bf16[208,1152]{1,0:T(8,128)(2,1)S(1)}, bf16[208,1152]{1,0:T(8,128)(2,1)S(1)}, u32[]{:S(2)}, u32[]{:S(2)}) %collective-permute-start.32) | collective-permute-done | bytes 479264 | tf_op jit(solution)/shard_map/ppermute | solution.py:937
  872.0 15.5 %collective-permute-start.41 = (bf16[208,1152]{1,0:T(8,128)(2,1)S(1)}, bf16[208,1152]{1,0:T(8,128)(2,1)S(1)}, u32[]{:S(2)}, u32[]{:S(2)}) collective-permute-start(bf16[208,1152]{1,0:T(8,128)(2,1)S(1)} %add_convert_fusion.6), channel_id=1, source_target_pairs={{0,24},{4,28},{8,0},{12,4},{16,8},{20,12},{24,16},{28,20},{1,25},{... | collective-permute-start | bytes 1437704 | tf_op jit(solution)/shard_map/ppermute | solution.py:937
  890.0 19.4 %collective-permute-done.39 = bf16[208,1152]{1,0:T(8,128)(2,1)S(1)} collective-permute-done((bf16[208,1152]{1,0:T(8,128)(2,1)S(1)}, bf16[208,1152]{1,0:T(8,128)(2,1)S(1)}, u32[]{:S(2)}, u32[]{:S(2)}) %collective-permute-start.39) | collective-permute-done | bytes 479264 | tf_op jit(solution)/shard_map/ppermute | solution.py:937
  924.0 18.4 %collective-permute-done.45 = bf16[192,3072]{1,0:T(8,128)(2,1)} collective-permute-done((bf16[192,3072]{1,0:T(8,128)(2,1)}, bf16[192,3072]{1,0:T(8,128)(2,1)}, u32[]{:S(2)}, u32[]{:S(2)}) %collective-permute-start.45) | collective-permute-done | bytes 1179680 | tf_op jit(solution)/shard_map/ppermute | solution.py:937
  944.7 23.0 %collective-permute-done.47 = bf16[192,3072]{1,0:T(8,128)(2,1)} collective-permute-done((bf16[192,3072]{1,0:T(8,128)(2,1)}, bf16[192,3072]{1,0:T(8,128)(2,1)}, u32[]{:S(2)}, u32[]{:S(2)}) %collective-permute-start.47) | collective-permute-done | bytes 1179680 | tf_op jit(solution)/shard_map/ppermute | solution.py:937
  969.5 23.4 %collective-permute-done.50 = bf16[192,3072]{1,0:T(8,128)(2,1)S(1)} collective-permute-done((bf16[192,3072]{1,0:T(8,128)(2,1)}, bf16[192,3072]{1,0:T(8,128)(2,1)S(1)}, u32[]{:S(2)}, u32[]{:S(2)}) %collective-permute-start.50) | collective-permute-done | bytes 1179680 | tf_op jit(solution)/shard_map/ppermute | solution.py:937
  995.2 23.0 %collective-permute-done.52 = bf16[192,3072]{1,0:T(8,128)(2,1)S(1)} collective-permute-done((bf16[192,3072]{1,0:T(8,128)(2,1)S(1)}, bf16[192,3072]{1,0:T(8,128)(2,1)S(1)}, u32[]{:S(2)}, u32[]{:S(2)}) %collective-permute-start.52) | collective-permute-done | bytes 1179680 | tf_op jit(solution)/shard_map/ppermute | solution.py:937
  1021.0 21.0 %collective-permute-done.54 = bf16[192,3072]{1,0:T(8,128)(2,1)S(1)} collective-permute-done((bf16[192,3072]{1,0:T(8,128)(2,1)S(1)}, bf16[192,3072]{1,0:T(8,128)(2,1)S(1)}, u32[]{:S(2)}, u32[]{:S(2)}) %collective-permute-start.54) | collective-permute-done | bytes 1179680 | tf_op jit(solution)/shard_map/ppermute | solution.py:937
  1047.0 62.6 %collective-permute-done.46 = bf16[192,3072]{1,0:T(8,128)(2,1)S(1)} collective-permute-done((bf16[192,3072]{1,0:T(8,128)(2,1)S(1)}, bf16[192,3072]{1,0:T(8,128)(2,1)S(1)}, u32[]{:S(2)}, u32[]{:S(2)}) %collective-permute-start.46) | collective-permute-done | bytes 1179680 | tf_op jit(solution)/shard_map/ppermute | solution.py:937
  1113.3 58.5 %collective-permute-done.53 = bf16[192,3072]{1,0:T(8,128)(2,1)S(1)} collective-permute-done((bf16[192,3072]{1,0:T(8,128)(2,1)S(1)}, bf16[192,3072]{1,0:T(8,128)(2,1)S(1)}, u32[]{:S(2)}, u32[]{:S(2)}) %collective-permute-start.53) | collective-permute-done | bytes 1179680 | tf_op jit(solution)/shard_map/ppermute | solution.py:937
  (259 shorter events, 133.3 us)
Async XLA Ops:
  9.9 64.2 %collective-permute-start.14 = (bf16[208,1152]{1,0:T(8,128)(2,1)}, bf16[208,1152]{1,0:T(8,128)(2,1)}, u32[]{:S(2)}, u32[]{:S(2)}) collective-permute-start(bf16[208,1152]{1,0:T(8,128)(2,1)} %pad_maximum_fusion.5.refs_5_.refs_14_), channel_id=1, source_target_pairs={{0,4},{4,0},{8,12},{12,8},{16,20},{20,16},{24,28},{28,24},{1,5},{5... | collective-permute-start | bytes 1437704 | tf_op jit(solution)/shard_map/ppermute | solution.py:937
  11.8 62.3 %collective-permute-start.5 = (bf16[208,1152]{1,0:T(8,128)(2,1)S(1)}, bf16[208,1152]{1,0:T(8,128)(2,1)}, u32[]{:S(2)}, u32[]{:S(2)}) collective-permute-start(bf16[208,1152]{1,0:T(8,128)(2,1)S(1)} %pad_maximum_fusion.4.refs_5_.refs_14_), channel_id=1, source_target_pairs={{0,24},{4,28},{8,0},{12,4},{16,8},{20,12},{24,16},{28,20},{1,25},{... | collective-permute-start | bytes 1437704 | tf_op jit(solution)/shard_map/ppermute | solution.py:937
  22.1 111.1 %collective-permute-start.3 = (bf16[208,1152]{1,0:T(8,128)(2,1)S(1)}, bf16[208,1152]{1,0:T(8,128)(2,1)S(1)}, u32[]{:S(2)}, u32[]{:S(2)}) collective-permute-start(bf16[208,1152]{1,0:T(8,128)(2,1)S(1)} %pad_maximum_fusion.4.refs_5_.refs_14_), channel_id=1, source_target_pairs={{0,16},{4,20},{8,24},{12,28},{16,0},{20,4},{24,8},{28,12},{1,17},{... | collective-permute-start | bytes 1437704 | tf_op jit(solution)/shard_map/ppermute | solution.py:937
  61.1 73.6 %collective-permute-start.1 = (bf16[208,1152]{1,0:T(8,128)(2,1)S(1)}, bf16[208,1152]{1,0:T(8,128)(2,1)S(1)}, u32[]{:S(2)}, u32[]{:S(2)}) collective-permute-start(bf16[208,1152]{1,0:T(8,128)(2,1)S(1)} %pad_maximum_fusion.4.refs_5_.refs_14_), channel_id=1, source_target_pairs={{0,8},{4,12},{8,16},{12,20},{16,24},{20,28},{24,0},{28,4},{1,9},{5... | collective-permute-start | bytes 1437704 | tf_op jit(solution)/shard_map/ppermute | solution.py:937
  62.6 116.8 %collective-permute-start.12 = (bf16[192,3072]{1,0:T(8,128)(2,1)S(1)}, bf16[192,3072]{1,0:T(8,128)(2,1)}, u32[]{:S(2)}, u32[]{:S(2)}) collective-permute-start(bf16[192,3072]{1,0:T(8,128)(2,1)S(1)} %pad_maximum_fusion.refs_2_.refs_6_), channel_id=1, source_target_pairs={{0,24},{4,28},{8,0},{12,4},{16,8},{20,12},{24,16},{28,20},{1,25},{... | collective-permute-start | bytes 3538952 | tf_op jit(solution)/shard_map/ppermute | solution.py:937
  74.1 105.8 %collective-permute-start.10 = (bf16[192,3072]{1,0:T(8,128)(2,1)S(1)}, bf16[192,3072]{1,0:T(8,128)(2,1)}, u32[]{:S(2)}, u32[]{:S(2)}) collective-permute-start(bf16[192,3072]{1,0:T(8,128)(2,1)S(1)} %pad_maximum_fusion.refs_2_.refs_6_), channel_id=1, source_target_pairs={{0,16},{4,20},{8,24},{12,28},{16,0},{20,4},{24,8},{28,12},{1,17},{... | collective-permute-start | bytes 3538952 | tf_op jit(solution)/shard_map/ppermute | solution.py:937
  74.1 107.3 %collective-permute-start.8 = (bf16[192,3072]{1,0:T(8,128)(2,1)S(1)}, bf16[192,3072]{1,0:T(8,128)(2,1)}, u32[]{:S(2)}, u32[]{:S(2)}) collective-permute-start(bf16[192,3072]{1,0:T(8,128)(2,1)S(1)} %pad_maximum_fusion.refs_2_.refs_6_), channel_id=1, source_target_pairs={{0,8},{4,12},{8,16},{12,20},{16,24},{20,28},{24,0},{28,4},{1,9},{5... | collective-permute-start | bytes 3538952 | tf_op jit(solution)/shard_map/ppermute | solution.py:937
  167.7 96.7 %collective-permute-start.7 = (bf16[192,3072]{1,0:T(8,128)(2,1)S(1)}, bf16[192,3072]{1,0:T(8,128)(2,1)S(1)}, u32[]{:S(2)}, u32[]{:S(2)}) collective-permute-start(bf16[192,3072]{1,0:T(8,128)(2,1)S(1)} %pad_maximum_fusion.refs_2_.refs_6_), channel_id=1, source_target_pairs={{0,4},{4,0},{8,12},{12,8},{16,20},{20,16},{24,28},{28,24},{1,5},{5... | collective-permute-start | bytes 3538952 | tf_op jit(solution)/shard_map/ppermute | solution.py:937
  177.9 73.1 %collective-permute-start.20 = (bf16[208,1152]{1,0:T(8,128)(2,1)}, bf16[208,1152]{1,0:T(8,128)(2,1)}, u32[]{:S(2)}, u32[]{:S(2)}) collective-permute-start(bf16[208,1152]{1,0:T(8,128)(2,1)} %collective-permute-done.19.refs_11_.refs_20_), channel_id=1, source_target_pairs={{0,4},{4,0},{8,12},{12,8},{16,20},{20,16},{24,28},{28,24},{1,5},{5... | collective-permute-start | bytes 1437704 | tf_op jit(solution)/shard_map/ppermute | solution.py:937
  179.4 85.6 %collective-permute-start.13 = (bf16[192,3072]{1,0:T(8,128)(2,1)}, bf16[192,3072]{1,0:T(8,128)(2,1)}, u32[]{:S(2)}, u32[]{:S(2)}) collective-permute-start(bf16[192,3072]{1,0:T(8,128)(2,1)} %collective-permute-done.12.refs_8_.refs_12_), channel_id=1, source_target_pairs={{0,4},{4,0},{8,12},{12,8},{16,20},{20,16},{24,28},{28,24},{1,5},{5... | collective-permute-start | bytes 3538952 | tf_op jit(solution)/shard_map/ppermute | solution.py:937
  180.0 86.9 %collective-permute-start.11 = (bf16[192,3072]{1,0:T(8,128)(2,1)}, bf16[192,3072]{1,0:T(8,128)(2,1)}, u32[]{:S(2)}, u32[]{:S(2)}) collective-permute-start(bf16[192,3072]{1,0:T(8,128)(2,1)} %collective-permute-done.10.refs_6_.refs_10_), channel_id=1, source_target_pairs={{0,4},{4,0},{8,12},{12,8},{16,20},{20,16},{24,28},{28,24},{1,5},{5... | collective-permute-start | bytes 3538952 | tf_op jit(solution)/shard_map/ppermute | solution.py:937
  181.5 108.0 %collective-permute-start.9 = (bf16[192,3072]{1,0:T(8,128)(2,1)}, bf16[192,3072]{1,0:T(8,128)(2,1)}, u32[]{:S(2)}, u32[]{:S(2)}) collective-permute-start(bf16[192,3072]{1,0:T(8,128)(2,1)} %collective-permute-done.8.refs_4_.refs_8_), channel_id=1, source_target_pairs={{0,4},{4,0},{8,12},{12,8},{16,20},{20,16},{24,28},{28,24},{1,5},{5... | collective-permute-start | bytes 3538952 | tf_op jit(solution)/shard_map/ppermute | solution.py:937
  251.0 93.3 %collective-permute-start.26 = (bf16[192,3072]{1,0:T(8,128)(2,1)S(1)}, bf16[192,3072]{1,0:T(8,128)(2,1)}, u32[]{:S(2)}, u32[]{:S(2)}) collective-permute-start(bf16[192,3072]{1,0:T(8,128)(2,1)S(1)} %pad_maximum_fusion.1.refs_2_.refs_6_), channel_id=1, source_target_pairs={{0,24},{4,28},{8,0},{12,4},{16,8},{20,12},{24,16},{28,20},{1,25},{... | collective-permute-start | bytes 3538952 | tf_op jit(solution)/shard_map/ppermute | solution.py:937
  264.4 81.4 %collective-permute-start.24 = (bf16[192,3072]{1,0:T(8,128)(2,1)S(1)}, bf16[192,3072]{1,0:T(8,128)(2,1)S(1)}, u32[]{:S(2)}, u32[]{:S(2)}) collective-permute-start(bf16[192,3072]{1,0:T(8,128)(2,1)S(1)} %pad_maximum_fusion.1.refs_2_.refs_6_), channel_id=1, source_target_pairs={{0,16},{4,20},{8,24},{12,28},{16,0},{20,4},{24,8},{28,12},{1,17},{... | collective-permute-start | bytes 3538952 | tf_op jit(solution)/shard_map/ppermute | solution.py:937
  265.0 81.3 %collective-permute-start.22 = (bf16[192,3072]{1,0:T(8,128)(2,1)S(1)}, bf16[192,3072]{1,0:T(8,128)(2,1)}, u32[]{:S(2)}, u32[]{:S(2)}) collective-permute-start(bf16[192,3072]{1,0:T(8,128)(2,1)S(1)} %pad_maximum_fusion.1.refs_2_.refs_6_), channel_id=1, source_target_pairs={{0,8},{4,12},{8,16},{12,20},{16,24},{20,28},{24,0},{28,4},{1,9},{5... | collective-permute-start | bytes 3538952 | tf_op jit(solution)/shard_map/ppermute | solution.py:937
  266.9 76.8 %collective-permute-start.18 = (bf16[208,1152]{1,0:T(8,128)(2,1)}, bf16[208,1152]{1,0:T(8,128)(2,1)S(1)}, u32[]{:S(2)}, u32[]{:S(2)}) collective-permute-start(bf16[208,1152]{1,0:T(8,128)(2,1)} %collective-permute-done.17.refs_9_.refs_18_), channel_id=1, source_target_pairs={{0,4},{4,0},{8,12},{12,8},{16,20},{20,16},{24,28},{28,24},{1,5},{5... | collective-permute-start | bytes 1437704 | tf_op jit(solution)/shard_map/ppermute | solution.py:937
  343.7 73.6 %collective-permute-start.21 = (bf16[192,3072]{1,0:T(8,128)(2,1)S(1)}, bf16[192,3072]{1,0:T(8,128)(2,1)S(1)}, u32[]{:S(2)}, u32[]{:S(2)}) collective-permute-start(bf16[192,3072]{1,0:T(8,128)(2,1)S(1)} %pad_maximum_fusion.1.refs_2_.refs_6_), channel_id=1, source_target_pairs={{0,4},{4,0},{8,12},{12,8},{16,20},{20,16},{24,28},{28,24},{1,5},{5... | collective-permute-start | bytes 3538952 | tf_op jit(solution)/shard_map/ppermute | solution.py:937
  344.3 73.0 %collective-permute-start.27 = (bf16[192,3072]{1,0:T(8,128)(2,1)}, bf16[192,3072]{1,0:T(8,128)(2,1)}, u32[]{:S(2)}, u32[]{:S(2)}) collective-permute-start(bf16[192,3072]{1,0:T(8,128)(2,1)} %collective-permute-done.26.refs_8_.refs_12_), channel_id=1, source_target_pairs={{0,4},{4,0},{8,12},{12,8},{16,20},{20,16},{24,28},{28,24},{1,5},{5... | collective-permute-start | bytes 3538952 | tf_op jit(solution)/shard_map/ppermute | solution.py:937
  345.8 77.5 %collective-permute-start.25 = (bf16[192,3072]{1,0:T(8,128)(2,1)S(1)}, bf16[192,3072]{1,0:T(8,128)(2,1)}, u32[]{:S(2)}, u32[]{:S(2)}) collective-permute-start(bf16[192,3072]{1,0:T(8,128)(2,1)S(1)} %collective-permute-done.24.refs_6_.refs_10_), channel_id=1, source_target_pairs={{0,4},{4,0},{8,12},{12,8},{16,20},{20,16},{24,28},{28,24},{1,5},{5... | collective-permute-start | bytes 3538952 | tf_op jit(solution)/shard_map/ppermute | solution.py:937
  346.3 100.2 %collective-permute-start.23 = (bf16[192,3072]{1,0:T(8,128)(2,1)}, bf16[192,3072]{1,0:T(8,128)(2,1)}, u32[]{:S(2)}, u32[]{:S(2)}) collective-permute-start(bf16[192,3072]{1,0:T(8,128)(2,1)} %collective-permute-done.22.refs_4_.refs_8_), channel_id=1, source_target_pairs={{0,4},{4,0},{8,12},{12,8},{16,20},{20,16},{24,28},{28,24},{1,5},{5... | collective-permute-start | bytes 3538952 | tf_op jit(solution)/shard_map/ppermute | solution.py:937
  763.4 84.0 %collective-permute-start.28 = (bf16[208,1152]{1,0:T(8,128)(2,1)}, bf16[208,1152]{1,0:T(8,128)(2,1)S(1)}, u32[]{:S(2)}, u32[]{:S(2)}) collective-permute-start(bf16[208,1152]{1,0:T(8,128)(2,1)} %get-tuple-element.117), channel_id=1, source_target_pairs={{0,4},{4,0},{8,12},{12,8},{16,20},{20,16},{24,28},{28,24},{1,5},{5... | collective-permute-start | bytes 1437704 | tf_op jit(solution)/shard_map/ppermute | solution.py:937
  767.0 120.9 %collective-permute-start.35 = (bf16[208,1152]{1,0:T(8,128)(2,1)S(1)}, bf16[208,1152]{1,0:T(8,128)(2,1)S(1)}, u32[]{:S(2)}, u32[]{:S(2)}) collective-permute-start(bf16[208,1152]{1,0:T(8,128)(2,1)S(1)} %copy-done.44), channel_id=1, source_target_pairs={{0,4},{4,0},{8,12},{12,8},{16,20},{20,16},{24,28},{28,24},{1,5},{5... | collective-permute-start | bytes 1437704 | tf_op jit(solution)/shard_map/ppermute | solution.py:937
  847.4 195.6 %collective-permute-start.42 = (bf16[192,3072]{1,0:T(8,128)(2,1)}, bf16[192,3072]{1,0:T(8,128)(2,1)}, u32[]{:S(2)}, u32[]{:S(2)}) collective-permute-start(bf16[192,3072]{1,0:T(8,128)(2,1)} %get-tuple-element.133), channel_id=1, source_target_pairs={{0,4},{4,0},{8,12},{12,8},{16,20},{20,16},{24,28},{28,24},{1,5},{5... | collective-permute-start | bytes 3538952 | tf_op jit(solution)/shard_map/ppermute | solution.py:937
  909.9 83.0 %collective-permute-start.50 = (bf16[192,3072]{1,0:T(8,128)(2,1)}, bf16[192,3072]{1,0:T(8,128)(2,1)S(1)}, u32[]{:S(2)}, u32[]{:S(2)}) collective-permute-start(bf16[192,3072]{1,0:T(8,128)(2,1)} %get-tuple-element.143), channel_id=1, source_target_pairs={{0,4},{4,0},{8,12},{12,8},{16,20},{20,16},{24,28},{28,24},{1,5},{5... | collective-permute-start | bytes 3538952 | tf_op jit(solution)/shard_map/ppermute | solution.py:937
  921.6 96.5 %collective-permute-start.52 = (bf16[192,3072]{1,0:T(8,128)(2,1)S(1)}, bf16[192,3072]{1,0:T(8,128)(2,1)S(1)}, u32[]{:S(2)}, u32[]{:S(2)}) collective-permute-start(bf16[192,3072]{1,0:T(8,128)(2,1)S(1)} %copy-done.34), channel_id=1, source_target_pairs={{0,4},{4,0},{8,12},{12,8},{16,20},{20,16},{24,28},{28,24},{1,5},{5... | collective-permute-start | bytes 3538952 | tf_op jit(solution)/shard_map/ppermute | solution.py:937
  942.4 99.6 %collective-permute-start.54 = (bf16[192,3072]{1,0:T(8,128)(2,1)S(1)}, bf16[192,3072]{1,0:T(8,128)(2,1)S(1)}, u32[]{:S(2)}, u32[]{:S(2)}) collective-permute-start(bf16[192,3072]{1,0:T(8,128)(2,1)S(1)} %copy-done.33), channel_id=1, source_target_pairs={{0,4},{4,0},{8,12},{12,8},{16,20},{20,16},{24,28},{28,24},{1,5},{5... | collective-permute-start | bytes 3538952 | tf_op jit(solution)/shard_map/ppermute | solution.py:937
  967.7 75.4 %collective-permute-start.44 = (bf16[192,3072]{1,0:T(8,128)(2,1)S(1)}, bf16[192,3072]{1,0:T(8,128)(2,1)S(1)}, u32[]{:S(2)}, u32[]{:S(2)}) collective-permute-start(bf16[192,3072]{1,0:T(8,128)(2,1)S(1)} %add_convert_fusion.5), channel_id=1, source_target_pairs={{0,8},{4,12},{8,16},{12,20},{16,24},{20,28},{24,0},{28,4},{1,9},{5... | collective-permute-start | bytes 3538952 | tf_op jit(solution)/shard_map/ppermute | solution.py:937
  992.9 116.8 %collective-permute-start.46 = (bf16[192,3072]{1,0:T(8,128)(2,1)S(1)}, bf16[192,3072]{1,0:T(8,128)(2,1)S(1)}, u32[]{:S(2)}, u32[]{:S(2)}) collective-permute-start(bf16[192,3072]{1,0:T(8,128)(2,1)S(1)} %add_convert_fusion.4), channel_id=1, source_target_pairs={{0,16},{4,20},{8,24},{12,28},{16,0},{20,4},{24,8},{28,12},{1,17},{... | collective-permute-start | bytes 3538952 | tf_op jit(solution)/shard_map/ppermute | solution.py:937
  1018.1 91.5 %collective-permute-start.48 = (bf16[192,3072]{1,0:T(8,128)(2,1)S(1)}, bf16[192,3072]{1,0:T(8,128)(2,1)S(1)}, u32[]{:S(2)}, u32[]{:S(2)}) collective-permute-start(bf16[192,3072]{1,0:T(8,128)(2,1)S(1)} %add_convert_fusion.3), channel_id=1, source_target_pairs={{0,24},{4,28},{8,0},{12,4},{16,8},{20,12},{24,16},{28,20},{1,25},{... | collective-permute-start | bytes 3538952 | tf_op jit(solution)/shard_map/ppermute | solution.py:937
  1042.1 71.3 %collective-permute-start.49 = (bf16[192,3072]{1,0:T(8,128)(2,1)S(1)}, bf16[192,3072]{1,0:T(8,128)(2,1)S(1)}, u32[]{:S(2)}, u32[]{:S(2)}) collective-permute-start(bf16[192,3072]{1,0:T(8,128)(2,1)S(1)} %copy-done.32), channel_id=1, source_target_pairs={{0,4},{4,0},{8,12},{12,8},{16,20},{20,16},{24,28},{28,24},{1,5},{5... | collective-permute-start | bytes 3538952 | tf_op jit(solution)/shard_map/ppermute | solution.py:937
  1043.0 70.3 %collective-permute-start.51 = (bf16[192,3072]{1,0:T(8,128)(2,1)S(1)}, bf16[192,3072]{1,0:T(8,128)(2,1)S(1)}, u32[]{:S(2)}, u32[]{:S(2)}) collective-permute-start(bf16[192,3072]{1,0:T(8,128)(2,1)S(1)} %add_convert_fusion.2), channel_id=1, source_target_pairs={{0,8},{4,12},{8,16},{12,20},{16,24},{20,28},{24,0},{28,4},{1,9},{5... | collective-permute-start | bytes 3538952 | tf_op jit(solution)/shard_map/ppermute | solution.py:937
  1043.1 128.7 %collective-permute-start.53 = (bf16[192,3072]{1,0:T(8,128)(2,1)S(1)}, bf16[192,3072]{1,0:T(8,128)(2,1)S(1)}, u32[]{:S(2)}, u32[]{:S(2)}) collective-permute-start(bf16[192,3072]{1,0:T(8,128)(2,1)S(1)} %add_convert_fusion.1), channel_id=1, source_target_pairs={{0,16},{4,20},{8,24},{12,28},{16,0},{20,4},{24,8},{28,12},{1,17},{... | collective-permute-start | bytes 3538952 | tf_op jit(solution)/shard_map/ppermute | solution.py:937
  (75 other events, 2408.1 us)

commit v2 on v1

v2 whole, which is shorter than its diff:
```python
import functools
import math
import types

import jax
import jax.numpy as jnp
import numpy as np
from jax import lax
from jax.experimental import pallas as pl
from jax.experimental.pallas import tpu as pltpu
from jax.sharding import PartitionSpec as P

HEAD_DIM = 96
HALF = HEAD_DIM // 2
BLOCK = 256
PAD = 128
GAIN_ROWS = 16
LIMIT = 60 * 1024 * 1024

epsilon = 1e-05
rope_base = 100000.0
masked_value = -1e30
scale = 1.0 / math.sqrt(HEAD_DIM)

BF = jnp.bfloat16
F32 = jnp.float32
MESH = pl.DeviceIdType.MESH
ANY = pl.BlockSpec(memory_space=pl.ANY)
VM = pl.BlockSpec(memory_space=pltpu.VMEM)


def nn(left, right):
    return lax.dot_general(left, right, (((1,), (0,)), ((), ())), preferred_element_type=F32)


def nt(left, right):
    return lax.dot_general(left, right, (((1,), (1,)), ((), ())), preferred_element_type=F32)


def tn(left, right):
    return lax.dot_general(left, right, (((0,), (0,)), ((), ())), preferred_element_type=F32)


def tile(index, size):
    return pl.ds(pl.multiple_of(index * size, size), size)


def each(count, body):
    def step(index, carry):
        body(index)
        return carry

    lax.fori_loop(0, count, step, 0)


class Group:
    def __init__(self):
        self.me = lax.axis_index("tensor")
        self.core_bit = lax.rem(self.me, 2)
        self.chip = self.me // 2
        self.core = self.me + 1 - 2 * self.core_bit
        self.other = lax.rem(self.me + 2, 4)

    def greet(self, barrier):
        for near in (self.core, self.other):
            pl.semaphore_signal(barrier, inc=1, device_id={"tensor": near}, device_id_type=MESH)

    def peers(self):
        return 2

    def remote(self, source, target, send, recv, device):
        return pltpu.make_async_remote_copy(
            src_ref=source,
            dst_ref=target,
            send_sem=send,
            recv_sem=recv,
            device_id={"tensor": device},
            device_id_type=MESH,
        )


class Gather:
    def __init__(self, group, full, send, recv):
        self.group, self.full, self.send, self.recv = group, full, send, recv
        half = full.shape[1] // 2
        mine = full.at[group.me]
        self.to_core = group.remote(mine, mine, send.at[0], recv.at[0], group.core)
        self.to_other = []
        self.onward = []
        for part in range(2):
            piece = full.at[group.me, pl.ds(part * half, half)]
            self.to_other.append(
                group.remote(piece, piece, send.at[1 + part], recv.at[1 + part], group.other)
            )
            piece = full.at[group.other, pl.ds(part * half, half)]
            self.onward.append(
                group.remote(piece, piece, send.at[3 + part], recv.at[3 + part], group.core)
            )

    def start(self):
        for copy in self.to_other:
            copy.start()
        self.to_core.start()

    def wait_chip(self):
        self.to_core.wait_recv()

    def forward(self):
        for here, there in zip(self.to_other, self.onward):
            here.wait_recv()
            there.start()

    def wait_other(self):
        for copy in self.onward:
            copy.wait_recv()

    def finish(self):
        self.to_core.wait_send()
        for copy in self.to_other + self.onward:
            copy.wait_send()


class Scatter:
    def __init__(self, group, parts, near, away, landed, send, recv):
        self.group, self.parts, self.near = group, parts, near
        self.away, self.landed = away, landed
        self.to_core = [
            group.remote(
                parts.at[turn, 1 - group.core_bit], near.at[turn], send.at[turn], recv.at[turn], group.core
            )
            for turn in range(2)
        ]
        half = away.shape[0] // 2
        self.to_other = [
            group.remote(
                away.at[pl.ds(part * half, half)],
                landed.at[pl.ds(part * half, half)],
                send.at[2 + part],
                recv.at[2 + part],
                group.other,
            )
            for part in range(2)
        ]

    def rows_of(self, turn):
        return 1 - self.group.chip if turn == 0 else self.group.chip

    def send_core(self, turn):
        self.to_core[turn].start()

    def send_away(self):
        self.to_core[0].wait_recv()
        half = self.away.shape[0] // 2
        for part in range(2):

            def add(index):
                rows = pl.ds(pl.multiple_of(part * half + index * 32, 32), 32)
                total = self.parts[0, self.group.core_bit, rows, :].astype(F32) + self.near[
                    0, rows, :
                ].astype(F32)
                self.away[rows, :] = total.astype(BF)

            each(half // 32, add)
            self.to_other[part].start()

    def wait(self):
        self.to_core[1].wait_recv()
        for copy in self.to_other:
            copy.wait_recv()

    def total(self, rows):
        return (
            self.parts[1, self.group.core_bit, rows, :].astype(F32)
            + self.near[1, rows, :].astype(F32)
            + self.landed[rows, :].astype(F32)
        )

    def finish(self):
        for copy in self.to_core + self.to_other:
            copy.wait_send()


class Line:
    def __init__(self, n_dp):
        mine = lax.axis_index("dp")
        self.count = n_dp // 2
        self.z, self.x = mine // 2, lax.rem(mine, 2)
        self.mine = mine
        self.pair = self.z * 2 + 1 - self.x
        self.up = jnp.minimum(self.z + 1, self.count - 1) * 2 + self.x
        self.down = jnp.maximum(self.z - 1, 0) * 2 + self.x
        self.has_up = self.z + 1 < self.count
        self.has_down = self.z > 0

    def greet(self, barrier):
        def hello(device):
            pl.semaphore_signal(barrier, inc=1, device_id={"dp": device}, device_id_type=MESH)

        hello(self.pair)
        pl.when(self.has_up)(lambda: hello(self.up))
        pl.when(self.has_down)(lambda: hello(self.down))

    def peers(self):
        return 1 + jnp.minimum(self.count - 1 - self.z, 1) + jnp.minimum(self.z, 1)

    def remote(self, source, target, send, recv, device):
        return pltpu.make_async_remote_copy(
            src_ref=source, dst_ref=target, send_sem=send, recv_sem=recv,
            device_id={"dp": device}, device_id_type=MESH)


class Fetch:
    def __init__(self, line, own, blocks, send, recv):
        self.line, self.own, self.blocks, self.send, self.recv = line, own, blocks, send, recv

    @staticmethod
    def scratch(n_dp):
        return [pltpu.SemaphoreType.DMA((n_dp, 3))] * 2

    def copy(self, slot, block, device, way):
        source = self.own if slot == 0 else self.blocks.at[block]
        return self.line.remote(
            source, self.blocks.at[block], self.send.at[slot, way], self.recv.at[slot, way], device)

    def upward(self, step):
        line = self.line
        return self.copy(step, jnp.maximum(line.z - step, 0) * 2 + line.x, line.up, 1)

    def downward(self, step):
        line = self.line
        return self.copy(step, jnp.minimum(line.z + step, line.count - 1) * 2 + line.x, line.down, 2)

    def sideways(self, step, low):
        line = self.line
        if low:
            return self.copy(step, jnp.maximum(line.z - step, 0) * 2 + line.x, line.pair, 0)
        return self.copy(line.count + step, jnp.minimum(line.z + step, line.count - 1) * 2 + line.x, line.pair, 0)

    def start(self):
        line = self.line
        pl.when(line.has_up)(lambda: self.upward(0).start())
        pl.when(line.has_down)(lambda: self.downward(0).start())
        self.sideways(0, True).start()

    def step(self, step):
        line = self.line

        @pl.when(line.z >= step)
        def _():
            self.upward_in(step).wait_recv()
            pl.when(line.has_up)(lambda: self.upward(step).start())
            self.sideways(step, True).start()

        @pl.when(line.z + step < line.count)
        def _():
            self.downward_in(step).wait_recv()
            pl.when(line.has_down)(lambda: self.downward(step).start())
            self.sideways(step, False).start()

    def upward_in(self, step):
        line = self.line
        return self.copy(step - 1, jnp.maximum(line.z - step, 0) * 2 + line.x, line.up, 1)

    def downward_in(self, step):
        line = self.line
        return self.copy(step - 1, jnp.minimum(line.z + step, line.count - 1) * 2 + line.x, line.down, 2)

    def finish(self):
        line = self.line
        for step in range(line.count):

            @pl.when(line.z >= step)
            def _():
                pl.when(line.has_up)(lambda: self.upward(step).wait_send())
                self.sideways(step, True).wait()

            @pl.when(line.z + step < line.count)
            def _():
                pl.when(line.has_down)(lambda: self.downward(step).wait_send())
                if step:
                    self.sideways(step, False).wait()

    def actions(self):
        return [self.start] + [functools.partial(self.step, s) for s in range(1, self.line.count)] + [self.finish]


class Reduce:
    def __init__(self, line, blocks, out, pair_in, line_in, mine, x_send, x_recv, z_send, z_recv, local):
        self.line, self.blocks, self.out = line, blocks, out
        self.pair_in, self.line_in, self.mine = pair_in, line_in, mine
        self.x_send, self.x_recv, self.z_send, self.z_recv, self.local = x_send, x_recv, z_send, z_recv, local

    @staticmethod
    def scratch(n_dp, rows, columns):
        count = n_dp // 2
        dma = pltpu.SemaphoreType.DMA
        return [
            pltpu.VMEM((count, rows, columns), BF),
            pltpu.VMEM((count + 1, rows, columns), BF),
            pltpu.VMEM((2, rows, columns), BF),
            dma((count,)), dma((count,)), dma((count,)), dma((count + 1,)), dma((2,)),
        ]

    def sideways(self, target):
        line = self.line
        return line.remote(self.blocks.at[target * 2 + 1 - line.x], self.pair_in.at[target],
                           self.x_send.at[target], self.x_recv.at[target], line.pair)

    def along(self, target, up):
        line = self.line
        slot = target + 1 if up else target
        return line.remote(self.pair_in.at[target], self.line_in.at[slot],
                           self.z_send.at[target], self.z_recv.at[slot], line.up if up else line.down)

    def load(self, target, slot):
        return pltpu.make_async_copy(self.blocks.at[target * 2 + self.line.x], self.mine.at[slot], self.local.at[slot])

    def above(self, step):
        return self.line.z + step < self.line.count, jnp.minimum(self.line.z + step, self.line.count - 1)

    def below(self, step):
        return self.line.z - step >= 0, jnp.maximum(self.line.z - step, 0)

    def fetch(self, step):
        there, target = self.above(step)
        pl.when(there)(lambda: self.load(target, 0).start())
        if step:
            there2, target2 = self.below(step)
            pl.when(there2)(lambda: self.load(target2, 1).start())

    def start(self):
        line = self.line
        for step in range(line.count - 1, 0, -1):
            for there, target in (self.above(step), self.below(step)):
                pl.when(there)(lambda: self.sideways(target).start())
        self.sideways(line.z).start()
        self.fetch(line.count - 1)

    def add(self, target, slot, more):
        rows = self.out.shape[0]

        def some(index):
            part = pl.ds(pl.multiple_of(index * 16, 16), 16)
            total = self.pair_in[target, part, :].astype(F32) + self.mine[slot, part, :].astype(F32)
            for other in more:
                total += self.line_in[other, part, :].astype(F32)
            self.pair_in[target, part, :] = total.astype(BF)

        each(rows // 16, some)

    def pass_on(self, target, slot, up):
        line = self.line
        self.load(target, slot).wait()
        self.sideways(target).wait_recv()
        fed = line.has_down if up else line.has_up

        @pl.when(fed)
        def _():
            self.along(target, up).wait_recv()
            self.add(target, slot, [target + 1 if up else target])

        pl.when(jnp.logical_not(fed))(lambda: self.add(target, slot, []))
        self.along(target, up).start()

    def step(self, step):
        for slot, (there, target) in enumerate((self.above(step), self.below(step))):
            pl.when(there)(lambda: self.pass_on(target, slot, slot == 0))
        self.fetch(step - 1)

    def close(self):
        line = self.line
        z = line.z
        self.load(z, 0).wait()
        self.sideways(z).wait_recv()
        rows = self.out.shape[0]

        def final(more):
            def some(index):
                part = pl.ds(pl.multiple_of(index * 16, 16), 16)
                total = self.pair_in[z, part, :].astype(F32) + self.mine[0, part, :].astype(F32)
                for other in more:
                    total += self.line_in[other, part, :].astype(F32)
                self.out[part, :] = total

            each(rows // 16, some)

        pl.when(line.has_down)(lambda: self.along(z, True).wait_recv())
        pl.when(line.has_up)(lambda: self.along(z, False).wait_recv())
        pl.when(jnp.logical_not(line.has_down))(lambda: final([z]))
        pl.when(jnp.logical_not(line.has_up))(lambda: final([z + 1]))
        pl.when(line.has_down & line.has_up)(lambda: final([z, z + 1]))
        for step in range(line.count - 1, 0, -1):
            for up, (there, target) in ((True, self.above(step)), (False, self.below(step))):

                @pl.when(there)
                def _():
                    self.sideways(target).wait_send()
                    self.along(target, up).wait_send()

        self.sideways(z).wait_send()

    def actions(self):
        return [self.start] + [functools.partial(self.step, s) for s in range(self.line.count - 1, 0, -1)] + [self.close]


def spread(block, depth, lanes, width):
    row = lax.broadcasted_iota(jnp.int32, (lanes, width), 0)
    column = lax.broadcasted_iota(jnp.int32, (lanes, width), 1)
    hit = (column - row == block * depth) & (row < depth)
    return jnp.where(hit, 1.0, 0.0).astype(BF)


def turn_half(values):
    return pltpu.roll(values, PAD // 2, 1)


def meet(*circles):
    barrier = pltpu.get_barrier_semaphore()
    for circle in circles:
        circle.greet(barrier)
    pl.semaphore_wait(barrier, sum(circle.peers() for circle in circles))


class Weights:
    def __init__(self, line, own, blocks, held, sems):
        self.copies = []
        depth = own.shape[0]
        count = line.count
        for index in range(2 * count):
            shift, side = index // 2, index % 2
            block = lax.rem(line.z + shift, count) * 2 + lax.rem(line.x + side, 2)
            source = blocks.at[block] if index else own
            rows = pl.ds(pl.multiple_of(block * depth, 16), depth)
            self.copies.append(pltpu.make_async_copy(source, held.at[rows], sems.at[index]))

    def start(self):
        for copy in self.copies:
            copy.start()

    def wait(self):
        for copy in self.copies:
            copy.wait()


class Pump:
    def __init__(self, tasks, plan):
        self.steps = [step for task in tasks for step in task.actions()]
        self.plan = list(plan)

    def __call__(self):
        count = self.plan.pop(0) if self.plan else 0
        self.do(count)

    def do(self, count):
        for step in self.steps[:count]:
            step()
        self.steps = self.steps[count:]

    def rest(self):
        self.do(len(self.steps))


def fetches_of(line, r, count):
    return [
        Fetch(
            line,
            getattr(r, f"own{i}"),
            getattr(r, f"blocks{i}"),
            getattr(r, f"fetch_send{i}"),
            getattr(r, f"fetch_recv{i}"),
        )
        for i in range(count)
    ]


def reduces_of(line, r, count):
    return [
        Reduce(
            line,
            getattr(r, f"sum{i}"),
            getattr(r, f"total{i}"),
            *[getattr(r, f"reduce{i}_{j}") for j in range(8)],
        )
        for i in range(count)
    ]


def comm_of(r):
    group = Group()
    gather = Gather(group, r.full, r.g_send, r.g_recv)
    scatter = Scatter(group, r.parts, r.near, r.away, r.landed, r.s_send, r.s_recv)
    return group, gather, scatter


def out_columns(scatter, turn, left_rows, right_tile, columns):
    product = nt(left_rows, right_tile)
    rows = product.shape[0] // 2
    scatter.parts[turn, 0, :, columns] = product[:rows].astype(BF)
    scatter.parts[turn, 1, :, columns] = product[rows:].astype(BF)


def norm_rows(source, gain, full, slot):
    def norm(index):
        part = tile(index, 32)
        values = source[part, :]
        factor = lax.rsqrt(jnp.mean(values * values, axis=-1, keepdims=True) + epsilon)
        full[slot, part, :] = (values * factor * gain).astype(BF)

    each(source.shape[0] // 32, norm)


def add_rows(scatter, source, target):
    def close(index):
        part = tile(index, 32)
        target[part, :] = source[part, :] + scatter.total(part)

    each(source.shape[0] // 32, close)


def attn_forward_kernel(first, level, fetch_count, plan, r):
    rows, width = r.x.shape
    n_dp, depth = r.w_sems.shape[0], r.own.shape[0]
    line = Line(n_dp)
    group, gather, scatter = comm_of(r)
    tasks = fetches_of(line, r, fetch_count)
    weights = Weights(line, r.own, r.blocks, r.held, r.w_sems)
    circles = (group, line) if first or tasks else (group,)
    meet(*circles)
    if first:
        lanes = r.gain_own.shape[1]
        gain_fetch = Fetch(line, r.gain_own, r.gain_blocks, r.gain_send, r.gain_recv)
        weight_fetch = Fetch(line, r.own, r.blocks, r.weight_send, r.weight_recv)
        gain_fetch.start()
        weight_fetch.start()
        for step in gain_fetch.actions()[1:]:
            step()
        r.gains[...] = jnp.zeros_like(r.gains)

        def gather_gain(block):
            chosen = spread(block, depth, lanes, width)

            @pl.when(block == line.mine)
            def _():
                r.gains[...] += nn(r.gain_own[...], chosen)

            @pl.when(block != line.mine)
            def _():
                r.gains[...] += nn(r.gain_blocks[block], chosen)

        each(n_dp, gather_gain)
        norm_rows(r.x, r.gains[2 * level : 2 * level + 1, :], r.full, group.me)
        gather.start()
        for step in weight_fetch.actions()[1:-1]:
            step()
        pump = Pump(tasks, plan)
        pump()
        weight_fetch.finish()
        weights.start()
    else:
        weights.start()
        pump = Pump(tasks, plan)
        pump()
        norm_rows(r.x, r.gains[2 * level : 2 * level + 1, :], r.full, group.me)
        gather.start()
    weights.wait()
    place = r.place[...]
    heads = place.shape[1] // PAD
    compact_width, head_width = place.shape
    padded, qkv, mixed, compact, held = r.padded, r.qkv, r.mixed, r.compact, r.held

    def pad(index):
        part = tile(index, 256)
        padded[part, 0:head_width] = nn(held[part, 0:compact_width], place).astype(BF)
        padded[part, head_width : 2 * head_width] = nn(
            held[part, compact_width : 2 * compact_width], place
        ).astype(BF)

    each(width // 256, pad)

    def project(chip):
        left = r.full[pl.ds(2 * chip, 2)].reshape(2 * rows, width)
        where = tile(chip, 2 * rows)
        cosine, sine = r.cosine[where, :], r.sine[where, :]

        def turned(index):
            columns = tile(index, 2 * PAD)
            product = nn(left, padded[:, columns])
            for half in range(2):
                u = product[:, half * PAD : (half + 1) * PAD]
                qkv[where, tile(2 * index + half, PAD)] = (u * cosine + turn_half(u) * sine).astype(BF)

        each(3 * heads // 4, turned)
        columns = pl.ds(3 * heads // 2 * PAD, heads // 2 * PAD)
        qkv[where, columns] = nn(left, padded[:, columns]).astype(BF)

    gather.wait_chip()
    project(group.chip)
    pump()
    gather.forward()
    pump()
    gather.wait_other()
    project(1 - group.chip)
    copies = [
        pltpu.make_async_copy(r.full, r.a_out, r.out_sems.at[0]),
        pltpu.make_async_copy(qkv, r.qkv_out, r.out_sems.at[1]),
    ]
    for copy in copies:
        copy.start()
    pump()
    kv_at = heads * PAD
    value_at = kv_at + heads // 2 * PAD
    for turn in range(4):
        prob = getattr(r, f"prob{turn}")
        reach = prob.shape[2]
        where = pl.ds(turn * rows, rows)

        def attend(head):
            query = qkv[where, tile(head, PAD)]
            key = qkv[0:reach, pl.ds(pl.multiple_of(kv_at + head // 2 * PAD, PAD), PAD)]
            value = qkv[0:reach, pl.ds(pl.multiple_of(value_at + head // 2 * PAD, PAD), PAD)]
            scores = nt(query, key) * scale
            place_of = lax.broadcasted_iota(jnp.int32, scores.shape, 1)
            begin = r.spans[where, 0:1]
            end = r.spans[where, 1:2]
            scores = jnp.where((place_of >= begin) & (place_of < end), scores, masked_value)
            exponent = jnp.exp(scores - jnp.max(scores, axis=-1, keepdims=True))
            summed = jnp.sum(exponent, axis=-1, keepdims=True)
            low = (exponent * (1.0 / summed)).astype(BF)
            prob[head] = low
            mixed[where, tile(head, PAD)] = nn(low, value).astype(BF)

        each(heads, attend)
        copy = pltpu.make_async_copy(prob, getattr(r, f"p_out{turn}"), r.out_sems.at[2 + turn])
        copy.start()
        copies.append(copy)
        compact[where, :] = nt(mixed[where, :], place).astype(BF)
        pump()
    copy = pltpu.make_async_copy(compact, r.o_out, r.out_sems.at[6])
    copy.start()
    copies.append(copy)
    for turn in range(2):
        left = compact[tile(scatter.rows_of(turn), 2 * rows), :]

        def part_of(index):
            columns = tile(index, 256)
            out_columns(scatter, turn, left, held[columns, 2 * compact_width :], columns)

        each(width // 256, part_of)
        scatter.send_core(turn)
        if turn == 0:
            scatter.send_away()
        pump()
    scatter.wait()
    pump()
    add_rows(scatter, r.x, r.middle)
    pump.rest()
    gather.finish()
    scatter.finish()
    for copy in copies:
        copy.wait()


def mlp_forward_kernel(level, fetch_count, plan, r):
    rows, width = r.middle.shape
    units = r.hid.shape[1]
    line = Line(r.wide_sems.shape[0])
    group, gather, scatter = comm_of(r)
    tasks = fetches_of(line, r, fetch_count)
    wide, held, gu, hid = r.wide, r.held, r.gu, r.hid
    weights = [
        Weights(line, r.wide_own, r.wide_blocks, wide, r.wide_sems),
        Weights(line, r.own, r.blocks, held, r.w_sems),
    ]
    meet(*((group, line) if tasks else (group,)))
    for each_of in weights:
        each_of.start()
    pump = Pump(tasks, plan)
    pump()
    norm_rows(r.middle, r.gains[2 * level + 1 : 2 * level + 2, :], r.full, group.me)
    gather.start()
    weights[0].wait()

    def expand(chip):
        left = r.full[pl.ds(2 * chip, 2)].reshape(2 * rows, width)
        where = tile(chip, 2 * rows)

        def unit(index):
            columns = tile(index, 256)
            further = pl.ds(pl.multiple_of(units + index * 256, 256), 256)
            gate = nn(left, wide[:, columns])
            up = nn(left, wide[:, further])
            hid[where, columns] = (gate / (1.0 + jnp.exp(-gate)) * up).astype(BF)
            gu[where, columns] = gate.astype(BF)
            gu[where, further] = up.astype(BF)

        each(units // 256, unit)

    gather.wait_chip()
    expand(group.chip)
    pump()
    gather.forward()
    pump()
    gather.wait_other()
    expand(1 - group.chip)
    copies = [
        pltpu.make_async_copy(r.full, r.m_out, r.out_sems.at[0]),
        pltpu.make_async_copy(gu, r.gu_out, r.out_sems.at[1]),
        pltpu.make_async_copy(hid, r.hid_out, r.out_sems.at[2]),
    ]
    for copy in copies:
        copy.start()
    pump()
    weights[1].wait()
    for turn in range(2):
        left = hid[tile(scatter.rows_of(turn), 2 * rows), :]

        def part_of(index):
            columns = tile(index, 256)
            out_columns(scatter, turn, left, held[columns, :], columns)

        each(width // 256, part_of)
        scatter.send_core(turn)
        if turn == 0:
            scatter.send_away()
        pump()
    scatter.wait()
    pump()
    add_rows(scatter, r.middle, r.result)
    pump.rest()
    gather.finish()
    scatter.finish()
    for copy in copies:
        copy.wait()


def flip(source, target, slot):
    _, rows, width = source.shape

    def block(index):
        columns = tile(index, 256)
        target[columns, slot * rows : (slot + 1) * rows] = source[slot, :, columns].T

    each(width // 256, block)


def flip_pairs(source, target, slot):
    rows, width = source.shape[2:]

    def block(index):
        columns = tile(index, 256)
        target[columns, slot * rows : (slot + 1) * rows] = source[slot // 2, slot % 2, :, columns].T

    each(width // 256, block)


def close_back(scatter, grad_in_ref, state_ref, gain, grad_out, dgain):
    rows = state_ref.shape[0]
    dgain[...] = jnp.zeros_like(dgain)

    def close(index):
        part = tile(index, 32)
        values = state_ref[part, :]
        factor = lax.rsqrt(jnp.mean(values * values, axis=-1, keepdims=True) + epsilon)
        normed = values * factor
        grad_in = scatter.total(part)
        dgain[...] += jnp.sum((grad_in * normed).reshape(4, 8, -1), axis=0)
        grad_norm = grad_in * gain
        inner = jnp.mean(grad_norm * normed, axis=-1, keepdims=True)
        grad_out[part, :] = grad_in_ref[part, :] + factor * (grad_norm - normed * inner)

    each(rows // 32, close)


def mlp_backward_kernel(level, reduce_count, plan, r):
    rows, width = r.middle.shape
    units = r.hid.shape[1]
    n_dp = r.wide_sems.shape[0]
    depth = width // n_dp
    line = Line(n_dp)
    group, gather, scatter = comm_of(r)
    tasks = reduces_of(line, r, reduce_count)
    wide, held, gu, hid, flipped = r.wide, r.held, r.gu, r.hid, r.flipped
    weights = [
        Weights(line, r.own, r.blocks, held, r.w_sems),
        Weights(line, r.wide_own, r.wide_blocks, wide, r.wide_sems),
    ]
    fetches = [
        pltpu.make_async_copy(r.m_in, r.parts, r.in_sems.at[0]),
        pltpu.make_async_copy(r.gu_in, gu, r.in_sems.at[1]),
        pltpu.make_async_copy(r.hid_in, hid, r.in_sems.at[2]),
    ]
    meet(*((group, line) if tasks else (group,)))
    for copy in fetches + weights:
        copy.start()
    pump = Pump(tasks, plan)
    pump()
    r.full[group.me] = r.grad[...].astype(BF)
    gather.start()
    fetches[0].wait()
    for slot in range(4):
        flip_pairs(r.parts, flipped, slot)
    pump()
    for copy in weights + fetches[1:]:
        copy.wait()

    def inward(chip):
        left = r.full[pl.ds(2 * chip, 2)].reshape(2 * rows, width)
        where = tile(chip, 2 * rows)

        def unit(index):
            columns = tile(index, 256)
            further = pl.ds(pl.multiple_of(units + index * 256, 256), 256)
            grad = nn(left, held[:, columns])
            gate = gu[where, columns].astype(F32)
            up = gu[where, further].astype(F32)
            sig = 1.0 / (1.0 + jnp.exp(-gate))
            gu[where, columns] = (grad * up * sig * (1.0 + gate * (1.0 - sig))).astype(BF)
            gu[where, further] = (grad * gate * sig).astype(BF)

        each(units // 256, unit)

    gather.wait_chip()
    inward(group.chip)
    pump()
    gather.forward()
    pump()
    gather.wait_other()
    inward(1 - group.chip)
    pump()
    for turn in range(2):
        where = tile(scatter.rows_of(turn), 2 * rows)

        def part_of(index):
            columns = tile(index, 256)
            out_columns(scatter, turn, gu[where, :], wide[columns, :], columns)

        each(width // 256, part_of)
        scatter.send_core(turn)
        if turn == 0:
            scatter.send_away()
        pump()

    def grads_of(block, target, slot, right):
        left = flipped[pl.ds(pl.multiple_of(block * depth, 16), depth), :]

        def some(index):
            columns = tile(index, 512)
            target[slot, :, columns] = nn(left, right[:, columns]).astype(BF)

        each(right.shape[1] // 512, some)

    half = n_dp // 2
    copies = []
    for part in range(2):
        for copy in copies:
            copy.wait()
        each(half, lambda slot: grads_of(part * half + slot, r.wide_grads, slot, gu))
        copies = [
            pltpu.make_async_copy(r.wide_grads, r.wide_out.at[pl.ds(part * half, half)], r.out_sems.at[part])
        ]
        copies[0].start()
        pump()
    for slot in range(4):
        flip(r.full, flipped, slot)
    each(n_dp, lambda block: grads_of(block, r.grads, block, hid))
    copies.append(pltpu.make_async_copy(r.grads, r.grads_out, r.out_sems.at[2]))
    copies[-1].start()
    pump()
    scatter.wait()
    pump()
    close_back(
        scatter, r.grad, r.middle, r.gains[2 * level + 1 : 2 * level + 2, :], r.grad_out, r.dgain
    )
    pump.rest()
    gather.finish()
    scatter.finish()
    for copy in copies:
        copy.wait()


def attn_backward_kernel(level, reduce_count, plan, r):
    rows, width = r.x.shape
    n_dp = r.w_sems.shape[0]
    depth = width // n_dp
    line = Line(n_dp)
    group, gather, scatter = comm_of(r)
    tasks = reduces_of(line, r, reduce_count)
    held, qkv, compact, flipped = r.held, r.qkv, r.compact, r.flipped
    probs = [getattr(r, f"prob{turn}") for turn in range(4)]
    weights = Weights(line, r.own, r.blocks, held, r.w_sems)
    fetches = [
        pltpu.make_async_copy(r.a_in, r.parts, r.in_sems.at[0]),
        pltpu.make_async_copy(r.o_in, compact, r.in_sems.at[1]),
        pltpu.make_async_copy(r.qkv_in, qkv, r.in_sems.at[2]),
    ] + [
        pltpu.make_async_copy(getattr(r, f"p_in{turn}"), probs[turn], r.in_sems.at[3 + turn])
        for turn in range(4)
    ]
    meet(*((group, line) if tasks else (group,)))
    fetches[0].start()
    weights.start()
    for copy in fetches[1:]:
        copy.start()
    pump = Pump(tasks, plan)
    pump()
    r.full[group.me] = r.grad[...].astype(BF)
    gather.start()
    fetches[0].wait()
    for slot in range(4):
        flip_pairs(r.parts, flipped, slot)
    pump()
    weights.wait()
    for copy in fetches[1:]:
        copy.wait()
    place = r.place[...]
    heads = place.shape[1] // PAD
    compact_width, head_width = place.shape

    def inward(chip):
        left = r.full[pl.ds(2 * chip, 2)].reshape(2 * rows, width)
        where = tile(chip, 2 * rows)
        grad = nn(left, held[:, 2 * compact_width :]).astype(BF)
        r.grad_mixed[where, :] = nn(grad, place).astype(BF)

    gather.wait_chip()
    inward(group.chip)
    pump()
    gather.forward()
    pump()
    gather.wait_other()
    inward(1 - group.chip)
    kv_at = heads * PAD
    value_at = kv_at + heads // 2 * PAD
    r.grad_k[...] = jnp.zeros_like(r.grad_k)
    r.grad_v[...] = jnp.zeros_like(r.grad_v)
    for turn, prob in enumerate(probs):
        reach = prob.shape[2]
        where = pl.ds(turn * rows, rows)
        cosine, sine = r.cosine[where, :], r.sine[where, :]

        def attend(head):
            mine = tile(head, PAD)
            shared = tile(head // 2, PAD)
            query = qkv[where, mine]
            key = qkv[0:reach, pl.ds(pl.multiple_of(kv_at + head // 2 * PAD, PAD), PAD)]
            value = qkv[0:reach, pl.ds(pl.multiple_of(value_at + head // 2 * PAD, PAD), PAD)]
            grad = r.grad_mixed[where, mine]
            low = prob[head]
            grad_prob = nt(grad, value)
            weight = low.astype(F32)
            inner = jnp.sum(weight * grad_prob, axis=-1, keepdims=True)
            grad_score = (weight * (grad_prob - inner)).astype(BF)
            u = nn(grad_score, key) * scale
            r.grad_q[where, mine] = (u * cosine - turn_half(u) * sine).astype(BF)
            r.grad_k[0:reach, shared] += tn(grad_score, query)
            r.grad_v[0:reach, shared] += tn(low, grad)

        each(heads, attend)
        pump()
    for pair in range(heads // 2):
        columns = pl.ds(pair * PAD, PAD)
        u = r.grad_k[:, columns] * scale
        r.grad_kv[:, columns] = (u * r.cosine[...] - turn_half(u) * r.sine[...]).astype(BF)
        r.grad_kv[:, pl.ds((heads // 2 + pair) * PAD, PAD)] = r.grad_v[:, columns].astype(BF)
    grad_low = r.grad_low
    grad_low[:, 0:compact_width] = nt(r.grad_q[...], place).astype(BF)
    grad_low[:, compact_width : 2 * compact_width] = nt(r.grad_kv[...], place).astype(BF)
    for turn in range(2):
        where = tile(scatter.rows_of(turn), 2 * rows)

        def part_of(index):
            columns = tile(index, 256)
            out_columns(
                scatter, turn, grad_low[where, :], held[columns, 0 : 2 * compact_width], columns
            )

        each(width // 256, part_of)
        scatter.send_core(turn)
        if turn == 0:
            scatter.send_away()
        pump()
    grads = r.grads

    def grads_of(block, begin, right):
        left = flipped[pl.ds(pl.multiple_of(block * depth, 16), depth), :]
        grads[block, :, begin : begin + right.shape[1]] = nn(left, right[...]).astype(BF)

    each(n_dp, lambda block: grads_of(block, 0, grad_low))
    for slot in range(4):
        flip(r.full, flipped, slot)
    each(n_dp, lambda block: grads_of(block, 2 * compact_width, compact))
    copy = pltpu.make_async_copy(grads, r.grads_out, r.out_sems.at[0])
    copy.start()
    pump()
    scatter.wait()
    pump()
    close_back(scatter, r.grad, r.x, r.gains[2 * level : 2 * level + 1, :], r.grad_out, r.dgain)
    pump.rest()
    gather.finish()
    scatter.finish()
    copy.wait()


def last_kernel(reduce_count, r):
    n_dp, _, lanes = r.gain_blocks.shape
    width = r.rows.shape[1]
    depth = width // n_dp
    line = Line(n_dp)
    group = Group()
    tasks = reduces_of(line, r, reduce_count)
    gains = Reduce(line, r.gain_blocks, r.gain_total, *[getattr(r, f"gain{j}") for j in range(8)])
    meet(group, line)
    for task in tasks:
        task.start()
    for row in range(4):
        r.rows[row : row + 1, :] = jnp.sum(getattr(r, f"dgain{row}")[...], axis=0, keepdims=True)
    r.rows[4:8, :] = jnp.zeros((4, width), F32)
    for turn, device in enumerate((group.core, group.other)):
        copy = group.remote(r.rows, r.others.at[turn], r.row_send.at[turn], r.row_recv.at[turn], device)
        copy.start()
        copy.wait()
        r.rows[...] += r.others[turn]
    both = jnp.concatenate([r.rows[...], jnp.zeros((GAIN_ROWS - 8, width), F32)], axis=0).astype(BF)

    def gain_rows(block):
        r.gain_blocks[block] = nt(both, spread(block, depth, lanes, width)).astype(BF)

    each(n_dp, gain_rows)
    gains.start()
    for task in tasks:
        for step in task.actions()[1:]:
            step()
    for step in gains.actions()[1:]:
        step()


def shaped(shape, dtype):
    return jax.ShapeDtypeStruct(shape, dtype)


def dma(count):
    return pltpu.SemaphoreType.DMA((count,))


def vmem(*shape, dtype=BF):
    return pltpu.VMEM(shape, dtype)


def reaches(rows):
    return [min((turn + 1) * rows + PAD, 4 * rows) for turn in range(4)]


def launch(kernel, which, name, ins, outs, scratch):
    names = list(ins) + list(outs) + list(scratch)

    def entry(*refs):
        kernel(types.SimpleNamespace(**dict(zip(names, refs))))

    results = pl.pallas_call(
        entry,
        out_shape=[shape for shape, _ in outs.values()],
        in_specs=[spec for _, spec in ins.values()],
        out_specs=[spec for _, spec in outs.values()],
        scratch_shapes=list(scratch.values()),
        compiler_params=pltpu.CompilerParams(
            collective_id=which, has_side_effects=True, vmem_limit_bytes=LIMIT
        ),
        cost_estimate=pl.CostEstimate(
            flops=20_000_000_000, bytes_accessed=60_000_000, transcendentals=0
        ),
        name=name,
    )(*[array for array, _ in ins.values()])
    return dict(zip(outs, results))


def comm_scratch(rows, width):
    return dict(
        full=vmem(4, rows, width),
        parts=vmem(2, 2, rows, width),
        near=vmem(2, rows, width),
        away=vmem(rows, width),
        landed=vmem(rows, width),
        g_send=dma(5),
        g_recv=dma(5),
        s_send=dma(4),
        s_recv=dma(4),
    )


def blocks_of(pack, n_dp):
    return shaped((n_dp,) + pack.shape, pack.dtype)


def fetch_refs(packs, n_dp):
    ins, outs, scratch = {}, {}, {}
    for i, pack in enumerate(packs):
        ins[f"own{i}"] = (pack, ANY)
        outs[f"blocks{i}"] = (blocks_of(pack, n_dp), ANY)
        scratch[f"fetch_send{i}"], scratch[f"fetch_recv{i}"] = Fetch.scratch(n_dp)
    return ins, outs, scratch


def reduce_refs(sums):
    ins, outs, scratch = {}, {}, {}
    for i, blocks in enumerate(sums):
        n_dp, depth, columns = blocks.shape
        ins[f"sum{i}"] = (blocks, ANY)
        outs[f"total{i}"] = (shaped((depth, columns), F32), VM)
        for j, each_of in enumerate(Reduce.scratch(n_dp, depth, columns)):
            scratch[f"reduce{i}_{j}"] = each_of
    return ins, outs, scratch


def totals(out, count):
    return [out[f"total{i}"] for i in range(count)]


def fetched(out, count):
    return [out[f"blocks{i}"] for i in range(count)]


def attn_forward(level, which, states, tables, gains, pack, blocks, packs, plan, gain_pack=None):
    cosine, sine, spans, place = tables
    rows, width = states.shape
    first = blocks is None
    n_dp = width // pack.shape[0]
    columns = pack.shape[1]
    heads = place.shape[1] // PAD
    length = 4 * rows
    ins = dict(
        x=(states, VM), cosine=(cosine, VM), sine=(sine, VM), spans=(spans, VM), place=(place, VM), own=(pack, ANY)
    )
    outs = dict(
        middle=(shaped((rows, width), F32), VM),
        a_out=(shaped((4, rows, width), BF), ANY),
        qkv_out=(shaped((length, 2 * heads * PAD), BF), ANY),
        o_out=(shaped((length, place.shape[0]), BF), ANY),
    )
    scratch = comm_scratch(rows, width) | dict(
        held=vmem(width, columns),
        padded=vmem(width, 2 * heads * PAD),
        qkv=vmem(length, 2 * heads * PAD),
        mixed=vmem(length, heads * PAD),
        compact=vmem(length, place.shape[0]),
        w_sems=dma(n_dp),
        out_sems=dma(7),
    )
    for turn, reach in enumerate(reaches(rows)):
        outs[f"p_out{turn}"] = (shaped((heads, rows, reach), BF), ANY)
        scratch[f"prob{turn}"] = vmem(heads, rows, reach)
    if first:
        ins["gain_own"] = (gain_pack, VM)
        outs["gains"] = (shaped((gain_pack.shape[0], width), F32), VM)
        outs["blocks"] = (blocks_of(pack, n_dp), ANY)
        scratch["gain_blocks"] = vmem(n_dp, *gain_pack.shape)
        scratch["gain_send"], scratch["gain_recv"] = Fetch.scratch(n_dp)
        scratch["weight_send"], scratch["weight_recv"] = Fetch.scratch(n_dp)
    else:
        ins["gains"] = (gains, VM)
        ins["blocks"] = (blocks, ANY)
    more = fetch_refs(packs, n_dp)
    return launch(
        functools.partial(attn_forward_kernel, first, level, len(packs), plan),
        which, f"attn_forward_{level}", ins | more[0], outs | more[1], scratch | more[2],
    )


def mlp_refs(rows, width, wide, down):
    n_dp = width // wide[0].shape[0]
    units = down[0].shape[1]
    ins = dict(wide_own=(wide[0], ANY), wide_blocks=(wide[1], ANY), own=(down[0], ANY), blocks=(down[1], ANY))
    scratch = comm_scratch(rows, width) | dict(
        wide=vmem(width, 2 * units),
        held=vmem(width, units),
        gu=vmem(4 * rows, 2 * units),
        hid=vmem(4 * rows, units),
        wide_sems=dma(n_dp),
        w_sems=dma(n_dp),
    )
    return n_dp, units, ins, scratch


def mlp_forward(level, which, middle, gains, wide, down, packs, plan):
    rows, width = middle.shape
    n_dp, units, ins, scratch = mlp_refs(rows, width, wide, down)
    ins |= dict(middle=(middle, VM), gains=(gains, VM))
    outs = dict(
        result=(shaped((rows, width), F32), VM),
        m_out=(shaped((4, rows, width), BF), ANY),
        gu_out=(shaped((4 * rows, 2 * units), BF), ANY),
        hid_out=(shaped((4 * rows, units), BF), ANY),
    )
    scratch |= dict(out_sems=dma(3))
    more = fetch_refs(packs, n_dp)
    return launch(
        functools.partial(mlp_forward_kernel, level, len(packs), plan),
        which, f"mlp_forward_{level}", ins | more[0], outs | more[1], scratch | more[2],
    )


def mlp_backward(level, which, grad, middle, gains, saved, wide, down, sums, plan):
    rows, width = middle.shape
    n_dp, units, ins, scratch = mlp_refs(rows, width, wide, down)
    depth = width // n_dp
    ins |= dict(
        grad=(grad, VM), middle=(middle, VM), gains=(gains, VM),
        m_in=(saved["m_out"].reshape(2, 2, rows, width), ANY), gu_in=(saved["gu_out"], ANY), hid_in=(saved["hid_out"], ANY),
    )
    outs = dict(
        grad_out=(shaped((rows, width), F32), VM),
        dgain=(shaped((8, width), F32), VM),
        wide_out=(shaped((n_dp, depth, 2 * units), BF), ANY),
        grads_out=(shaped((n_dp, depth, units), BF), ANY),
    )
    scratch |= dict(
        flipped=vmem(width, 4 * rows),
        wide_grads=vmem(n_dp // 2, depth, 2 * units),
        grads=vmem(n_dp, depth, units),
        in_sems=dma(3),
        out_sems=dma(3),
    )
    more = reduce_refs(sums)
    return launch(
        functools.partial(mlp_backward_kernel, level, len(sums), plan),
        which, f"mlp_backward_{level}", ins | more[0], outs | more[1], scratch | more[2],
    )


def attn_backward(level, which, grad, states, gains, tables, saved, weights, sums, plan):
    cosine, sine, _, place = tables
    pack, blocks = weights
    rows, width = states.shape
    depth, columns = pack.shape
    n_dp = width // depth
    heads = place.shape[1] // PAD
    length = 4 * rows
    ins = dict(
        grad=(grad, VM), x=(states, VM), gains=(gains, VM), cosine=(cosine, VM), sine=(sine, VM), place=(place, VM),
        own=(pack, ANY), blocks=(blocks, ANY),
        a_in=(saved["a_out"].reshape(2, 2, rows, width), ANY), qkv_in=(saved["qkv_out"], ANY), o_in=(saved["o_out"], ANY),
    )
    outs = dict(
        grad_out=(shaped((rows, width), F32), VM),
        dgain=(shaped((8, width), F32), VM),
        grads_out=(shaped((n_dp, depth, columns), BF), ANY),
    )
    scratch = comm_scratch(rows, width) | dict(
        held=vmem(width, columns),
        flipped=vmem(width, length),
        qkv=vmem(length, 2 * heads * PAD),
        compact=vmem(length, place.shape[0]),
        grad_mixed=vmem(length, heads * PAD),
        grad_q=vmem(length, heads * PAD),
        grad_kv=vmem(length, heads * PAD),
        grad_k=vmem(length, heads // 2 * PAD, dtype=F32),
        grad_v=vmem(length, heads // 2 * PAD, dtype=F32),
        grad_low=vmem(length, 2 * place.shape[0]),
        grads=vmem(n_dp, depth, columns),
        w_sems=dma(n_dp),
        in_sems=dma(7),
        out_sems=dma(1),
    )
    for turn, reach in enumerate(reaches(rows)):
        ins[f"p_in{turn}"] = (saved[f"p_out{turn}"], ANY)
        scratch[f"prob{turn}"] = vmem(heads, rows, reach)
    more = reduce_refs(sums)
    return launch(
        functools.partial(attn_backward_kernel, level, len(sums), plan),
        which, f"attn_backward_{level}", ins | more[0], outs | more[1], scratch | more[2],
    )


def last_sums(which, dgains, sums):
    n_dp = sums[0].shape[0]
    width = dgains[0].shape[1]
    ins = {f"dgain{i}": (dgain, VM) for i, dgain in enumerate(dgains)}
    outs = dict(gain_total=(shaped((GAIN_ROWS, 256), F32), VM))
    scratch = dict(
        gain_blocks=vmem(n_dp, GAIN_ROWS, 256),
        rows=vmem(8, width, dtype=F32),
        others=vmem(2, 8, width, dtype=F32),
        row_send=dma(2),
        row_recv=dma(2),
    )
    for j, each_of in enumerate(Reduce.scratch(n_dp, GAIN_ROWS, 256)):
        scratch[f"gain{j}"] = each_of
    more = reduce_refs(sums)
    return launch(
        functools.partial(last_kernel, len(sums)),
        which, "last_sums", ins | more[0], outs | more[1], scratch | more[2],
    )


def tables_of(documents, heads):
    length = documents.shape[0]
    places = jnp.arange(length, dtype=jnp.int32)
    head = jnp.sum((documents == 0).astype(jnp.int32))
    body_end = jnp.sum((documents <= 1).astype(jnp.int32))
    starts = jnp.where(documents == 0, 0, jnp.where(documents == 1, head, body_end))
    ends = jnp.where(documents == 0, head, jnp.where(documents == 1, body_end, length))
    offset = places - starts
    last = jnp.minimum(starts + (offset // BLOCK + 1) * BLOCK, ends)
    spans = jnp.stack([starts, last], axis=1)
    freqs = jnp.exp(
        jnp.arange(HALF, dtype=F32) * (-2.0 * math.log(rope_base) / HEAD_DIM)
    )
    angles = offset.astype(F32)[:, None] * freqs[None, :]
    gap = ((0, 0), (0, PAD // 2 - HALF))
    cos_half = jnp.pad(jnp.cos(angles), gap)
    sin_half = jnp.pad(jnp.sin(angles), gap)
    cosine = jnp.concatenate([cos_half, cos_half], axis=1)
    sine = jnp.concatenate([-sin_half, sin_half], axis=1)
    place = np.zeros((heads * HEAD_DIM, heads * PAD), np.float32)
    for row in range(heads * HEAD_DIM):
        which, column = divmod(row, HEAD_DIM)
        place[row, which * PAD + column + (PAD // 2 - HALF if column >= HALF else 0)] = 1.0
    return cosine, sine, spans, jnp.asarray(place, BF)


def pack_gains(gains):
    stacked = jnp.stack(gains).astype(BF)
    return jnp.pad(stacked, ((0, GAIN_ROWS - stacked.shape[0]), (0, 256 - stacked.shape[1])))


def body(states_in, documents, *rest):
    cotangent = rest[-1]
    one, two = rest[0:9], rest[9:18]
    heads = one[1].shape[1] // HEAD_DIM
    tables = tables_of(documents, heads)
    attn_pack = [jnp.concatenate([w[1], w[2], w[3], w[4].T], axis=1).astype(BF) for w in (one, two)]
    wide_pack = [jnp.concatenate([w[6], w[7]], axis=1).astype(BF) for w in (one, two)]
    down_pack = [w[8].T.astype(BF) for w in (one, two)]
    gain_pack = pack_gains([one[0], one[5], two[0], two[5]])

    attn1 = attn_forward(
        0, 0, states_in, tables, None, attn_pack[0], None, [wide_pack[0], down_pack[0]],
        [1, 0, 1, 0, 1, 0, 1, 1, 1, 1], gain_pack,
    )
    gains = attn1["gains"]
    wide1, down1 = fetched(attn1, 2)
    mlp1 = mlp_forward(
        0, 1, attn1["middle"], gains, (wide_pack[0], wide1), (down_pack[0], down1),
        [attn_pack[1], down_pack[1]], [1, 1, 1, 1, 2, 1, 1],
    )
    attn2_blocks, down2 = fetched(mlp1, 2)
    attn2 = attn_forward(
        1, 2, mlp1["result"], tables, gains, attn_pack[1], attn2_blocks, [wide_pack[1]],
        [1, 0, 1, 0, 0, 1, 0, 0, 1, 0, 0],
    )
    (wide2,) = fetched(attn2, 1)
    mlp2 = mlp_forward(1, 3, attn2["middle"], gains, (wide_pack[1], wide2), (down_pack[1], down2), [], [])

    back_mlp2 = mlp_backward(
        1, 4, cotangent, attn2["middle"], gains, mlp2, (wide_pack[1], wide2), (down_pack[1], down2), [], []
    )
    back_attn2 = attn_backward(
        1, 5, back_mlp2["grad_out"], mlp1["result"], gains, tables, attn2, (attn_pack[1], attn2_blocks),
        [back_mlp2["wide_out"]], [1, 0, 0, 1, 0, 1, 0, 0, 0, 1],
    )
    back_mlp1 = mlp_backward(
        0, 6, back_attn2["grad_out"], attn1["middle"], gains, mlp1, (wide_pack[0], wide1), (down_pack[0], down1),
        [back_mlp2["grads_out"], back_attn2["grads_out"]], [1, 1, 1, 1, 1, 1, 1, 0, 1, 0, 1],
    )
    back_attn1 = attn_backward(
        0, 7, back_mlp1["grad_out"], states_in, gains, tables, attn1, (attn_pack[0], attn1["blocks"]),
        [back_mlp1["wide_out"]], [1, 0, 0, 1, 0, 1, 0, 0, 0, 1],
    )
    last = last_sums(
        8,
        [back_attn1["dgain"], back_mlp1["dgain"], back_attn2["dgain"], back_mlp2["dgain"]],
        [back_mlp1["grads_out"], back_attn1["grads_out"]],
    )
    (wide_total2,) = totals(back_attn2, 1)
    down_total2, attn_total2 = totals(back_mlp1, 2)
    (wide_total1,) = totals(back_attn1, 1)
    down_total1, attn_total1 = totals(last, 2)
    gain_total = last["gain_total"]
    depth = down_total1.shape[0]
    bounds = [0]
    for w in one[1:4]:
        bounds.append(bounds[-1] + w.shape[1])
    units = one[6].shape[1]
    outs = [mlp2["result"], back_attn1["grad_out"]]
    for level, (attn_total, wide_total, down_total) in enumerate(
        ((attn_total1, wide_total1, down_total1), (attn_total2, wide_total2, down_total2))
    ):
        outs.append(gain_total[2 * level, 0:depth])
        outs += [attn_total[:, low:high] for low, high in zip(bounds, bounds[1:])]
        outs.append(attn_total[:, bounds[-1] :].T)
        outs.append(gain_total[2 * level + 1, 0:depth])
        outs += [wide_total[:, 0:units], wide_total[:, units:], down_total.T]
    return tuple(outs)


def solution(mesh):
    layer = (
        P("dp"),
        P("dp", "tensor"),
        P("dp", "tensor"),
        P("dp", "tensor"),
        P("tensor", "dp"),
        P("dp"),
        P("dp", "tensor"),
        P("dp", "tensor"),
        P("tensor", "dp"),
    )
    rows = P(("dp", "tensor"), None)
    return jax.shard_map(
        body,
        mesh=mesh,
        in_specs=(rows, P("dp"), *layer, *layer, rows),
        out_specs=(rows, rows, *layer, *layer),
        check_vma=False,
    )
```

time: 1190 us -> 829 us (0.70)
  waiting for transfers between devices: 513 us -> 0 us
  Pallas kernels: 507 us -> 780 us
  starting transfers between devices: 111 us -> 0 us
    ppermute x56 -> x0, waiting for transfers between devices: 513 us -> none  [across(): return lax.ppermute(value, 'dp', pairs)]
    pallas_call x8 -> x9, Pallas kernels: 507 us -> 780 us  [launch(): pl.pallas_call(entry, out_shape=[shape for shape, _ in outs.values()], in...]
    ppermute x56 -> x0, starting transfers between devices: 111 us -> none  [across(): return lax.ppermute(value, 'dp', pairs)]
  transfers between devices with their start and end apart: 56 -> 0, of which waited for: 25 -> 0; matrix products, arithmetic and copies ran while one was open for 2% -> 0% of each run, Pallas kernels for 16% -> 0%
where the time goes in v2:
time: 829 us; the launch traced here: 819 us
  Pallas kernels  780 us (94%)
  other arithmetic  19.3 us (2%)
  local copies, waits for them, and re-layouts  19 us (2%)
    pallas_call x9, Pallas kernels, launch(): pl.pallas_call(entry, out_shape=[shape for shape, _ in outs.values()], in...  780 us

profile of v2, /device:TPU:28, one launch (start us, length us, event | category | flops | bytes accessed | tf_op | source)
XLA Modules:
  0.0 819.2 jit_solution(9926153919538612218)
XLA Ops:
  3.5 1.3 convert_reduce_fusion.1
  5.5 2.0 select_select_fusion
  7.5 1.3 fusion.16
  8.8 0.9 convert.59
  9.7 0.9 convert.60
  10.7 0.9 convert.67
  11.6 0.9 convert.68
  12.6 1.1 convert.58
  13.7 0.9 concatenate.26.refs_5_.refs_6_
  14.6 0.9 concatenate.27.refs_6_.refs_5_
  15.7 0.9 pad_maximum_fusion.1.refs_7_.refs_0_
  17.3 0.9 pad_maximum_fusion.refs_8_.refs_0_
  18.2 1.0 copy.44.refs_3_
  19.2 1.0 convert_bitcast_fusion
  20.2 1.9 multiply_sine_fusion
  22.2 1.3 pad_maximum_fusion.2
  23.6 166.2 %attn_forward_0.1 = (f32[256,1536]{1,0:T(8,128)}, bf16[4,256,1536]{2,1,0:T(8,128)(2,1)}, bf16[1024,1024]{1,0:T(8,128)(2,1)}, bf16[1024,384]{1,0:T(8,128)(2,1)}, ...) custom-call(f32[256,1536]{1,0:T(8,128)} %refs_1_.1, ...), custom_call_target="tpu_custom_call" | custom-call | flops 20000000000 | bytes 60000000 | tf_op jit(solution)/shard_map/attn_forward_0/pallas_call | solution.py:1059
  189.7 81.1 %mlp_forward_0.1 = (f32[256,1536]{1,0:T(8,128)}, bf16[4,256,1536]{2,1,0:T(8,128)(2,1)}, bf16[1024,2048]{1,0:T(8,128)(2,1)}, bf16[1024,1024]{1,0:T(8,128)(2,1)}, ...) custom-call(bf16[192,2048]{1,0:T(8,128)(2,1)} %pad_maximum_fusion.1.refs_7_.refs_0_, ...), custom_call_target="tpu_custom_call" | custom-call | flops 20000000000 | bytes 60000000 | tf_op jit(solution)/shard_map/mlp_forward_0/pallas_call | solution.py:1059
  270.8 75.2 %attn_forward_1.1 = (f32[256,1536]{1,0:T(8,128)}, bf16[4,256,1536]{2,1,0:T(8,128)(2,1)}, bf16[1024,1024]{1,0:T(8,128)(2,1)}, bf16[1024,384]{1,0:T(8,128)(2,1)}, ...) custom-call(f32[256,1536]{1,0:T(8,128)} %get-tuple-element.76.refs_0, ...), custom_call_target="tpu_custom_call" | custom-call | flops 20000000000 | bytes 60000000 | tf_op jit(solution)/shard_map/attn_forward_1/pallas_call | solution.py:1059
  346.0 51.7 %mlp_forward_1.1 = (f32[256,1536]{1,0:T(8,128)}, bf16[4,256,1536]{2,1,0:T(8,128)(2,1)}, bf16[1024,2048]{1,0:T(8,128)(2,1)}, bf16[1024,1024]{1,0:T(8,128)(2,1)}) custom-call(bf16[192,2048]{1,0:T(8,128)(2,1)} %pad_maximum_fusion.refs_8_.refs_0_, bf16[8,192,2048]{2,1,0:T(8,128)(2,1)} %get-tuple-element.78.refs_1_, ...), custom_call_target="tpu_custom_call" | custom-call | flops 20000000000 | bytes 60000000 | tf_op jit(solution)/shard_map/mlp_forward_1/pallas_call | solution.py:1059
  397.7 64.8 %mlp_backward_1.1 = (f32[256,1536]{1,0:T(8,128)}, f32[8,1536]{1,0:T(8,128)}, bf16[8,192,2048]{2,1,0:T(8,128)(2,1)}, bf16[8,192,1024]{2,1,0:T(8,128)(2,1)}) custom-call(bf16[192,2048]{1,0:T(8,128)(2,1)} %pad_maximum_fusion.refs_8_.refs_0_, bf16[8,192,2048]{2,1,0:T(8,128)(2,1)} %get-tuple-element.78.refs_1_, ...), custom_call_target="tpu_custom_call" | custom-call | flops 20000000000 | bytes 60000000 | tf_op jit(solution)/shard_map/mlp_backward_1/pallas_call | solution.py:1059
  462.5 78.0 %attn_backward_1.1 = (f32[256,1536]{1,0:T(8,128)}, f32[8,1536]{1,0:T(8,128)}, bf16[8,192,1152]{2,1,0:T(8,128)(2,1)}, f32[192,2048]{1,0:T(8,128)}) custom-call(f32[256,1536]{1,0:T(8,128)} %get-tuple-element.85.refs_0_, f32[256,1536]{1,0:T(8,128)} %get-tuple-element.76.refs_0_.refs_1_, f32[16,1536]{1,0:T(8,128)} %get-tuple-element.75.refs_5_.refs_6_.refs_2_, ...), custom_call_target="tpu_custom_call" | custom-call | flops 20000000000 | bytes 60000000 | tf_op jit(solution)/shard_map/attn_backward_1/pallas_call | solution.py:1059
  540.5 93.3 %mlp_backward_0.1 = (f32[256,1536]{1,0:T(8,128)}, f32[8,1536]{1,0:T(8,128)}, bf16[8,192,2048]{2,1,0:T(8,128)(2,1)}, bf16[8,192,1024]{2,1,0:T(8,128)(2,1)}, f32[192,1024]{1,0:T(8,128)}, /*index=5*/f32[192,1152]{1,0:T(8,128)}) custom-call(bf16[192,2048]{1,0:T(8,128)(2,1)} %pad_maximum_fusion.1.refs_7_.refs_0_, ...), custom_call_target="tpu_custom_call" | custom-call | flops 20000000000 | bytes 60000000 | tf_op jit(solution)/shard_map/mlp_backward_0/pallas_call | solution.py:1059
  633.8 83.6 %attn_backward_0.1 = (f32[256,1536]{1,0:T(8,128)}, f32[8,1536]{1,0:T(8,128)}, bf16[8,192,1152]{2,1,0:T(8,128)(2,1)}, f32[192,2048]{1,0:T(8,128)}) custom-call(f32[256,1536]{1,0:T(8,128)} %get-tuple-element.100.refs_0_, f32[256,1536]{1,0:T(8,128)} %refs_1_.1, f32[16,1536]{1,0:T(8,128)} %get-tuple-element.75.refs_5_.refs_6_.refs_2_, ...), custom_call_target="tpu_custom_call" | custom-call | flops 20000000000 | bytes 60000000 | tf_op jit(solution)/shard_map/attn_backward_0/pallas_call | solution.py:1059
  717.4 86.1 %last_sums.1 = (f32[16,256]{1,0:T(8,128)}, f32[192,1024]{1,0:T(8,128)}, f32[192,1152]{1,0:T(8,128)}) custom-call(f32[8,1536]{1,0:T(8,128)} %get-tuple-element.111.refs_0_, f32[8,1536]{1,0:T(8,128)} %get-tuple-element.112.refs_1_, f32[8,1536]{1,0:T(8,128)} %get-tuple-element.113.refs_2_, f32[8,1536]{1,0:T(8,128)} %get-tuple-element.114.refs_3_, ...), custom_call_target="tpu_custom_call" | custom-call | flops 20000000000 | bytes 60000000 | tf_op jit(solution)/shard_map/last_sums/pallas_call | solution.py:1059
  803.5 1.4 fusion.23
  804.9 1.9 fusion.22
  806.9 1.9 slice_bitcast_fusion.1
  810.4 1.2 fusion.20
  812.4 1.2 fusion.19
  813.6 1.1 copy.50
  815.6 1.1 copy.51
  (56 shorter events, 9.9 us)
Async XLA Ops:
  0.7 13.9 %copy-start.15 = (f32[384,192]{0,1:T(8,128)S(1)}, f32[384,192]{0,1:T(8,128)}, u32[]{:S(2)}) copy-start(f32[384,192]{0,1:T(8,128)} %param.37) | copy-start | bytes 884740
  0.7 13.9 %copy-start.14 = (f32[192,384]{1,0:T(8,128)S(1)}, f32[192,384]{1,0:T(8,128)}, u32[]{:S(2)}) copy-start(f32[192,384]{1,0:T(8,128)} %param.34) | copy-start | bytes 884740
  0.7 13.0 %copy-start.13 = (f32[384,192]{0,1:T(8,128)S(1)}, f32[384,192]{0,1:T(8,128)}, u32[]{:S(2)}) copy-start(f32[384,192]{0,1:T(8,128)} %param.28) | copy-start | bytes 884740
  12.6 3.0 copy-start.5
  13.7 1.9 copy-start.6
  15.5 1.2 copy-start.7
  15.6 1.6 copy-start.8
  17.2 2.0 copy-start.11
  17.2 2.0 copy-start.12
  803.5 5.3 copy-start.4
  804.9 5.5 copy-start.3
  810.4 2.0 copy-start.1
  811.7 2.0 copy-start
  813.6 2.0 copy-start.2
  815.6 1.7 copy-start.10
  815.6 2.6 copy-start.9

commit v3 on v2

--- a/solution.py
+++ b/solution.py
@@ -42,6 +42,8 @@
 
 
 def tile(index, size):
+    if isinstance(index, int):
+        return pl.ds(index * size, size)
     return pl.ds(pl.multiple_of(index * size, size), size)
 
 
@@ -212,29 +214,63 @@
 class Fetch:
     def __init__(self, line, own, blocks, send, recv):
         self.line, self.own, self.blocks, self.send, self.recv = line, own, blocks, send, recv
+        rows = own.shape[0]
+        self.edge = max(rows // 6 // 16, 1) * 16 if rows > 32 else 0
+        self.rows = rows
 
     @staticmethod
     def scratch(n_dp):
-        return [pltpu.SemaphoreType.DMA((n_dp, 3))] * 2
-
-    def copy(self, slot, block, device, way):
-        source = self.own if slot == 0 else self.blocks.at[block]
+        return [pltpu.SemaphoreType.DMA((n_dp, 5))] * 2
+
+    def low(self, step):
+        return jnp.maximum(self.line.z - step, 0) * 2
+
+    def high(self, step):
+        return jnp.minimum(self.line.z + step, self.line.count - 1) * 2
+
+    def copy(self, slot, block, device, way, rows=None):
+        source = self.own if slot == 0 and way < 3 else self.blocks.at[block]
+        target = self.blocks.at[block]
+        if rows is not None:
+            source, target = source.at[rows], target.at[rows]
         return self.line.remote(
-            source, self.blocks.at[block], self.send.at[slot, way], self.recv.at[slot, way], device)
+            source, target, self.send.at[slot, way], self.recv.at[slot, way], device
+        )
 
     def upward(self, step):
-        line = self.line
-        return self.copy(step, jnp.maximum(line.z - step, 0) * 2 + line.x, line.up, 1)
+        return self.copy(step, self.low(step) + self.line.x, self.line.up, 1)
 
     def downward(self, step):
-        line = self.line
-        return self.copy(step, jnp.minimum(line.z + step, line.count - 1) * 2 + line.x, line.down, 2)
+        return self.copy(step, self.high(step) + self.line.x, self.line.down, 2)
+
+    def edge_up(self, step):
+        block = self.low(step) + 1 - self.line.x
+        return self.copy(step, block, self.line.up, 3, pl.ds(0, self.edge))
+
+    def edge_down(self, step):
+        block = self.high(step) + 1 - self.line.x
+        return self.copy(step, block, self.line.down, 4, pl.ds(0, self.edge))
 
     def sideways(self, step, low):
         line = self.line
+        rows = pl.ds(self.edge, self.rows - self.edge) if step and self.edge else None
         if low:
-            return self.copy(step, jnp.maximum(line.z - step, 0) * 2 + line.x, line.pair, 0)
-        return self.copy(line.count + step, jnp.minimum(line.z + step, line.count - 1) * 2 + line.x, line.pair, 0)
+            return self.copy(step, self.low(step) + line.x, line.pair, 0, rows)
+        return self.copy(line.count + step, self.high(step) + line.x, line.pair, 0, rows)
+
+    def upward_in(self, step):
+        return self.copy(step - 1, self.low(step) + self.line.x, self.line.up, 1)
+
+    def downward_in(self, step):
+        return self.copy(step - 1, self.high(step) + self.line.x, self.line.down, 2)
+
+    def edge_up_in(self, step):
+        block = self.low(step) + 1 - self.line.x
+        return self.copy(step - 1, block, self.line.up, 3, pl.ds(0, self.edge))
+
+    def edge_down_in(self, step):
+        block = self.high(step) + 1 - self.line.x
+        return self.copy(step - 1, block, self.line.down, 4, pl.ds(0, self.edge))
 
     def start(self):
         line = self.line
@@ -257,31 +293,60 @@
             pl.when(line.has_down)(lambda: self.downward(step).start())
             self.sideways(step, False).start()
 
-    def upward_in(self, step):
+        self.edges(step - 1)
+
+    def edges(self, step):
         line = self.line
-        return self.copy(step - 1, jnp.maximum(line.z - step, 0) * 2 + line.x, line.up, 1)
-
-    def downward_in(self, step):
-        line = self.line
-        return self.copy(step - 1, jnp.minimum(line.z + step, line.count - 1) * 2 + line.x, line.down, 2)
+        if step == 0:
+            self.sideways(0, True).wait_recv()
+        if not self.edge:
+            return
+        if step == 0:
+            pl.when(line.has_up)(lambda: self.edge_up(0).start())
+            pl.when(line.has_down)(lambda: self.edge_down(0).start())
+            return
+
+        @pl.when(line.z >= step)
+        def _():
+            self.edge_up_in(step).wait_recv()
+            pl.when(line.has_up)(lambda: self.edge_up(step).start())
+
+        @pl.when(line.z + step < line.count)
+        def _():
+            self.edge_down_in(step).wait_recv()
+            pl.when(line.has_down)(lambda: self.edge_down(step).start())
 
     def finish(self):
         line = self.line
+        self.edges(line.count - 1)
         for step in range(line.count):
 
             @pl.when(line.z >= step)
             def _():
-                pl.when(line.has_up)(lambda: self.upward(step).wait_send())
-                self.sideways(step, True).wait()
+                @pl.when(line.has_up)
+                def _():
+                    self.upward(step).wait_send()
+                    if self.edge:
+                        self.edge_up(step).wait_send()
+
+                self.sideways(step, True).wait_send()
+                if step:
+                    self.sideways(step, True).wait_recv()
 
             @pl.when(line.z + step < line.count)
             def _():
-                pl.when(line.has_down)(lambda: self.downward(step).wait_send())
+                @pl.when(line.has_down)
+                def _():
+                    self.downward(step).wait_send()
+                    if self.edge:
+                        self.edge_down(step).wait_send()
+
                 if step:
                     self.sideways(step, False).wait()
 
     def actions(self):
-        return [self.start] + [functools.partial(self.step, s) for s in range(1, self.line.count)] + [self.finish]
+        steps = [functools.partial(self.step, step) for step in range(1, self.line.count)]
+        return [self.start] + steps + [self.finish]
 
 
 class Reduce:
@@ -422,8 +487,9 @@
 
 
 class Weights:
-    def __init__(self, line, own, blocks, held, sems):
+    def __init__(self, line, own, blocks, held, sems, first=0):
         self.copies = []
+        columns = pl.ds(first, own.shape[1])
         depth = own.shape[0]
         count = line.count
         for index in range(2 * count):
@@ -431,7 +497,7 @@
             block = lax.rem(line.z + shift, count) * 2 + lax.rem(line.x + side, 2)
             source = blocks.at[block] if index else own
             rows = pl.ds(pl.multiple_of(block * depth, 16), depth)
-            self.copies.append(pltpu.make_async_copy(source, held.at[rows], sems.at[index]))
+            self.copies.append(pltpu.make_async_copy(source, held.at[rows, columns], sems.at[index]))
 
     def start(self):
         for copy in self.copies:
@@ -444,7 +510,7 @@
 
 class Pump:
     def __init__(self, tasks, plan):
-        self.steps = [step for task in tasks for step in task.actions()]
+        self.steps = [step for together in zip(*[task.actions() for task in tasks]) for step in together]
         self.plan = list(plan)
 
     def __call__(self):
@@ -517,6 +583,40 @@
     each(source.shape[0] // 32, close)
 
 
+def pack_attn(query, key, value, output, target):
+    width, each_kv = query.shape[1], key.shape[1]
+    target[:, 0:width] = query[...].astype(BF)
+    both = jnp.concatenate([key[...], value[...]], axis=1)
+    target[:, width : width + 2 * each_kv] = both.astype(BF)
+    target[:, width + 2 * each_kv :] = output[...].astype(BF)
+
+
+def count_rows(documents, below):
+    hits = jnp.where(documents < below, 1.0, 0.0)
+    return jnp.sum(jnp.sum(hits, axis=1, keepdims=True), axis=0, keepdims=True).astype(jnp.int32)
+
+
+def starts_of(marks, places):
+    head, body_end = marks[0:1, 0:1], marks[1:2, 0:1]
+    return jnp.where(places < head, 0, jnp.where(places < body_end, head, body_end))
+
+
+def make_tables(r):
+    marks = jnp.concatenate([count_rows(r.documents[...], 1), count_rows(r.documents[...], 2)], axis=0)
+    r.marks[0:2, :] = jnp.broadcast_to(marks, (2, PAD))
+    r.marks[2:, :] = jnp.zeros((6, PAD), jnp.int32)
+
+    def some(index):
+        where = tile(index, 128)
+        places = lax.broadcasted_iota(jnp.int32, (128, PAD), 0) + index * 128
+        offset = places - starts_of(r.marks, places)
+        angles = offset.astype(F32) * r.freqs[0:1, :]
+        r.cosine[where, :] = jnp.cos(angles)
+        r.sine[where, :] = jnp.sin(angles) * r.freqs[1:2, :]
+
+    each(r.cosine.shape[0] // 128, some)
+
+
 def attn_forward_kernel(first, level, fetch_count, plan, r):
     rows, width = r.x.shape
     n_dp, depth = r.w_sems.shape[0], r.own.shape[0]
@@ -527,7 +627,18 @@
     circles = (group, line) if first or tasks else (group,)
     meet(*circles)
     if first:
+        raw = {}
+        for name in ("gate0", "up0", "down0", "query1", "key1", "value1", "output1", "gate1", "up1", "down1"):
+            raw[name] = pltpu.make_async_copy(
+                getattr(r, "raw_" + name), getattr(r, name), r.raw_sems.at[len(raw)]
+            )
+            raw[name].start()
         lanes = r.gain_own.shape[1]
+        r.gain_raw[...] = jnp.zeros_like(r.gain_raw)
+        for row in range(4):
+            r.gain_raw[row : row + 1, 0:depth] = getattr(r, f"gain{row}")[...]
+        r.gain_own[...] = r.gain_raw[...].astype(BF)
+        pack_attn(r.raw_query0, r.raw_key0, r.raw_value0, r.raw_output0, r.own)
         gain_fetch = Fetch(line, r.gain_own, r.gain_blocks, r.gain_send, r.gain_recv)
         weight_fetch = Fetch(line, r.own, r.blocks, r.weight_send, r.weight_recv)
         gain_fetch.start()
@@ -550,10 +661,22 @@
         each(n_dp, gather_gain)
         norm_rows(r.x, r.gains[2 * level : 2 * level + 1, :], r.full, group.me)
         gather.start()
+        for name in ("gate0", "up0"):
+            raw[name].wait()
+        r.own0[...] = r.gate0[...].astype(BF)
+        r.own1[...] = r.up0[...].astype(BF)
         for step in weight_fetch.actions()[1:-1]:
             step()
         pump = Pump(tasks, plan)
         pump()
+        make_tables(r)
+        for name in list(raw)[2:]:
+            raw[name].wait()
+        pack_attn(r.query1, r.key1, r.value1, r.output1, r.attn_pack1)
+        r.down_pack0[...] = r.down0[...].astype(BF)
+        r.down_pack1[...] = r.down1[...].astype(BF)
+        r.gate_pack1[...] = r.gate1[...].astype(BF)
+        r.up_pack1[...] = r.up1[...].astype(BF)
         weight_fetch.finish()
         weights.start()
     else:
@@ -613,23 +736,28 @@
         prob = getattr(r, f"prob{turn}")
         reach = prob.shape[2]
         where = pl.ds(turn * rows, rows)
+        places = lax.broadcasted_iota(jnp.int32, (rows, PAD), 0) + turn * rows
+        begin = starts_of(r.marks, places)
+        head, body_end = r.marks[0:1, 0:1], r.marks[1:2, 0:1]
+        end = jnp.where(places < head, head, jnp.where(places < body_end, body_end, 4 * rows))
+        end = jnp.minimum(begin + ((places - begin) // BLOCK + 1) * BLOCK, end)
+        place_of = lax.broadcasted_iota(jnp.int32, (rows, reach), 1)
+        inside = (place_of >= begin[:, 0:1]) & (place_of < end[:, 0:1])
+        r.bias[:, 0:reach] = jnp.where(inside, 0.0, masked_value)
 
         def attend(head):
             query = qkv[where, tile(head, PAD)]
-            key = qkv[0:reach, pl.ds(pl.multiple_of(kv_at + head // 2 * PAD, PAD), PAD)]
-            value = qkv[0:reach, pl.ds(pl.multiple_of(value_at + head // 2 * PAD, PAD), PAD)]
-            scores = nt(query, key) * scale
-            place_of = lax.broadcasted_iota(jnp.int32, scores.shape, 1)
-            begin = r.spans[where, 0:1]
-            end = r.spans[where, 1:2]
-            scores = jnp.where((place_of >= begin) & (place_of < end), scores, masked_value)
+            key = qkv[0:reach, pl.ds(kv_at + head // 2 * PAD, PAD)]
+            value = qkv[0:reach, pl.ds(value_at + head // 2 * PAD, PAD)]
+            scores = nt(query, key) * scale + r.bias[:, 0:reach]
             exponent = jnp.exp(scores - jnp.max(scores, axis=-1, keepdims=True))
             summed = jnp.sum(exponent, axis=-1, keepdims=True)
             low = (exponent * (1.0 / summed)).astype(BF)
             prob[head] = low
             mixed[where, tile(head, PAD)] = nn(low, value).astype(BF)
 
-        each(heads, attend)
+        for head in range(heads):
+            attend(head)
         copy = pltpu.make_async_copy(prob, getattr(r, f"p_out{turn}"), r.out_sems.at[2 + turn])
         copy.start()
         copies.append(copy)
@@ -660,25 +788,33 @@
         copy.wait()
 
 
+def wide_of(line, r):
+    return [
+        Weights(line, r.gate_own, r.gate_blocks, r.wide, r.gate_sems),
+        Weights(line, r.up_own, r.up_blocks, r.wide, r.up_sems, r.gate_own.shape[1]),
+    ]
+
+
 def mlp_forward_kernel(level, fetch_count, plan, r):
     rows, width = r.middle.shape
     units = r.hid.shape[1]
-    line = Line(r.wide_sems.shape[0])
+    line = Line(r.w_sems.shape[0])
     group, gather, scatter = comm_of(r)
-    tasks = fetches_of(line, r, fetch_count)
+    down = Fetch(line, r.own, r.blocks, r.down_send, r.down_recv)
+    down_steps = down.actions()[1:-1]
     wide, held, gu, hid = r.wide, r.held, r.gu, r.hid
-    weights = [
-        Weights(line, r.wide_own, r.wide_blocks, wide, r.wide_sems),
-        Weights(line, r.own, r.blocks, held, r.w_sems),
-    ]
-    meet(*((group, line) if tasks else (group,)))
-    for each_of in weights:
-        each_of.start()
-    pump = Pump(tasks, plan)
+    wide_weights = wide_of(line, r)
+    weights = Weights(line, r.own, r.blocks, held, r.w_sems)
+    meet(group, line)
+    down.start()
+    for copy in wide_weights:
+        copy.start()
+    pump = Pump(fetches_of(line, r, fetch_count), plan)
     pump()
     norm_rows(r.middle, r.gains[2 * level + 1 : 2 * level + 2, :], r.full, group.me)
     gather.start()
-    weights[0].wait()
+    for copy in wide_weights:
+        copy.wait()
 
     def expand(chip):
         left = r.full[pl.ds(2 * chip, 2)].reshape(2 * rows, width)
@@ -697,11 +833,17 @@
 
     gather.wait_chip()
     expand(group.chip)
-    pump()
+    for step in down_steps[:1]:
+        step()
     gather.forward()
+    for step in down_steps[1:2]:
+        step()
     pump()
     gather.wait_other()
     expand(1 - group.chip)
+    for step in down_steps[2:]:
+        step()
+    pump()
     copies = [
         pltpu.make_async_copy(r.full, r.m_out, r.out_sems.at[0]),
         pltpu.make_async_copy(gu, r.gu_out, r.out_sems.at[1]),
@@ -709,8 +851,9 @@
     ]
     for copy in copies:
         copy.start()
-    pump()
-    weights[1].wait()
+    down.finish()
+    weights.start()
+    weights.wait()
     for turn in range(2):
         left = hid[tile(scatter.rows_of(turn), 2 * rows), :]
 
@@ -733,24 +876,19 @@
         copy.wait()
 
 
-def flip(source, target, slot):
-    _, rows, width = source.shape
-
-    def block(index):
-        columns = tile(index, 256)
-        target[columns, slot * rows : (slot + 1) * rows] = source[slot, :, columns].T
-
-    each(width // 256, block)
-
-
-def flip_pairs(source, target, slot):
-    rows, width = source.shape[2:]
-
-    def block(index):
-        columns = tile(index, 256)
-        target[columns, slot * rows : (slot + 1) * rows] = source[slot // 2, slot % 2, :, columns].T
-
-    each(width // 256, block)
+def weight_grads(source, right, target, columns):
+    width = source.shape[-1]
+    depth = target.shape[1]
+    chunk = math.lcm(depth, PAD)
+
+    def some(index):
+        left = source[..., tile(index, chunk)].reshape(right.shape[0], chunk)
+        product = tn(left, right[...]).astype(BF)
+        for part in range(chunk // depth):
+            rows = slice(part * depth, (part + 1) * depth)
+            target[index * (chunk // depth) + part, :, columns] = product[rows]
+
+    each(width // chunk, some)
 
 
 def close_back(scatter, grad_in_ref, state_ref, gain, grad_out, dgain):
@@ -774,33 +912,29 @@
 def mlp_backward_kernel(level, reduce_count, plan, r):
     rows, width = r.middle.shape
     units = r.hid.shape[1]
-    n_dp = r.wide_sems.shape[0]
-    depth = width // n_dp
+    n_dp = r.w_sems.shape[0]
     line = Line(n_dp)
     group, gather, scatter = comm_of(r)
-    tasks = reduces_of(line, r, reduce_count)
-    wide, held, gu, hid, flipped = r.wide, r.held, r.gu, r.hid, r.flipped
+    wide, held, gu, hid = r.wide, r.held, r.gu, r.hid
     weights = [
         Weights(line, r.own, r.blocks, held, r.w_sems),
-        Weights(line, r.wide_own, r.wide_blocks, wide, r.wide_sems),
+        *wide_of(line, r),
     ]
     fetches = [
-        pltpu.make_async_copy(r.m_in, r.parts, r.in_sems.at[0]),
+        pltpu.make_async_copy(r.hid_in, hid, r.in_sems.at[2]),
         pltpu.make_async_copy(r.gu_in, gu, r.in_sems.at[1]),
-        pltpu.make_async_copy(r.hid_in, hid, r.in_sems.at[2]),
+        pltpu.make_async_copy(r.m_in, r.m_full, r.in_sems.at[0]),
     ]
-    meet(*((group, line) if tasks else (group,)))
-    for copy in fetches + weights:
+    down = Reduce(line, r.grads, r.down_total, *[getattr(r, f"down{j}") for j in range(8)])
+    meet(group, line)
+    pump = Pump(reduces_of(line, r, reduce_count), plan)
+    pump.steps += down.actions()[1:]
+    pump()
+    for copy in weights[:1] + fetches + weights[1:]:
         copy.start()
-    pump = Pump(tasks, plan)
-    pump()
     r.full[group.me] = r.grad[...].astype(BF)
     gather.start()
-    fetches[0].wait()
-    for slot in range(4):
-        flip_pairs(r.parts, flipped, slot)
-    pump()
-    for copy in weights + fetches[1:]:
+    for copy in weights[:1] + fetches[:2]:
         copy.wait()
 
     def inward(chip):
@@ -825,7 +959,11 @@
     gather.forward()
     pump()
     gather.wait_other()
+    weight_grads(r.full, hid, r.grads, slice(0, units))
+    down.start()
     inward(1 - group.chip)
+    for copy in weights[1:] + fetches[2:]:
+        copy.wait()
     pump()
     for turn in range(2):
         where = tile(scatter.rows_of(turn), 2 * rows)
@@ -839,33 +977,12 @@
         if turn == 0:
             scatter.send_away()
         pump()
-
-    def grads_of(block, target, slot, right):
-        left = flipped[pl.ds(pl.multiple_of(block * depth, 16), depth), :]
-
-        def some(index):
-            columns = tile(index, 512)
-            target[slot, :, columns] = nn(left, right[:, columns]).astype(BF)
-
-        each(right.shape[1] // 512, some)
-
-    half = n_dp // 2
-    copies = []
     for part in range(2):
-        for copy in copies:
-            copy.wait()
-        each(half, lambda slot: grads_of(part * half + slot, r.wide_grads, slot, gu))
-        copies = [
-            pltpu.make_async_copy(r.wide_grads, r.wide_out.at[pl.ds(part * half, half)], r.out_sems.at[part])
-        ]
-        copies[0].start()
+        columns = slice(part * units, (part + 1) * units)
+        weight_grads(r.m_full, gu.at[:, columns], r.wide_grads, columns)
         pump()
-    for slot in range(4):
-        flip(r.full, flipped, slot)
-    each(n_dp, lambda block: grads_of(block, r.grads, block, hid))
-    copies.append(pltpu.make_async_copy(r.grads, r.grads_out, r.out_sems.at[2]))
-    copies[-1].start()
-    pump()
+    copies = [pltpu.make_async_copy(r.wide_grads, r.wide_out, r.out_sems.at[0])]
+    copies[0].start()
     scatter.wait()
     pump()
     close_back(
@@ -885,11 +1002,11 @@
     line = Line(n_dp)
     group, gather, scatter = comm_of(r)
     tasks = reduces_of(line, r, reduce_count)
-    held, qkv, compact, flipped = r.held, r.qkv, r.compact, r.flipped
+    held, qkv, compact = r.held, r.qkv, r.compact
     probs = [getattr(r, f"prob{turn}") for turn in range(4)]
     weights = Weights(line, r.own, r.blocks, held, r.w_sems)
     fetches = [
-        pltpu.make_async_copy(r.a_in, r.parts, r.in_sems.at[0]),
+        pltpu.make_async_copy(r.a_in, r.a_full, r.in_sems.at[0]),
         pltpu.make_async_copy(r.o_in, compact, r.in_sems.at[1]),
         pltpu.make_async_copy(r.qkv_in, qkv, r.in_sems.at[2]),
     ] + [
@@ -897,20 +1014,16 @@
         for turn in range(4)
     ]
     meet(*((group, line) if tasks else (group,)))
-    fetches[0].start()
     weights.start()
-    for copy in fetches[1:]:
+    for copy in fetches:
         copy.start()
     pump = Pump(tasks, plan)
     pump()
     r.full[group.me] = r.grad[...].astype(BF)
     gather.start()
-    fetches[0].wait()
-    for slot in range(4):
-        flip_pairs(r.parts, flipped, slot)
     pump()
     weights.wait()
-    for copy in fetches[1:]:
+    for copy in fetches:
         copy.wait()
     place = r.place[...]
     heads = place.shape[1] // PAD
@@ -942,8 +1055,8 @@
             mine = tile(head, PAD)
             shared = tile(head // 2, PAD)
             query = qkv[where, mine]
-            key = qkv[0:reach, pl.ds(pl.multiple_of(kv_at + head // 2 * PAD, PAD), PAD)]
-            value = qkv[0:reach, pl.ds(pl.multiple_of(value_at + head // 2 * PAD, PAD), PAD)]
+            key = qkv[0:reach, pl.ds(kv_at + head // 2 * PAD, PAD)]
+            value = qkv[0:reach, pl.ds(value_at + head // 2 * PAD, PAD)]
             grad = r.grad_mixed[where, mine]
             low = prob[head]
             grad_prob = nt(grad, value)
@@ -955,7 +1068,8 @@
             r.grad_k[0:reach, shared] += tn(grad_score, query)
             r.grad_v[0:reach, shared] += tn(low, grad)
 
-        each(heads, attend)
+        for head in range(heads):
+            attend(head)
         pump()
     for pair in range(heads // 2):
         columns = pl.ds(pair * PAD, PAD)
@@ -980,15 +1094,8 @@
             scatter.send_away()
         pump()
     grads = r.grads
-
-    def grads_of(block, begin, right):
-        left = flipped[pl.ds(pl.multiple_of(block * depth, 16), depth), :]
-        grads[block, :, begin : begin + right.shape[1]] = nn(left, right[...]).astype(BF)
-
-    each(n_dp, lambda block: grads_of(block, 0, grad_low))
-    for slot in range(4):
-        flip(r.full, flipped, slot)
-    each(n_dp, lambda block: grads_of(block, 2 * compact_width, compact))
+    weight_grads(r.a_full, grad_low, grads, slice(0, 2 * compact_width))
+    weight_grads(r.full, compact, grads, slice(2 * compact_width, 3 * compact_width))
     copy = pltpu.make_async_copy(grads, r.grads_out, r.out_sems.at[0])
     copy.start()
     pump()
@@ -1070,7 +1177,7 @@
         ),
         name=name,
     )(*[array for array, _ in ins.values()])
-    return dict(zip(outs, results))
+    return types.SimpleNamespace(**dict(zip(outs, results)))
 
 
 def comm_scratch(rows, width):
@@ -1112,24 +1219,24 @@
 
 
 def totals(out, count):
-    return [out[f"total{i}"] for i in range(count)]
+    return [getattr(out, f"total{i}") for i in range(count)]
 
 
 def fetched(out, count):
-    return [out[f"blocks{i}"] for i in range(count)]
-
-
-def attn_forward(level, which, states, tables, gains, pack, blocks, packs, plan, gain_pack=None):
-    cosine, sine, spans, place = tables
+    return [getattr(out, f"blocks{i}") for i in range(count)]
+
+
+def attn_forward(level, which, states, tables, place, gains, pack, blocks, packs, plan, raw=None):
     rows, width = states.shape
-    first = blocks is None
-    n_dp = width // pack.shape[0]
-    columns = pack.shape[1]
+    first = raw is not None
+    if first:
+        depth, columns = raw["raw_query0"].shape[0], 3 * raw["raw_query0"].shape[1]
+        pack = shaped((depth, columns), BF)
+    depth, columns = pack.shape
+    n_dp = width // depth
     heads = place.shape[1] // PAD
     length = 4 * rows
-    ins = dict(
-        x=(states, VM), cosine=(cosine, VM), sine=(sine, VM), spans=(spans, VM), place=(place, VM), own=(pack, ANY)
-    )
+    ins = dict(x=(states, VM), place=(place, VM))
     outs = dict(
         middle=(shaped((rows, width), F32), VM),
         a_out=(shaped((4, rows, width), BF), ANY),
@@ -1142,6 +1249,7 @@
         qkv=vmem(length, 2 * heads * PAD),
         mixed=vmem(length, heads * PAD),
         compact=vmem(length, place.shape[0]),
+        bias=vmem(rows, length, dtype=F32),
         w_sems=dma(n_dp),
         out_sems=dma(7),
     )
@@ -1149,48 +1257,79 @@
         outs[f"p_out{turn}"] = (shaped((heads, rows, reach), BF), ANY)
         scratch[f"prob{turn}"] = vmem(heads, rows, reach)
     if first:
-        ins["gain_own"] = (gain_pack, VM)
-        outs["gains"] = (shaped((gain_pack.shape[0], width), F32), VM)
-        outs["blocks"] = (blocks_of(pack, n_dp), ANY)
-        scratch["gain_blocks"] = vmem(n_dp, *gain_pack.shape)
-        scratch["gain_send"], scratch["gain_recv"] = Fetch.scratch(n_dp)
-        scratch["weight_send"], scratch["weight_recv"] = Fetch.scratch(n_dp)
+        units = raw["raw_gate0"].shape[1]
+        now = ("raw_query0", "raw_key0", "raw_value0", "raw_output0")
+        for name, array in raw.items():
+            late = name.startswith("raw_") and name not in now
+            ins[name] = (array, ANY if late else VM)
+            if late:
+                scratch[name[4:]] = vmem(*array.shape, dtype=F32)
+        outs |= dict(
+            gains=(shaped((GAIN_ROWS, width), F32), VM),
+            blocks=(blocks_of(pack, n_dp), ANY),
+            own=(pack, VM),
+            own0=(shaped((depth, units), BF), VM),
+            own1=(shaped((depth, units), BF), VM),
+            blocks0=(shaped((n_dp, depth, units), BF), ANY),
+            blocks1=(shaped((n_dp, depth, units), BF), ANY),
+            down_pack0=(shaped((depth, units), BF), VM),
+            attn_pack1=(pack, VM),
+            gate_pack1=(shaped((depth, units), BF), VM),
+            up_pack1=(shaped((depth, units), BF), VM),
+            down_pack1=(shaped((depth, units), BF), VM),
+            cosine=(shaped((length, PAD), F32), VM),
+            sine=(shaped((length, PAD), F32), VM),
+            marks=(shaped((8, PAD), jnp.int32), VM),
+        )
+        scratch["gain_raw"] = vmem(GAIN_ROWS, 256, dtype=F32)
+        scratch["gain_own"] = vmem(GAIN_ROWS, 256)
+        scratch["gain_blocks"] = vmem(n_dp, GAIN_ROWS, 256)
+        scratch["raw_sems"] = dma(10)
+        for name, tail in (("gain", ""), ("weight", ""), ("fetch", "0"), ("fetch", "1")):
+            scratch[f"{name}_send{tail}"], scratch[f"{name}_recv{tail}"] = Fetch.scratch(n_dp)
+        more = {}, {}, {}
     else:
-        ins["gains"] = (gains, VM)
-        ins["blocks"] = (blocks, ANY)
-    more = fetch_refs(packs, n_dp)
+        cosine, sine, marks = tables
+        ins |= dict(
+            gains=(gains, VM), cosine=(cosine, VM), sine=(sine, VM), marks=(marks, VM), own=(pack, ANY), blocks=(blocks, ANY)
+        )
+        more = fetch_refs(packs, n_dp)
     return launch(
-        functools.partial(attn_forward_kernel, first, level, len(packs), plan),
+        functools.partial(attn_forward_kernel, first, level, 2 if first else len(packs), plan),
         which, f"attn_forward_{level}", ins | more[0], outs | more[1], scratch | more[2],
     )
 
 
-def mlp_refs(rows, width, wide, down):
-    n_dp = width // wide[0].shape[0]
-    units = down[0].shape[1]
-    ins = dict(wide_own=(wide[0], ANY), wide_blocks=(wide[1], ANY), own=(down[0], ANY), blocks=(down[1], ANY))
+def mlp_refs(rows, width, wide, own):
+    depth, units = own.shape
+    n_dp = width // depth
+    ins = dict(own=(own, ANY))
+    ins |= {name: (array, ANY) for name, array in wide.items()}
     scratch = comm_scratch(rows, width) | dict(
         wide=vmem(width, 2 * units),
         held=vmem(width, units),
         gu=vmem(4 * rows, 2 * units),
         hid=vmem(4 * rows, units),
-        wide_sems=dma(n_dp),
+        gate_sems=dma(n_dp),
+        up_sems=dma(n_dp),
         w_sems=dma(n_dp),
     )
     return n_dp, units, ins, scratch
 
 
-def mlp_forward(level, which, middle, gains, wide, down, packs, plan):
+def mlp_forward(level, which, middle, gains, wide, down_own, packs, plan):
     rows, width = middle.shape
-    n_dp, units, ins, scratch = mlp_refs(rows, width, wide, down)
+    n_dp, units, ins, scratch = mlp_refs(rows, width, wide, down_own)
     ins |= dict(middle=(middle, VM), gains=(gains, VM))
     outs = dict(
         result=(shaped((rows, width), F32), VM),
         m_out=(shaped((4, rows, width), BF), ANY),
         gu_out=(shaped((4 * rows, 2 * units), BF), ANY),
         hid_out=(shaped((4 * rows, units), BF), ANY),
+        blocks=(blocks_of(down_own, n_dp), ANY),
     )
     scratch |= dict(out_sems=dma(3))
+    scratch["down_send"], scratch["down_recv"] = Fetch.scratch(n_dp)
     more = fetch_refs(packs, n_dp)
     return launch(
         functools.partial(mlp_forward_kernel, level, len(packs), plan),
@@ -1200,25 +1339,28 @@
 
 def mlp_backward(level, which, grad, middle, gains, saved, wide, down, sums, plan):
     rows, width = middle.shape
-    n_dp, units, ins, scratch = mlp_refs(rows, width, wide, down)
+    n_dp, units, ins, scratch = mlp_refs(rows, width, wide, down[0])
     depth = width // n_dp
     ins |= dict(
+        blocks=(down[1], ANY),
         grad=(grad, VM), middle=(middle, VM), gains=(gains, VM),
-        m_in=(saved["m_out"].reshape(2, 2, rows, width), ANY), gu_in=(saved["gu_out"], ANY), hid_in=(saved["hid_out"], ANY),
+        m_in=(saved.m_out, ANY), gu_in=(saved.gu_out, ANY), hid_in=(saved.hid_out, ANY),
     )
     outs = dict(
         grad_out=(shaped((rows, width), F32), VM),
         dgain=(shaped((8, width), F32), VM),
         wide_out=(shaped((n_dp, depth, 2 * units), BF), ANY),
-        grads_out=(shaped((n_dp, depth, units), BF), ANY),
+        down_total=(shaped((depth, units), F32), VM),
     )
     scratch |= dict(
-        flipped=vmem(width, 4 * rows),
-        wide_grads=vmem(n_dp // 2, depth, 2 * units),
+        m_full=vmem(4, rows, width),
+        wide_grads=vmem(n_dp, depth, 2 * units),
         grads=vmem(n_dp, depth, units),
         in_sems=dma(3),
         out_sems=dma(3),
     )
+    for j, each_of in enumerate(Reduce.scratch(n_dp, depth, units)):
+        scratch[f"down{j}"] = each_of
     more = reduce_refs(sums)
     return launch(
         functools.partial(mlp_backward_kernel, level, len(sums), plan),
@@ -1226,8 +1368,8 @@
     )
 
 
-def attn_backward(level, which, grad, states, gains, tables, saved, weights, sums, plan):
-    cosine, sine, _, place = tables
+def attn_backward(level, which, grad, states, gains, tables, place, saved, weights, sums, plan):
+    cosine, sine, _ = tables
     pack, blocks = weights
     rows, width = states.shape
     depth, columns = pack.shape
@@ -1237,7 +1379,7 @@
     ins = dict(
         grad=(grad, VM), x=(states, VM), gains=(gains, VM), cosine=(cosine, VM), sine=(sine, VM), place=(place, VM),
         own=(pack, ANY), blocks=(blocks, ANY),
-        a_in=(saved["a_out"].reshape(2, 2, rows, width), ANY), qkv_in=(saved["qkv_out"], ANY), o_in=(saved["o_out"], ANY),
+        a_in=(saved.a_out, ANY), qkv_in=(saved.qkv_out, ANY), o_in=(saved.o_out, ANY),
     )
     outs = dict(
         grad_out=(shaped((rows, width), F32), VM),
@@ -1246,7 +1388,7 @@
     )
     scratch = comm_scratch(rows, width) | dict(
         held=vmem(width, columns),
-        flipped=vmem(width, length),
+        a_full=vmem(4, rows, width),
         qkv=vmem(length, 2 * heads * PAD),
         compact=vmem(length, place.shape[0]),
         grad_mixed=vmem(length, heads * PAD),
@@ -1261,7 +1403,7 @@
         out_sems=dma(1),
     )
     for turn, reach in enumerate(reaches(rows)):
-        ins[f"p_in{turn}"] = (saved[f"p_out{turn}"], ANY)
+        ins[f"p_in{turn}"] = (getattr(saved, f"p_out{turn}"), ANY)
         scratch[f"prob{turn}"] = vmem(heads, rows, reach)
     more = reduce_refs(sums)
     return launch(
@@ -1291,96 +1433,89 @@
     )
 
 
-def tables_of(documents, heads):
-    length = documents.shape[0]
-    places = jnp.arange(length, dtype=jnp.int32)
-    head = jnp.sum((documents == 0).astype(jnp.int32))
-    body_end = jnp.sum((documents <= 1).astype(jnp.int32))
-    starts = jnp.where(documents == 0, 0, jnp.where(documents == 1, head, body_end))
-    ends = jnp.where(documents == 0, head, jnp.where(documents == 1, body_end, length))
-    offset = places - starts
-    last = jnp.minimum(starts + (offset // BLOCK + 1) * BLOCK, ends)
-    spans = jnp.stack([starts, last], axis=1)
-    freqs = jnp.exp(
-        jnp.arange(HALF, dtype=F32) * (-2.0 * math.log(rope_base) / HEAD_DIM)
-    )
-    angles = offset.astype(F32)[:, None] * freqs[None, :]
-    gap = ((0, 0), (0, PAD // 2 - HALF))
-    cos_half = jnp.pad(jnp.cos(angles), gap)
-    sin_half = jnp.pad(jnp.sin(angles), gap)
-    cosine = jnp.concatenate([cos_half, cos_half], axis=1)
-    sine = jnp.concatenate([-sin_half, sin_half], axis=1)
+def constants(heads):
     place = np.zeros((heads * HEAD_DIM, heads * PAD), np.float32)
     for row in range(heads * HEAD_DIM):
         which, column = divmod(row, HEAD_DIM)
         place[row, which * PAD + column + (PAD // 2 - HALF if column >= HALF else 0)] = 1.0
-    return cosine, sine, spans, jnp.asarray(place, BF)
-
-
-def pack_gains(gains):
-    stacked = jnp.stack(gains).astype(BF)
-    return jnp.pad(stacked, ((0, GAIN_ROWS - stacked.shape[0]), (0, 256 - stacked.shape[1])))
+    freqs = np.zeros((8, PAD), np.float32)
+    for start in (0, PAD // 2):
+        freqs[0, start : start + HALF] = np.exp(np.arange(HALF) * (-2.0 * math.log(rope_base) / HEAD_DIM))
+    freqs[1, 0 : PAD // 2] = -1.0
+    freqs[1, PAD // 2 :] = 1.0
+    return jnp.asarray(place, BF), jnp.asarray(freqs)
 
 
 def body(states_in, documents, *rest):
     cotangent = rest[-1]
     one, two = rest[0:9], rest[9:18]
     heads = one[1].shape[1] // HEAD_DIM
-    tables = tables_of(documents, heads)
-    attn_pack = [jnp.concatenate([w[1], w[2], w[3], w[4].T], axis=1).astype(BF) for w in (one, two)]
-    wide_pack = [jnp.concatenate([w[6], w[7]], axis=1).astype(BF) for w in (one, two)]
-    down_pack = [w[8].T.astype(BF) for w in (one, two)]
-    gain_pack = pack_gains([one[0], one[5], two[0], two[5]])
+    place, freqs = constants(heads)
+    raw = dict(documents=documents.reshape(-1, PAD), freqs=freqs)
+    for level, w in enumerate((one, two)):
+        raw[f"gain{2 * level}"] = w[0].reshape(1, -1)
+        raw[f"gain{2 * level + 1}"] = w[5].reshape(1, -1)
+        for name, array in zip(("query", "key", "value", "output", "", "gate", "up", "down"), w[1:]):
+            if name:
+                raw[f"raw_{name}{level}"] = array.T if name in ("output", "down") else array
 
     attn1 = attn_forward(
-        0, 0, states_in, tables, None, attn_pack[0], None, [wide_pack[0], down_pack[0]],
-        [1, 0, 1, 0, 1, 0, 1, 1, 1, 1], gain_pack,
-    )
-    gains = attn1["gains"]
-    wide1, down1 = fetched(attn1, 2)
+        0, 0, states_in, None, place, None, None, None, None, [2, 1, 0, 1, 0, 0, 1, 0, 0, 2, 1], raw
+    )
+    tables = (attn1.cosine, attn1.sine, attn1.marks)
+    attn_pack = [attn1.own, attn1.attn_pack1]
+    down_pack = [attn1.down_pack0, attn1.down_pack1]
+    gains = attn1.gains
+    wide1 = dict(
+        gate_own=attn1.own0, gate_blocks=attn1.blocks0, up_own=attn1.own1, up_blocks=attn1.blocks1
+    )
     mlp1 = mlp_forward(
-        0, 1, attn1["middle"], gains, (wide_pack[0], wide1), (down_pack[0], down1),
-        [attn_pack[1], down_pack[1]], [1, 1, 1, 1, 2, 1, 1],
-    )
-    attn2_blocks, down2 = fetched(mlp1, 2)
+        0, 1, attn1.middle, gains, wide1, down_pack[0], [attn_pack[1]], [0, 0, 1, 1, 2, 0]
+    )
+    down1 = (down_pack[0], mlp1.blocks)
+    (attn2_blocks,) = fetched(mlp1, 1)
     attn2 = attn_forward(
-        1, 2, mlp1["result"], tables, gains, attn_pack[1], attn2_blocks, [wide_pack[1]],
-        [1, 0, 1, 0, 0, 1, 0, 0, 1, 0, 0],
-    )
-    (wide2,) = fetched(attn2, 1)
-    mlp2 = mlp_forward(1, 3, attn2["middle"], gains, (wide_pack[1], wide2), (down_pack[1], down2), [], [])
+        1, 2, mlp1.result, tables, place, gains, attn_pack[1], attn2_blocks, [attn1.gate_pack1, attn1.up_pack1],
+        [2, 1, 1, 0, 0, 0, 1, 0, 0, 2, 1],
+    )
+    wide2 = dict(
+        gate_own=attn1.gate_pack1, gate_blocks=attn2.blocks0, up_own=attn1.up_pack1, up_blocks=attn2.blocks1
+    )
+    mlp2 = mlp_forward(1, 3, attn2.middle, gains, wide2, down_pack[1], [], [])
+    down2 = (down_pack[1], mlp2.blocks)
 
     back_mlp2 = mlp_backward(
-        1, 4, cotangent, attn2["middle"], gains, mlp2, (wide_pack[1], wide2), (down_pack[1], down2), [], []
+        1, 4, cotangent, attn2.middle, gains, mlp2, wide2, down2, [], [0, 0, 0, 0, 0, 1, 1, 1]
     )
     back_attn2 = attn_backward(
-        1, 5, back_mlp2["grad_out"], mlp1["result"], gains, tables, attn2, (attn_pack[1], attn2_blocks),
-        [back_mlp2["wide_out"]], [1, 0, 0, 1, 0, 1, 0, 0, 0, 1],
+        1, 5, back_mlp2.grad_out, mlp1.result, gains, tables, place, attn2, (attn_pack[1], attn2_blocks),
+        [back_mlp2.wide_out], [1, 0, 0, 1, 0, 1, 0, 0, 0, 1],
     )
     back_mlp1 = mlp_backward(
-        0, 6, back_attn2["grad_out"], attn1["middle"], gains, mlp1, (wide_pack[0], wide1), (down_pack[0], down1),
-        [back_mlp2["grads_out"], back_attn2["grads_out"]], [1, 1, 1, 1, 1, 1, 1, 0, 1, 0, 1],
+        0, 6, back_attn2.grad_out, attn1.middle, gains, mlp1, wide1, down1,
+        [back_attn2.grads_out], [1, 1, 1, 1, 1, 1, 0, 1, 1],
     )
     back_attn1 = attn_backward(
-        0, 7, back_mlp1["grad_out"], states_in, gains, tables, attn1, (attn_pack[0], attn1["blocks"]),
-        [back_mlp1["wide_out"]], [1, 0, 0, 1, 0, 1, 0, 0, 0, 1],
+        0, 7, back_mlp1.grad_out, states_in, gains, tables, place, attn1, (attn_pack[0], attn1.blocks),
+        [back_mlp1.wide_out], [1, 0, 0, 1, 0, 0, 1, 0, 0, 1],
     )
     last = last_sums(
         8,
-        [back_attn1["dgain"], back_mlp1["dgain"], back_attn2["dgain"], back_mlp2["dgain"]],
-        [back_mlp1["grads_out"], back_attn1["grads_out"]],
+        [back_attn1.dgain, back_mlp1.dgain, back_attn2.dgain, back_mlp2.dgain],
+        [back_attn1.grads_out],
     )
     (wide_total2,) = totals(back_attn2, 1)
-    down_total2, attn_total2 = totals(back_mlp1, 2)
+    (attn_total2,) = totals(back_mlp1, 1)
     (wide_total1,) = totals(back_attn1, 1)
-    down_total1, attn_total1 = totals(last, 2)
-    gain_total = last["gain_total"]
+    (attn_total1,) = totals(last, 1)
+    down_total1, down_total2 = back_mlp1.down_total, back_mlp2.down_total
+    gain_total = last.gain_total
     depth = down_total1.shape[0]
     bounds = [0]
     for w in one[1:4]:
         bounds.append(bounds[-1] + w.shape[1])
     units = one[6].shape[1]
-    outs = [mlp2["result"], back_attn1["grad_out"]]
+    outs = [mlp2.result, back_attn1.grad_out]
     for level, (attn_total, wide_total, down_total) in enumerate(
         ((attn_total1, wide_total1, down_total1), (attn_total2, wide_total2, down_total2))
     ):

time: 829 us -> 719 us (0.87)
  Pallas kernels: 780 us -> 697 us
  other arithmetic: 19.3 us -> 0 us
    pallas_call x9, Pallas kernels: 780 us -> 697 us  [launch(): pl.pallas_call(entry, out_shape=[shape for shape, _ in outs.values()], in...]
    another operation x16 -> x0, other arithmetic: 8.45 us -> none
where the time goes in v3:
time: 719 us; the launch traced here: 710 us
  Pallas kernels  697 us (97%)
  local copies, waits for them, and re-layouts  12.6 us (2%)
    pallas_call x9, Pallas kernels, launch(): pl.pallas_call(entry, out_shape=[shape for shape, _ in outs.values()], in...  697 us

profile of v3, /device:TPU:28, one launch (start us, length us, event | category | flops | bytes accessed | tf_op | source)
XLA Modules:
  0.0 710.3 jit_solution(9730882594539583651)
XLA Ops:
  0.7 115.8 %attn_forward_0.1 = (f32[256,1536]{1,0:T(8,128)}, bf16[4,256,1536]{2,1,0:T(8,128)(2,1)}, bf16[1024,1024]{1,0:T(8,128)(2,1)}, bf16[1024,384]{1,0:T(8,128)(2,1)}, ...) custom-call(f32[256,1536]{1,0:T(8,128)} %refs_1_.3, ...), custom_call_target="tpu_custom_call" | custom-call | flops 20000000000 | bytes 60000000 | tf_op jit(solution)/shard_map/attn_forward_0/pallas_call | solution.py:1166
  116.4 82.6 %mlp_forward_0.1 = (f32[256,1536]{1,0:T(8,128)}, bf16[4,256,1536]{2,1,0:T(8,128)(2,1)}, bf16[1024,2048]{1,0:T(8,128)(2,1)}, bf16[1024,1024]{1,0:T(8,128)(2,1)}, ...) custom-call(bf16[192,1024]{1,0:T(8,128)(2,1)} %get-tuple-element.85.refs_0_, ...), custom_call_target="tpu_custom_call" | custom-call | flops 20000000000 | bytes 60000000 | tf_op jit(solution)/shard_map/mlp_forward_0/pallas_call | solution.py:1166
  199.1 72.0 %attn_forward_1.1 = (f32[256,1536]{1,0:T(8,128)}, bf16[4,256,1536]{2,1,0:T(8,128)(2,1)}, bf16[1024,1024]{1,0:T(8,128)(2,1)}, bf16[1024,384]{1,0:T(8,128)(2,1)}, ...) custom-call(f32[256,1536]{1,0:T(8,128)} %get-tuple-element.93.refs_0, ...), custom_call_target="tpu_custom_call" | custom-call | flops 20000000000 | bytes 60000000 | tf_op jit(solution)/shard_map/attn_forward_1/pallas_call | solution.py:1166
  271.0 63.9 %mlp_forward_1.1 = (f32[256,1536]{1,0:T(8,128)}, bf16[4,256,1536]{2,1,0:T(8,128)(2,1)}, bf16[1024,2048]{1,0:T(8,128)(2,1)}, bf16[1024,1024]{1,0:T(8,128)(2,1)}, bf16[8,192,1024]{2,1,0:T(8,128)(2,1)}) custom-call(bf16[192,1024]{1,0:T(8,128)(2,1)} %get-tuple-element.83.refs_0_, bf16[192,1024]{1,0:T(8,128)(2,1)} %get-tuple-element.84.refs_8_.refs_1_, ...), custom_call_target="tpu_custom_call" | custom-call | flops 20000000000 | bytes 60000000 | tf_op jit(solution)/shard_map/mlp_forward_1/pallas_call | solution.py:1166
  335.0 75.5 %mlp_backward_1.1 = (f32[256,1536]{1,0:T(8,128)}, f32[8,1536]{1,0:T(8,128)}, bf16[8,192,2048]{2,1,0:T(8,128)(2,1)}, f32[192,1024]{1,0:T(8,128)}) custom-call(bf16[192,1024]{1,0:T(8,128)(2,1)} %get-tuple-element.83.refs_0_, bf16[192,1024]{1,0:T(8,128)(2,1)} %get-tuple-element.84.refs_8_.refs_1_, bf16[8,192,1024]{2,1,0:T(8,128)(2,1)} %get-tuple-element.99.refs_2_, ...), custom_call_target="tpu_custom_call" | custom-call | flops 20000000000 | bytes 60000000 | tf_op jit(solution)/shard_map/mlp_backward_1/pallas_call | solution.py:1166
  410.4 74.5 %attn_backward_1.1 = (f32[256,1536]{1,0:T(8,128)}, f32[8,1536]{1,0:T(8,128)}, bf16[8,192,1152]{2,1,0:T(8,128)(2,1)}, f32[192,2048]{1,0:T(8,128)}) custom-call(f32[256,1536]{1,0:T(8,128)} %get-tuple-element.108.refs_0_, f32[256,1536]{1,0:T(8,128)} %get-tuple-element.93.refs_0_.refs_1_, f32[16,1536]{1,0:T(8,128)} %get-tuple-element.91.refs_6_.refs_2_.refs_8_, ...), custom_call_target="tpu_custom_call" | custom-call | flops 20000000000 | bytes 60000000 | tf_op jit(solution)/shard_map/attn_backward_1/pallas_call | solution.py:1166
  485.0 83.1 %mlp_backward_0.1 = (f32[256,1536]{1,0:T(8,128)}, f32[8,1536]{1,0:T(8,128)}, bf16[8,192,2048]{2,1,0:T(8,128)(2,1)}, f32[192,1024]{1,0:T(8,128)}, f32[192,1152]{1,0:T(8,128)}) custom-call(bf16[192,1024]{1,0:T(8,128)(2,1)} %get-tuple-element.85.refs_0_, bf16[192,1024]{1,0:T(8,128)(2,1)} %get-tuple-element.86.refs_1_, ...), custom_call_target="tpu_custom_call" | custom-call | flops 20000000000 | bytes 60000000 | tf_op jit(solution)/shard_map/mlp_backward_0/pallas_call | solution.py:1166
  568.1 76.6 %attn_backward_0.1 = (f32[256,1536]{1,0:T(8,128)}, f32[8,1536]{1,0:T(8,128)}, bf16[8,192,1152]{2,1,0:T(8,128)(2,1)}, f32[192,2048]{1,0:T(8,128)}) custom-call(f32[256,1536]{1,0:T(8,128)} %get-tuple-element.122.refs_0_, f32[256,1536]{1,0:T(8,128)} %refs_1_.3, f32[16,1536]{1,0:T(8,128)} %get-tuple-element.91.refs_6_.refs_2_.refs_8_, ...), custom_call_target="tpu_custom_call" | custom-call | flops 20000000000 | bytes 60000000 | tf_op jit(solution)/shard_map/attn_backward_0/pallas_call | solution.py:1166
  644.8 0.0 copy-start.4
  644.8 52.6 %last_sums.1 = (f32[16,256]{1,0:T(8,128)}, f32[192,1152]{1,0:T(8,128)}) custom-call(f32[8,1536]{1,0:T(8,128)} %get-tuple-element.134.refs_0_, f32[8,1536]{1,0:T(8,128)} %get-tuple-element.135.refs_1_, f32[8,1536]{1,0:T(8,128)} %get-tuple-element.136.refs_2_, f32[8,1536]{1,0:T(8,128)} %get-tuple-element.137.refs_3_, ...), custom_call_target="tpu_custom_call" | custom-call | flops 20000000000 | bytes 60000000 | tf_op jit(solution)/shard_map/last_sums/pallas_call | solution.py:1166
  697.4 0.0 copy-start.2
  697.4 0.0 copy-start.3
  697.4 1.5 fusion.4
  698.9 0.0 copy-done.4
  698.9 2.0 fusion.2
  701.0 2.1 slice_bitcast_fusion
  703.0 0.0 copy-done.2
  703.0 0.0 copy-done.3
  703.0 0.0 copy-start
  703.0 1.7 fusion
  704.8 0.0 copy-start.1
  704.8 0.7 copy-done
  705.4 1.1 copy.47
  706.6 0.0 copy-done.1
  706.6 0.0 copy-start.6
  706.6 0.0 copy-start.5
  706.6 1.1 copy.48
  707.7 0.5 copy-done.6
  708.3 0.9 copy.49
  709.1 0.0 copy-done.5
  709.2 0.9 copy.50
Async XLA Ops:
  644.8 54.2 %copy-start.4 = (f32[192,1152]{1,0:T(8,128)S(1)}, f32[192,1152]{1,0:T(8,128)}, u32[]{:S(2)}) copy-start(f32[192,1152]{1,0:T(8,128)} %get-tuple-element.143) | copy-start | bytes 2654212
  697.4 5.6 copy-start.2
  697.4 5.6 copy-start.3
  703.0 2.4 copy-start
  704.8 1.8 copy-start.1
  706.6 1.7 copy-start.6
  706.6 2.6 copy-start.5

commit v4 on v3

--- a/solution.py
+++ b/solution.py
@@ -661,11 +661,17 @@
         each(n_dp, gather_gain)
         norm_rows(r.x, r.gains[2 * level : 2 * level + 1, :], r.full, group.me)
         gather.start()
+        weight_steps = weight_fetch.actions()[1:-1]
+        for step in weight_steps[:1]:
+            step()
+        ahead = Gather(group, r.ahead, r.a_send, r.a_recv)
+        r.ahead[group.me] = r.cotangent[...].astype(BF)
+        ahead.start()
         for name in ("gate0", "up0"):
             raw[name].wait()
         r.own0[...] = r.gate0[...].astype(BF)
         r.own1[...] = r.up0[...].astype(BF)
-        for step in weight_fetch.actions()[1:-1]:
+        for step in weight_steps[1:]:
             step()
         pump = Pump(tasks, plan)
         pump()
@@ -729,6 +735,9 @@
     ]
     for copy in copies:
         copy.start()
+    if first:
+        ahead.wait_chip()
+        ahead.forward()
     pump()
     kv_at = heads * PAD
     value_at = kv_at + heads // 2 * PAD
@@ -763,9 +772,13 @@
         copies.append(copy)
         compact[where, :] = nt(mixed[where, :], place).astype(BF)
         pump()
-    copy = pltpu.make_async_copy(compact, r.o_out, r.out_sems.at[6])
-    copy.start()
-    copies.append(copy)
+    copies.append(pltpu.make_async_copy(compact, r.o_out, r.out_sems.at[6]))
+    copies[-1].start()
+    if first:
+        ahead.wait_other()
+        copies.append(pltpu.make_async_copy(r.ahead, r.ahead_out, r.out_sems.at[7]))
+        copies[-1].start()
+        ahead.finish()
     for turn in range(2):
         left = compact[tile(scatter.rows_of(turn), 2 * rows), :]
 
@@ -909,7 +922,7 @@
     each(rows // 32, close)
 
 
-def mlp_backward_kernel(level, reduce_count, plan, r):
+def mlp_backward_kernel(level, reduce_count, plan, ready, r):
     rows, width = r.middle.shape
     units = r.hid.shape[1]
     n_dp = r.w_sems.shape[0]
@@ -932,8 +945,12 @@
     pump()
     for copy in weights[:1] + fetches + weights[1:]:
         copy.start()
-    r.full[group.me] = r.grad[...].astype(BF)
-    gather.start()
+    if ready:
+        whole = pltpu.make_async_copy(r.ahead_in, r.full, r.in_sems.at[3])
+        whole.start()
+    else:
+        r.full[group.me] = r.grad[...].astype(BF)
+        gather.start()
     for copy in weights[:1] + fetches[:2]:
         copy.wait()
 
@@ -953,14 +970,19 @@
 
         each(units // 256, unit)
 
-    gather.wait_chip()
-    inward(group.chip)
-    pump()
-    gather.forward()
-    pump()
-    gather.wait_other()
+    if ready:
+        whole.wait()
+    else:
+        gather.wait_chip()
+        inward(group.chip)
+        pump()
+        gather.forward()
+        pump()
+        gather.wait_other()
     weight_grads(r.full, hid, r.grads, slice(0, units))
     down.start()
+    if ready:
+        inward(group.chip)
     inward(1 - group.chip)
     for copy in weights[1:] + fetches[2:]:
         copy.wait()
@@ -989,13 +1011,14 @@
         scatter, r.grad, r.middle, r.gains[2 * level + 1 : 2 * level + 2, :], r.grad_out, r.dgain
     )
     pump.rest()
-    gather.finish()
+    if not ready:
+        gather.finish()
     scatter.finish()
     for copy in copies:
         copy.wait()
 
 
-def attn_backward_kernel(level, reduce_count, plan, r):
+def attn_backward_kernel(level, reduce_count, plan, final, r):
     rows, width = r.x.shape
     n_dp = r.w_sems.shape[0]
     depth = width // n_dp
@@ -1096,31 +1119,34 @@
     grads = r.grads
     weight_grads(r.a_full, grad_low, grads, slice(0, 2 * compact_width))
     weight_grads(r.full, compact, grads, slice(2 * compact_width, 3 * compact_width))
-    copy = pltpu.make_async_copy(grads, r.grads_out, r.out_sems.at[0])
-    copy.start()
+    if not final:
+        copy = pltpu.make_async_copy(grads, r.grads_out, r.out_sems.at[0])
+        copy.start()
     pump()
     scatter.wait()
     pump()
     close_back(scatter, r.grad, r.x, r.gains[2 * level : 2 * level + 1, :], r.grad_out, r.dgain)
+    if final:
+        attn = Reduce(line, grads, r.attn_total, *[getattr(r, f"attn{j}") for j in range(8)])
+        gains = gain_sums(line, group, r)
+        gains.start()
+        attn.start()
+        pump.rest()
+        for step in gains.actions()[1:] + attn.actions()[1:]:
+            step()
     pump.rest()
     gather.finish()
     scatter.finish()
-    copy.wait()
-
-
-def last_kernel(reduce_count, r):
+    if not final:
+        copy.wait()
+
+
+def gain_sums(line, group, r):
     n_dp, _, lanes = r.gain_blocks.shape
     width = r.rows.shape[1]
     depth = width // n_dp
-    line = Line(n_dp)
-    group = Group()
-    tasks = reduces_of(line, r, reduce_count)
-    gains = Reduce(line, r.gain_blocks, r.gain_total, *[getattr(r, f"gain{j}") for j in range(8)])
-    meet(group, line)
-    for task in tasks:
-        task.start()
-    for row in range(4):
-        r.rows[row : row + 1, :] = jnp.sum(getattr(r, f"dgain{row}")[...], axis=0, keepdims=True)
+    for row, part in enumerate((r.dgain, r.dgain1, r.dgain2, r.dgain3)):
+        r.rows[row : row + 1, :] = jnp.sum(part[...], axis=0, keepdims=True)
     r.rows[4:8, :] = jnp.zeros((4, width), F32)
     for turn, device in enumerate((group.core, group.other)):
         copy = group.remote(r.rows, r.others.at[turn], r.row_send.at[turn], r.row_recv.at[turn], device)
@@ -1133,12 +1159,7 @@
         r.gain_blocks[block] = nt(both, spread(block, depth, lanes, width)).astype(BF)
 
     each(n_dp, gain_rows)
-    gains.start()
-    for task in tasks:
-        for step in task.actions()[1:]:
-            step()
-    for step in gains.actions()[1:]:
-        step()
+    return Reduce(line, r.gain_blocks, r.gain_total, *[getattr(r, f"gain{j}") for j in range(8)])
 
 
 def shaped(shape, dtype):
@@ -1251,7 +1272,7 @@
         compact=vmem(length, place.shape[0]),
         bias=vmem(rows, length, dtype=F32),
         w_sems=dma(n_dp),
-        out_sems=dma(7),
+        out_sems=dma(8),
     )
     for turn, reach in enumerate(reaches(rows)):
         outs[f"p_out{turn}"] = (shaped((heads, rows, reach), BF), ANY)
@@ -1280,7 +1301,9 @@
             cosine=(shaped((length, PAD), F32), VM),
             sine=(shaped((length, PAD), F32), VM),
             marks=(shaped((8, PAD), jnp.int32), VM),
+            ahead_out=(shaped((4, rows, width), BF), ANY),
         )
+        scratch |= dict(ahead=vmem(4, rows, width), a_send=dma(5), a_recv=dma(5))
         scratch["gain_raw"] = vmem(GAIN_ROWS, 256, dtype=F32)
         scratch["gain_own"] = vmem(GAIN_ROWS, 256)
         scratch["gain_blocks"] = vmem(n_dp, GAIN_ROWS, 256)
@@ -1337,7 +1360,7 @@
     )
 
 
-def mlp_backward(level, which, grad, middle, gains, saved, wide, down, sums, plan):
+def mlp_backward(level, which, grad, middle, gains, saved, wide, down, sums, plan, ahead=None):
     rows, width = middle.shape
     n_dp, units, ins, scratch = mlp_refs(rows, width, wide, down[0])
     depth = width // n_dp
@@ -1356,19 +1379,21 @@
         m_full=vmem(4, rows, width),
         wide_grads=vmem(n_dp, depth, 2 * units),
         grads=vmem(n_dp, depth, units),
-        in_sems=dma(3),
+        in_sems=dma(4),
         out_sems=dma(3),
     )
+    if ahead is not None:
+        ins |= dict(ahead_in=(ahead, ANY))
     for j, each_of in enumerate(Reduce.scratch(n_dp, depth, units)):
         scratch[f"down{j}"] = each_of
     more = reduce_refs(sums)
     return launch(
-        functools.partial(mlp_backward_kernel, level, len(sums), plan),
+        functools.partial(mlp_backward_kernel, level, len(sums), plan, ahead is not None),
         which, f"mlp_backward_{level}", ins | more[0], outs | more[1], scratch | more[2],
     )
 
 
-def attn_backward(level, which, grad, states, gains, tables, place, saved, weights, sums, plan):
+def attn_backward(level, which, grad, states, gains, tables, place, saved, weights, sums, plan, dgains=()):
     cosine, sine, _ = tables
     pack, blocks = weights
     rows, width = states.shape
@@ -1384,7 +1409,6 @@
     outs = dict(
         grad_out=(shaped((rows, width), F32), VM),
         dgain=(shaped((8, width), F32), VM),
-        grads_out=(shaped((n_dp, depth, columns), BF), ANY),
     )
     scratch = comm_scratch(rows, width) | dict(
         held=vmem(width, columns),
@@ -1405,31 +1429,29 @@
     for turn, reach in enumerate(reaches(rows)):
         ins[f"p_in{turn}"] = (getattr(saved, f"p_out{turn}"), ANY)
         scratch[f"prob{turn}"] = vmem(heads, rows, reach)
+    if dgains:
+        ins |= {f"dgain{1 + i}": (dgain, VM) for i, dgain in enumerate(dgains)}
+        outs |= dict(
+            gain_total=(shaped((GAIN_ROWS, 256), F32), VM),
+            attn_total=(shaped((depth, columns), F32), VM),
+        )
+        scratch |= dict(
+            gain_blocks=vmem(n_dp, GAIN_ROWS, 256),
+            rows=vmem(8, width, dtype=F32),
+            others=vmem(2, 8, width, dtype=F32),
+            row_send=dma(2),
+            row_recv=dma(2),
+        )
+        for j, each_of in enumerate(Reduce.scratch(n_dp, GAIN_ROWS, 256)):
+            scratch[f"gain{j}"] = each_of
+        for j, each_of in enumerate(Reduce.scratch(n_dp, depth, columns)):
+            scratch[f"attn{j}"] = each_of
+    else:
+        outs |= dict(grads_out=(shaped((n_dp, depth, columns), BF), ANY))
     more = reduce_refs(sums)
     return launch(
-        functools.partial(attn_backward_kernel, level, len(sums), plan),
+        functools.partial(attn_backward_kernel, level, len(sums), plan, bool(dgains)),
         which, f"attn_backward_{level}", ins | more[0], outs | more[1], scratch | more[2],
-    )
-
-
-def last_sums(which, dgains, sums):
-    n_dp = sums[0].shape[0]
-    width = dgains[0].shape[1]
-    ins = {f"dgain{i}": (dgain, VM) for i, dgain in enumerate(dgains)}
-    outs = dict(gain_total=(shaped((GAIN_ROWS, 256), F32), VM))
-    scratch = dict(
-        gain_blocks=vmem(n_dp, GAIN_ROWS, 256),
-        rows=vmem(8, width, dtype=F32),
-        others=vmem(2, 8, width, dtype=F32),
-        row_send=dma(2),
-        row_recv=dma(2),
-    )
-    for j, each_of in enumerate(Reduce.scratch(n_dp, GAIN_ROWS, 256)):
-        scratch[f"gain{j}"] = each_of
-    more = reduce_refs(sums)
-    return launch(
-        functools.partial(last_kernel, len(sums)),
-        which, "last_sums", ins | more[0], outs | more[1], scratch | more[2],
     )
 
 
@@ -1451,7 +1473,7 @@
     one, two = rest[0:9], rest[9:18]
     heads = one[1].shape[1] // HEAD_DIM
     place, freqs = constants(heads)
-    raw = dict(documents=documents.reshape(-1, PAD), freqs=freqs)
+    raw = dict(documents=documents.reshape(-1, PAD), freqs=freqs, cotangent=cotangent)
     for level, w in enumerate((one, two)):
         raw[f"gain{2 * level}"] = w[0].reshape(1, -1)
         raw[f"gain{2 * level + 1}"] = w[5].reshape(1, -1)
@@ -1485,7 +1507,8 @@
     down2 = (down_pack[1], mlp2.blocks)
 
     back_mlp2 = mlp_backward(
-        1, 4, cotangent, attn2.middle, gains, mlp2, wide2, down2, [], [0, 0, 0, 0, 0, 1, 1, 1]
+        1, 4, cotangent, attn2.middle, gains, mlp2, wide2, down2, [], [0, 0, 1, 0, 1, 1, 0],
+        attn1.ahead_out,
     )
     back_attn2 = attn_backward(
         1, 5, back_mlp2.grad_out, mlp1.result, gains, tables, place, attn2, (attn_pack[1], attn2_blocks),
@@ -1498,18 +1521,14 @@
     back_attn1 = attn_backward(
         0, 7, back_mlp1.grad_out, states_in, gains, tables, place, attn1, (attn_pack[0], attn1.blocks),
         [back_mlp1.wide_out], [1, 0, 0, 1, 0, 0, 1, 0, 0, 1],
-    )
-    last = last_sums(
-        8,
-        [back_attn1.dgain, back_mlp1.dgain, back_attn2.dgain, back_mlp2.dgain],
-        [back_attn1.grads_out],
+        (back_mlp1.dgain, back_attn2.dgain, back_mlp2.dgain),
     )
     (wide_total2,) = totals(back_attn2, 1)
     (attn_total2,) = totals(back_mlp1, 1)
     (wide_total1,) = totals(back_attn1, 1)
-    (attn_total1,) = totals(last, 1)
+    attn_total1 = back_attn1.attn_total
     down_total1, down_total2 = back_mlp1.down_total, back_mlp2.down_total
-    gain_total = last.gain_total
+    gain_total = back_attn1.gain_total
     depth = down_total1.shape[0]
     bounds = [0]
     for w in one[1:4]:

time: 719 us -> 699 us (0.972)
  Pallas kernels: 697 us -> 676 us
    pallas_call x9 -> x8, Pallas kernels: 697 us -> 676 us  [launch(): pl.pallas_call(entry, out_shape=[shape for shape, _ in outs.values()], in...]
where the time goes in v4:
time: 699 us; the launch traced here: 689 us
  Pallas kernels  676 us (97%)
  local copies, waits for them, and re-layouts  12.6 us (2%)
    pallas_call x8, Pallas kernels, launch(): pl.pallas_call(entry, out_shape=[shape for shape, _ in outs.values()], in...  676 us

profile of v4, /device:TPU:28, one launch (start us, length us, event | category | flops | bytes accessed | tf_op | source)
XLA Modules:
  0.0 689.4 jit_solution(17292242626684548893)
XLA Ops:
  0.7 116.3 %attn_forward_0.1 = (f32[256,1536]{1,0:T(8,128)}, bf16[4,256,1536]{2,1,0:T(8,128)(2,1)}, bf16[1024,1024]{1,0:T(8,128)(2,1)}, bf16[1024,384]{1,0:T(8,128)(2,1)}, ...) custom-call(f32[256,1536]{1,0:T(8,128)} %refs_1_.3, ...), custom_call_target="tpu_custom_call" | custom-call | flops 20000000000 | bytes 60000000 | tf_op jit(solution)/shard_map/attn_forward_0/pallas_call | solution.py:1187
  117.0 82.3 %mlp_forward_0.1 = (f32[256,1536]{1,0:T(8,128)}, bf16[4,256,1536]{2,1,0:T(8,128)(2,1)}, bf16[1024,2048]{1,0:T(8,128)(2,1)}, bf16[1024,1024]{1,0:T(8,128)(2,1)}, ...) custom-call(bf16[192,1024]{1,0:T(8,128)(2,1)} %get-tuple-element.84.refs_0_, ...), custom_call_target="tpu_custom_call" | custom-call | flops 20000000000 | bytes 60000000 | tf_op jit(solution)/shard_map/mlp_forward_0/pallas_call | solution.py:1187
  199.3 72.4 %attn_forward_1.1 = (f32[256,1536]{1,0:T(8,128)}, bf16[4,256,1536]{2,1,0:T(8,128)(2,1)}, bf16[1024,1024]{1,0:T(8,128)(2,1)}, bf16[1024,384]{1,0:T(8,128)(2,1)}, ...) custom-call(f32[256,1536]{1,0:T(8,128)} %get-tuple-element.92.refs_0, ...), custom_call_target="tpu_custom_call" | custom-call | flops 20000000000 | bytes 60000000 | tf_op jit(solution)/shard_map/attn_forward_1/pallas_call | solution.py:1187
  271.6 63.2 %mlp_forward_1.1 = (f32[256,1536]{1,0:T(8,128)}, bf16[4,256,1536]{2,1,0:T(8,128)(2,1)}, bf16[1024,2048]{1,0:T(8,128)(2,1)}, bf16[1024,1024]{1,0:T(8,128)(2,1)}, bf16[8,192,1024]{2,1,0:T(8,128)(2,1)}) custom-call(bf16[192,1024]{1,0:T(8,128)(2,1)} %get-tuple-element.82.refs_0_, bf16[192,1024]{1,0:T(8,128)(2,1)} %get-tuple-element.83.refs_8_.refs_1_, ...), custom_call_target="tpu_custom_call" | custom-call | flops 20000000000 | bytes 60000000 | tf_op jit(solution)/shard_map/mlp_forward_1/pallas_call | solution.py:1187
  334.8 59.8 %mlp_backward_1.1 = (f32[256,1536]{1,0:T(8,128)}, f32[8,1536]{1,0:T(8,128)}, bf16[8,192,2048]{2,1,0:T(8,128)(2,1)}, f32[192,1024]{1,0:T(8,128)}) custom-call(bf16[192,1024]{1,0:T(8,128)(2,1)} %get-tuple-element.82.refs_0_, bf16[192,1024]{1,0:T(8,128)(2,1)} %get-tuple-element.83.refs_8_.refs_1_, bf16[8,192,1024]{2,1,0:T(8,128)(2,1)} %get-tuple-element.98.refs_2_, ...), custom_call_target="tpu_custom_call" | custom-call | flops 20000000000 | bytes 60000000 | tf_op jit(solution)/shard_map/mlp_backward_1/pallas_call | solution.py:1187
  394.6 79.5 %attn_backward_1.1 = (f32[256,1536]{1,0:T(8,128)}, f32[8,1536]{1,0:T(8,128)}, bf16[8,192,1152]{2,1,0:T(8,128)(2,1)}, f32[192,2048]{1,0:T(8,128)}) custom-call(f32[256,1536]{1,0:T(8,128)} %get-tuple-element.108.refs_0_, f32[256,1536]{1,0:T(8,128)} %get-tuple-element.92.refs_0_.refs_1_, f32[16,1536]{1,0:T(8,128)} %get-tuple-element.90.refs_6_.refs_2_.refs_8_, ...), custom_call_target="tpu_custom_call" | custom-call | flops 20000000000 | bytes 60000000 | tf_op jit(solution)/shard_map/attn_backward_1/pallas_call | solution.py:1187
  474.1 79.2 %mlp_backward_0.1 = (f32[256,1536]{1,0:T(8,128)}, f32[8,1536]{1,0:T(8,128)}, bf16[8,192,2048]{2,1,0:T(8,128)(2,1)}, f32[192,1024]{1,0:T(8,128)}, f32[192,1152]{1,0:T(8,128)}) custom-call(bf16[192,1024]{1,0:T(8,128)(2,1)} %get-tuple-element.84.refs_0_, bf16[192,1024]{1,0:T(8,128)(2,1)} %get-tuple-element.85.refs_1_, ...), custom_call_target="tpu_custom_call" | custom-call | flops 20000000000 | bytes 60000000 | tf_op jit(solution)/shard_map/mlp_backward_0/pallas_call | solution.py:1187
  553.3 0.0 copy-start.4
  553.3 123.2 %attn_backward_0.1 = (f32[256,1536]{1,0:T(8,128)}, f32[8,1536]{1,0:T(8,128)}, f32[16,256]{1,0:T(8,128)}, f32[192,1152]{1,0:T(8,128)}, f32[192,2048]{1,0:T(8,128)}) custom-call(f32[256,1536]{1,0:T(8,128)} %get-tuple-element.122.refs_0_, f32[256,1536]{1,0:T(8,128)} %refs_1_.3, f32[16,1536]{1,0:T(8,128)} %get-tuple-element.90.refs_6_.refs_2_.refs_8_, ...), custom_call_target="tpu_custom_call" | custom-call | flops 20000000000 | bytes 60000000 | tf_op jit(solution)/shard_map/attn_backward_0/pallas_call | solution.py:1187
  676.5 0.0 copy-start.2
  676.5 0.0 copy-start.3
  676.5 1.5 fusion.4
  678.0 0.0 copy-done.4
  678.0 2.0 fusion.2
  680.1 2.1 slice_bitcast_fusion
  682.1 0.0 copy-done.2
  682.1 0.0 copy-done.3
  682.1 0.0 copy-start
  682.1 1.7 fusion
  683.9 0.0 copy-start.1
  683.9 0.7 copy-done
  684.5 1.1 copy.47
  685.7 0.0 copy-done.1
  685.7 0.0 copy-start.6
  685.7 0.0 copy-start.5
  685.7 1.1 copy.48
  686.8 0.5 copy-done.6
  687.4 0.9 copy.49
  688.3 0.0 copy-done.5
  688.3 0.9 copy.50
Async XLA Ops:
  553.3 124.7 %copy-start.4 = (f32[192,1152]{1,0:T(8,128)S(1)}, f32[192,1152]{1,0:T(8,128)}, u32[]{:S(2)}) copy-start(f32[192,1152]{1,0:T(8,128)} %get-tuple-element.141) | copy-start | bytes 2654212
  676.5 5.6 copy-start.2
  676.5 5.6 copy-start.3
  682.1 2.4 copy-start
  683.9 1.8 copy-start.1
  685.7 1.7 copy-start.6
  685.7 2.6 copy-start.5

commit v5 on v4

--- a/solution.py
+++ b/solution.py
@@ -27,6 +27,7 @@
 MESH = pl.DeviceIdType.MESH
 ANY = pl.BlockSpec(memory_space=pl.ANY)
 VM = pl.BlockSpec(memory_space=pltpu.VMEM)
+SELF = None
 
 
 def nn(left, right):
@@ -506,6 +507,11 @@
     def wait(self):
         for copy in self.copies:
             copy.wait()
+
+
+def start_coming(r):
+    for copy in r.coming.values():
+        copy.start()
 
 
 class Pump:
@@ -639,6 +645,8 @@
             r.gain_raw[row : row + 1, 0:depth] = getattr(r, f"gain{row}")[...]
         r.gain_own[...] = r.gain_raw[...].astype(BF)
         pack_attn(r.raw_query0, r.raw_key0, r.raw_value0, r.raw_output0, r.own)
+        start_coming(r)
+        leave(r, "own")
         gain_fetch = Fetch(line, r.gain_own, r.gain_blocks, r.gain_send, r.gain_recv)
         weight_fetch = Fetch(line, r.own, r.blocks, r.weight_send, r.weight_recv)
         gain_fetch.start()
@@ -659,18 +667,21 @@
                 r.gains[...] += nn(r.gain_blocks[block], chosen)
 
         each(n_dp, gather_gain)
+        come(r, "x")
         norm_rows(r.x, r.gains[2 * level : 2 * level + 1, :], r.full, group.me)
         gather.start()
         weight_steps = weight_fetch.actions()[1:-1]
         for step in weight_steps[:1]:
             step()
         ahead = Gather(group, r.ahead, r.a_send, r.a_recv)
+        come(r, "cotangent")
         r.ahead[group.me] = r.cotangent[...].astype(BF)
         ahead.start()
         for name in ("gate0", "up0"):
             raw[name].wait()
         r.own0[...] = r.gate0[...].astype(BF)
         r.own1[...] = r.up0[...].astype(BF)
+        leave(r, "own0", "own1")
         for step in weight_steps[1:]:
             step()
         pump = Pump(tasks, plan)
@@ -683,14 +694,18 @@
         r.down_pack1[...] = r.down1[...].astype(BF)
         r.gate_pack1[...] = r.gate1[...].astype(BF)
         r.up_pack1[...] = r.up1[...].astype(BF)
+        leave(r, "down_pack0", "down_pack1", "attn_pack1", "gate_pack1", "up_pack1", "cosine", "sine")
+        come(r, "place")
         weight_fetch.finish()
         weights.start()
     else:
         weights.start()
         pump = Pump(tasks, plan)
         pump()
+        start_coming(r)
         norm_rows(r.x, r.gains[2 * level : 2 * level + 1, :], r.full, group.me)
         gather.start()
+        come(r, "place", "cosine", "sine")
     weights.wait()
     place = r.place[...]
     heads = place.shape[1] // PAD
@@ -794,6 +809,7 @@
     scatter.wait()
     pump()
     add_rows(scatter, r.x, r.middle)
+    leave(r, "middle")
     pump.rest()
     gather.finish()
     scatter.finish()
@@ -882,6 +898,7 @@
     scatter.wait()
     pump()
     add_rows(scatter, r.middle, r.result)
+    leave(r, "result")
     pump.rest()
     gather.finish()
     scatter.finish()
@@ -945,6 +962,7 @@
     pump()
     for copy in weights[:1] + fetches + weights[1:]:
         copy.start()
+    start_coming(r)
     if ready:
         whole = pltpu.make_async_copy(r.ahead_in, r.full, r.in_sems.at[3])
         whole.start()
@@ -1007,9 +1025,11 @@
     copies[0].start()
     scatter.wait()
     pump()
+    come(r, *r.coming)
     close_back(
         scatter, r.grad, r.middle, r.gains[2 * level + 1 : 2 * level + 2, :], r.grad_out, r.dgain
     )
+    leave(r, "grad_out")
     pump.rest()
     if not ready:
         gather.finish()
@@ -1037,17 +1057,19 @@
         for turn in range(4)
     ]
     meet(*((group, line) if tasks else (group,)))
+    pump = Pump(tasks, plan)
+    pump()
     weights.start()
     for copy in fetches:
         copy.start()
-    pump = Pump(tasks, plan)
-    pump()
+    start_coming(r)
     r.full[group.me] = r.grad[...].astype(BF)
     gather.start()
     pump()
     weights.wait()
     for copy in fetches:
         copy.wait()
+    come(r, *r.coming)
     place = r.place[...]
     heads = place.shape[1] // PAD
     compact_width, head_width = place.shape
@@ -1126,6 +1148,7 @@
     scatter.wait()
     pump()
     close_back(scatter, r.grad, r.x, r.gains[2 * level : 2 * level + 1, :], r.grad_out, r.dgain)
+    leave(r, "grad_out")
     if final:
         attn = Reduce(line, grads, r.attn_total, *[getattr(r, f"attn{j}") for j in range(8)])
         gains = gain_sums(line, group, r)
@@ -1178,17 +1201,43 @@
     return [min((turn + 1) * rows + PAD, 4 * rows) for turn in range(4)]
 
 
+def come(r, *names):
+    for name in names:
+        r.coming[name].wait()
+
+
+def leave(r, *names):
+    for name in names:
+        r.leaving[name].start()
+
+
 def launch(kernel, which, name, ins, outs, scratch):
-    names = list(ins) + list(outs) + list(scratch)
+    late = [each_of for each_of, (_, spec) in ins.items() if spec is SELF]
+    early = [each_of for each_of, (_, spec) in outs.items() if spec is SELF]
+    names = [n + "_" * (n in late) for n in ins] + [n + "_" * (n in early) for n in outs]
+    scratch = scratch | {n: vmem(*ins[n][0].shape, dtype=ins[n][0].dtype) for n in late}
+    scratch |= {n: vmem(*outs[n][0].shape, dtype=outs[n][0].dtype) for n in early}
+    scratch["own_sems"] = dma(len(late) + len(early) + 1)
+    names += list(scratch)
 
     def entry(*refs):
-        kernel(types.SimpleNamespace(**dict(zip(names, refs))))
+        r = types.SimpleNamespace(**dict(zip(names, refs)))
+        sems = iter(range(len(late) + len(early)))
+        r.coming = {
+            n: pltpu.make_async_copy(getattr(r, n + "_"), getattr(r, n), r.own_sems.at[next(sems)]) for n in late
+        }
+        r.leaving = {
+            n: pltpu.make_async_copy(getattr(r, n), getattr(r, n + "_"), r.own_sems.at[next(sems)]) for n in early
+        }
+        kernel(r)
+        for copy in r.leaving.values():
+            copy.wait()
 
     results = pl.pallas_call(
         entry,
         out_shape=[shape for shape, _ in outs.values()],
-        in_specs=[spec for _, spec in ins.values()],
-        out_specs=[spec for _, spec in outs.values()],
+        in_specs=[ANY if spec is SELF else spec for _, spec in ins.values()],
+        out_specs=[ANY if spec is SELF else spec for _, spec in outs.values()],
         scratch_shapes=list(scratch.values()),
         compiler_params=pltpu.CompilerParams(
             collective_id=which, has_side_effects=True, vmem_limit_bytes=LIMIT
@@ -1257,9 +1306,9 @@
     n_dp = width // depth
     heads = place.shape[1] // PAD
     length = 4 * rows
-    ins = dict(x=(states, VM), place=(place, VM))
+    ins = dict(x=(states, SELF if first else VM), place=(place, SELF))
     outs = dict(
-        middle=(shaped((rows, width), F32), VM),
+        middle=(shaped((rows, width), F32), SELF),
         a_out=(shaped((4, rows, width), BF), ANY),
         qkv_out=(shaped((length, 2 * heads * PAD), BF), ANY),
         o_out=(shaped((length, place.shape[0]), BF), ANY),
@@ -1282,24 +1331,24 @@
         now = ("raw_query0", "raw_key0", "raw_value0", "raw_output0")
         for name, array in raw.items():
             late = name.startswith("raw_") and name not in now
-            ins[name] = (array, ANY if late else VM)
+            ins[name] = (array, ANY if late else SELF if array.shape == states.shape else VM)
             if late:
                 scratch[name[4:]] = vmem(*array.shape, dtype=F32)
         outs |= dict(
             gains=(shaped((GAIN_ROWS, width), F32), VM),
             blocks=(blocks_of(pack, n_dp), ANY),
-            own=(pack, VM),
-            own0=(shaped((depth, units), BF), VM),
-            own1=(shaped((depth, units), BF), VM),
+            own=(pack, SELF),
+            own0=(shaped((depth, units), BF), SELF),
+            own1=(shaped((depth, units), BF), SELF),
             blocks0=(shaped((n_dp, depth, units), BF), ANY),
             blocks1=(shaped((n_dp, depth, units), BF), ANY),
-            down_pack0=(shaped((depth, units), BF), VM),
-            attn_pack1=(pack, VM),
-            gate_pack1=(shaped((depth, units), BF), VM),
-            up_pack1=(shaped((depth, units), BF), VM),
-            down_pack1=(shaped((depth, units), BF), VM),
-            cosine=(shaped((length, PAD), F32), VM),
-            sine=(shaped((length, PAD), F32), VM),
+            down_pack0=(shaped((depth, units), BF), SELF),
+            attn_pack1=(pack, SELF),
+            gate_pack1=(shaped((depth, units), BF), SELF),
+            up_pack1=(shaped((depth, units), BF), SELF),
+            down_pack1=(shaped((depth, units), BF), SELF),
+            cosine=(shaped((length, PAD), F32), SELF),
+            sine=(shaped((length, PAD), F32), SELF),
             marks=(shaped((8, PAD), jnp.int32), VM),
             ahead_out=(shaped((4, rows, width), BF), ANY),
         )
@@ -1314,7 +1363,7 @@
     else:
         cosine, sine, marks = tables
         ins |= dict(
-            gains=(gains, VM), cosine=(cosine, VM), sine=(sine, VM), marks=(marks, VM), own=(pack, ANY), blocks=(blocks, ANY)
+            gains=(gains, VM), cosine=(cosine, SELF), sine=(sine, SELF), marks=(marks, VM), own=(pack, ANY), blocks=(blocks, ANY)
         )
         more = fetch_refs(packs, n_dp)
     return launch(
@@ -1345,7 +1394,7 @@
     n_dp, units, ins, scratch = mlp_refs(rows, width, wide, down_own)
     ins |= dict(middle=(middle, VM), gains=(gains, VM))
     outs = dict(
-        result=(shaped((rows, width), F32), VM),
+        result=(shaped((rows, width), F32), SELF),
         m_out=(shaped((4, rows, width), BF), ANY),
         gu_out=(shaped((4 * rows, 2 * units), BF), ANY),
         hid_out=(shaped((4 * rows, units), BF), ANY),
@@ -1366,11 +1415,11 @@
     depth = width // n_dp
     ins |= dict(
         blocks=(down[1], ANY),
-        grad=(grad, VM), middle=(middle, VM), gains=(gains, VM),
+        grad=(grad, VM if ahead is None else SELF), middle=(middle, SELF), gains=(gains, VM),
         m_in=(saved.m_out, ANY), gu_in=(saved.gu_out, ANY), hid_in=(saved.hid_out, ANY),
     )
     outs = dict(
-        grad_out=(shaped((rows, width), F32), VM),
+        grad_out=(shaped((rows, width), F32), SELF),
         dgain=(shaped((8, width), F32), VM),
         wide_out=(shaped((n_dp, depth, 2 * units), BF), ANY),
         down_total=(shaped((depth, units), F32), VM),
@@ -1402,12 +1451,12 @@
     heads = place.shape[1] // PAD
     length = 4 * rows
     ins = dict(
-        grad=(grad, VM), x=(states, VM), gains=(gains, VM), cosine=(cosine, VM), sine=(sine, VM), place=(place, VM),
+        grad=(grad, VM), x=(states, SELF), gains=(gains, VM), cosine=(cosine, SELF), sine=(sine, SELF), place=(place, SELF),
         own=(pack, ANY), blocks=(blocks, ANY),
         a_in=(saved.a_out, ANY), qkv_in=(saved.qkv_out, ANY), o_in=(saved.o_out, ANY),
     )
     outs = dict(
-        grad_out=(shaped((rows, width), F32), VM),
+        grad_out=(shaped((rows, width), F32), SELF),
         dgain=(shaped((8, width), F32), VM),
     )
     scratch = comm_scratch(rows, width) | dict(

time: 699 us -> 687 us (0.983)
  Pallas kernels: 676 us -> 665 us
    pallas_call x8, Pallas kernels: 676 us -> 665 us  [launch(): pl.pallas_call(entry, out_shape=[shape for shape, _ in outs.values()], in...]
where the time goes in v5:
time: 687 us; the launch traced here: 678 us
  Pallas kernels  665 us (97%)
  local copies, waits for them, and re-layouts  12.6 us (2%)
    pallas_call x8, Pallas kernels, launch(): pl.pallas_call(entry, out_shape=[shape for shape, _ in outs.values()], in...  665 us

profile of v5, /device:TPU:28, one launch (start us, length us, event | category | flops | bytes accessed | tf_op | source)
XLA Modules:
  0.0 678.1 jit_solution(12824415391753223820)
XLA Ops:
  0.7 113.6 %attn_forward_0.1 = (f32[256,1536]{1,0:T(8,128)}, bf16[4,256,1536]{2,1,0:T(8,128)(2,1)}, bf16[1024,1024]{1,0:T(8,128)(2,1)}, bf16[1024,384]{1,0:T(8,128)(2,1)}, ...) custom-call(f32[256,1536]{1,0:T(8,128)} %refs_1_.3, ...), custom_call_target="tpu_custom_call" | custom-call | flops 20000000000 | bytes 60000000 | tf_op jit(solution)/shard_map/attn_forward_0/pallas_call | solution.py:1236
  114.3 81.7 %mlp_forward_0.1 = (f32[256,1536]{1,0:T(8,128)}, bf16[4,256,1536]{2,1,0:T(8,128)(2,1)}, bf16[1024,2048]{1,0:T(8,128)(2,1)}, bf16[1024,1024]{1,0:T(8,128)(2,1)}, ...) custom-call(bf16[192,1024]{1,0:T(8,128)(2,1)} %get-tuple-element.84.refs_0_, ...), custom_call_target="tpu_custom_call" | custom-call | flops 20000000000 | bytes 60000000 | tf_op jit(solution)/shard_map/mlp_forward_0/pallas_call | solution.py:1236
  196.0 70.5 %attn_forward_1.1 = (f32[256,1536]{1,0:T(8,128)}, bf16[4,256,1536]{2,1,0:T(8,128)(2,1)}, bf16[1024,1024]{1,0:T(8,128)(2,1)}, bf16[1024,384]{1,0:T(8,128)(2,1)}, ...) custom-call(f32[256,1536]{1,0:T(8,128)} %get-tuple-element.92.refs_0, ...), custom_call_target="tpu_custom_call" | custom-call | flops 20000000000 | bytes 60000000 | tf_op jit(solution)/shard_map/attn_forward_1/pallas_call | solution.py:1236
  266.5 63.4 %mlp_forward_1.1 = (f32[256,1536]{1,0:T(8,128)}, bf16[4,256,1536]{2,1,0:T(8,128)(2,1)}, bf16[1024,2048]{1,0:T(8,128)(2,1)}, bf16[1024,1024]{1,0:T(8,128)(2,1)}, bf16[8,192,1024]{2,1,0:T(8,128)(2,1)}) custom-call(bf16[192,1024]{1,0:T(8,128)(2,1)} %get-tuple-element.82.refs_0_, bf16[192,1024]{1,0:T(8,128)(2,1)} %get-tuple-element.83.refs_8_.refs_1_, ...), custom_call_target="tpu_custom_call" | custom-call | flops 20000000000 | bytes 60000000 | tf_op jit(solution)/shard_map/mlp_forward_1/pallas_call | solution.py:1236
  330.0 58.8 %mlp_backward_1.1 = (f32[256,1536]{1,0:T(8,128)}, f32[8,1536]{1,0:T(8,128)}, bf16[8,192,2048]{2,1,0:T(8,128)(2,1)}, f32[192,1024]{1,0:T(8,128)}) custom-call(bf16[192,1024]{1,0:T(8,128)(2,1)} %get-tuple-element.82.refs_0_, bf16[192,1024]{1,0:T(8,128)(2,1)} %get-tuple-element.83.refs_8_.refs_1_, bf16[8,192,1024]{2,1,0:T(8,128)(2,1)} %get-tuple-element.98.refs_2_, ...), custom_call_target="tpu_custom_call" | custom-call | flops 20000000000 | bytes 60000000 | tf_op jit(solution)/shard_map/mlp_backward_1/pallas_call | solution.py:1236
  388.8 76.9 %attn_backward_1.1 = (f32[256,1536]{1,0:T(8,128)}, f32[8,1536]{1,0:T(8,128)}, bf16[8,192,1152]{2,1,0:T(8,128)(2,1)}, f32[192,2048]{1,0:T(8,128)}) custom-call(f32[256,1536]{1,0:T(8,128)} %get-tuple-element.108.refs_0_, f32[256,1536]{1,0:T(8,128)} %get-tuple-element.92.refs_0_.refs_1_, f32[16,1536]{1,0:T(8,128)} %get-tuple-element.90.refs_6_.refs_2_.refs_8_, ...), custom_call_target="tpu_custom_call" | custom-call | flops 20000000000 | bytes 60000000 | tf_op jit(solution)/shard_map/attn_backward_1/pallas_call | solution.py:1236
  465.7 83.4 %mlp_backward_0.1 = (f32[256,1536]{1,0:T(8,128)}, f32[8,1536]{1,0:T(8,128)}, bf16[8,192,2048]{2,1,0:T(8,128)(2,1)}, f32[192,1024]{1,0:T(8,128)}, f32[192,1152]{1,0:T(8,128)}) custom-call(bf16[192,1024]{1,0:T(8,128)(2,1)} %get-tuple-element.84.refs_0_, bf16[192,1024]{1,0:T(8,128)(2,1)} %get-tuple-element.85.refs_1_, ...), custom_call_target="tpu_custom_call" | custom-call | flops 20000000000 | bytes 60000000 | tf_op jit(solution)/shard_map/mlp_backward_0/pallas_call | solution.py:1236
  549.1 0.0 copy-start.4
  549.1 116.1 %attn_backward_0.1 = (f32[256,1536]{1,0:T(8,128)}, f32[8,1536]{1,0:T(8,128)}, f32[16,256]{1,0:T(8,128)}, f32[192,1152]{1,0:T(8,128)}, f32[192,2048]{1,0:T(8,128)}) custom-call(f32[256,1536]{1,0:T(8,128)} %get-tuple-element.122.refs_0_, f32[256,1536]{1,0:T(8,128)} %refs_1_.3, f32[16,1536]{1,0:T(8,128)} %get-tuple-element.90.refs_6_.refs_2_.refs_8_, ...), custom_call_target="tpu_custom_call" | custom-call | flops 20000000000 | bytes 60000000 | tf_op jit(solution)/shard_map/attn_backward_0/pallas_call | solution.py:1236
  665.3 0.0 copy-start.2
  665.3 0.0 copy-start.3
  665.3 1.5 fusion.4
  666.8 0.0 copy-done.4
  666.8 2.0 fusion.2
  668.8 2.1 slice_bitcast_fusion
  670.9 0.0 copy-done.2
  670.9 0.0 copy-done.3
  670.9 0.0 copy-start
  670.9 1.7 fusion
  672.6 0.0 copy-start.1
  672.6 0.7 copy-done
  673.3 1.1 copy.47
  674.5 0.0 copy-done.1
  674.5 0.0 copy-start.6
  674.5 0.0 copy-start.5
  674.5 1.1 copy.48
  675.6 0.5 copy-done.6
  676.1 0.9 copy.49
  677.0 0.0 copy-done.5
  677.0 0.9 copy.50
Async XLA Ops:
  549.1 117.7 %copy-start.4 = (f32[192,1152]{1,0:T(8,128)S(1)}, f32[192,1152]{1,0:T(8,128)}, u32[]{:S(2)}) copy-start(f32[192,1152]{1,0:T(8,128)} %get-tuple-element.141) | copy-start | bytes 2654212
  665.3 5.6 copy-start.2
  665.3 5.6 copy-start.3
  670.9 2.4 copy-start
  672.6 1.8 copy-start.1
  674.5 1.7 copy-start.6
  674.5 2.6 copy-start.5

commit v6 on v5

--- a/solution.py
+++ b/solution.py
@@ -694,7 +694,7 @@
         r.down_pack1[...] = r.down1[...].astype(BF)
         r.gate_pack1[...] = r.gate1[...].astype(BF)
         r.up_pack1[...] = r.up1[...].astype(BF)
-        leave(r, "down_pack0", "down_pack1", "attn_pack1", "gate_pack1", "up_pack1", "cosine", "sine")
+        leave(r, *list(r.leaving)[4:])
         come(r, "place")
         weight_fetch.finish()
         weights.start()
@@ -1211,7 +1211,7 @@
         r.leaving[name].start()
 
 
-def launch(kernel, which, name, ins, outs, scratch):
+def launch(kernel, which, ins, outs, scratch):
     late = [each_of for each_of, (_, spec) in ins.items() if spec is SELF]
     early = [each_of for each_of, (_, spec) in outs.items() if spec is SELF]
     names = [n + "_" * (n in late) for n in ins] + [n + "_" * (n in early) for n in outs]
@@ -1240,12 +1240,12 @@
         out_specs=[ANY if spec is SELF else spec for _, spec in outs.values()],
         scratch_shapes=list(scratch.values()),
         compiler_params=pltpu.CompilerParams(
-            collective_id=which, has_side_effects=True, vmem_limit_bytes=LIMIT
+            collective_id=which, has_side_effects=which is not None, vmem_limit_bytes=LIMIT
         ),
         cost_estimate=pl.CostEstimate(
             flops=20_000_000_000, bytes_accessed=60_000_000, transcendentals=0
         ),
-        name=name,
+        name=kernel.func.__name__,
     )(*[array for array, _ in ins.values()])
     return types.SimpleNamespace(**dict(zip(outs, results)))
 
@@ -1368,7 +1368,7 @@
         more = fetch_refs(packs, n_dp)
     return launch(
         functools.partial(attn_forward_kernel, first, level, 2 if first else len(packs), plan),
-        which, f"attn_forward_{level}", ins | more[0], outs | more[1], scratch | more[2],
+        which, ins | more[0], outs | more[1], scratch | more[2],
     )
 
 
@@ -1405,7 +1405,7 @@
     more = fetch_refs(packs, n_dp)
     return launch(
         functools.partial(mlp_forward_kernel, level, len(packs), plan),
-        which, f"mlp_forward_{level}", ins | more[0], outs | more[1], scratch | more[2],
+        which, ins | more[0], outs | more[1], scratch | more[2],
     )
 
 
@@ -1438,7 +1438,7 @@
     more = reduce_refs(sums)
     return launch(
         functools.partial(mlp_backward_kernel, level, len(sums), plan, ahead is not None),
-        which, f"mlp_backward_{level}", ins | more[0], outs | more[1], scratch | more[2],
+        which, ins | more[0], outs | more[1], scratch | more[2],
     )
 
 
@@ -1500,8 +1500,59 @@
     more = reduce_refs(sums)
     return launch(
         functools.partial(attn_backward_kernel, level, len(sums), plan, bool(dgains)),
-        which, f"attn_backward_{level}", ins | more[0], outs | more[1], scratch | more[2],
-    )
+        which, ins | more[0], outs | more[1], scratch | more[2],
+    )
+
+
+def unpack_kernel(bounds, r):
+    start_coming(r)
+    copies = []
+
+    def put(source, target):
+        copies.append(pltpu.make_async_copy(source, target, r.put_sems.at[len(copies)]))
+        copies[-1].start()
+
+    low, middle, high, end = bounds
+    for level in (1, 0):
+        wide, down, attn, apart = (getattr(r, f"{n}{level}") for n in ("wide", "down", "attn", "apart"))
+        query, key, value, output, gate, up, lower = (getattr(r, f"out{level}_{i}") for i in range(7))
+        units = wide.shape[1] // 2
+        come(r, f"wide{level}")
+        put(wide.at[:, pl.ds(0, units)], gate)
+        put(wide.at[:, pl.ds(units, units)], up)
+        come(r, f"down{level}")
+        put(down, lower)
+        come(r, f"attn{level}")
+        put(attn.at[:, pl.ds(0, low)], query)
+        put(attn.at[:, pl.ds(high, end - high)], output)
+        apart[0] = attn[:, low:middle]
+        apart[1] = attn[:, middle:high]
+        put(apart.at[0], key)
+        put(apart.at[1], value)
+    for name in ("x", "y"):
+        come(r, name)
+        put(getattr(r, name), getattr(r, name + "out"))
+    for copy in copies:
+        copy.wait()
+
+
+def unpack(states, grad, bounds, attn, wide, down):
+    ins = dict(x=(states, SELF), y=(grad, SELF))
+    outs = dict(xout=(shaped(states.shape, F32), ANY), yout=(shaped(grad.shape, F32), ANY))
+    scratch = dict(put_sems=dma(16))
+    depth, units = down[0].shape
+    low, middle, high, end = bounds
+    for level in range(2):
+        ins |= {
+            f"wide{level}": (wide[level], SELF),
+            f"down{level}": (down[level], SELF),
+            f"attn{level}": (attn[level], SELF),
+        }
+        widths = (low, middle - low, high - middle, end - high, units, units, units)
+        outs |= {f"out{level}_{i}": (shaped((depth, each_of), F32), ANY) for i, each_of in enumerate(widths)}
+        scratch[f"apart{level}"] = vmem(2, depth, middle - low, dtype=F32)
+    out = launch(functools.partial(unpack_kernel, bounds), None, ins, outs, scratch)
+    return [out.xout, out.yout] + [[getattr(out, f"out{level}_{i}") for i in range(7)] for level in range(2)]
 
 
 def constants(heads):
@@ -1582,16 +1633,15 @@
     bounds = [0]
     for w in one[1:4]:
         bounds.append(bounds[-1] + w.shape[1])
-    units = one[6].shape[1]
-    outs = [mlp2.result, back_attn1.grad_out]
-    for level, (attn_total, wide_total, down_total) in enumerate(
-        ((attn_total1, wide_total1, down_total1), (attn_total2, wide_total2, down_total2))
-    ):
-        outs.append(gain_total[2 * level, 0:depth])
-        outs += [attn_total[:, low:high] for low, high in zip(bounds, bounds[1:])]
-        outs.append(attn_total[:, bounds[-1] :].T)
-        outs.append(gain_total[2 * level + 1, 0:depth])
-        outs += [wide_total[:, 0:units], wide_total[:, units:], down_total.T]
+    bounds = (*bounds[1:], attn_total1.shape[1])
+    states, grad, *layers = unpack(
+        mlp2.result, back_attn1.grad_out, bounds,
+        (attn_total1, attn_total2), (wide_total1, wide_total2), (down_total1, down_total2),
+    )
+    outs = [states, grad]
+    for level, (query, key, value, output, gate, up, down) in enumerate(layers):
+        outs += [gain_total[2 * level, 0:depth], query, key, value, output.T]
+        outs += [gain_total[2 * level + 1, 0:depth], gate, up, down.T]
     return tuple(outs)
 
 

time: 687 us -> 685 us (level)
  local copies, waits for them, and re-layouts: 12.6 us -> 1.43 us
  Pallas kernels: 665 us -> 672 us
    pallas_call x8 -> x9, Pallas kernels: 665 us -> 672 us  [launch(): pl.pallas_call(entry, out_shape=[shape for shape, _ in outs.values()], in...]
where the time goes in v6:
time: 685 us; the launch traced here: 675 us
  Pallas kernels  672 us (98%)
    pallas_call x9, Pallas kernels, launch(): pl.pallas_call(entry, out_shape=[shape for shape, _ in outs.values()], in...  672 us

profile of v6, /device:TPU:28, one launch (start us, length us, event | category | flops | bytes accessed | tf_op | source)
XLA Modules:
  0.0 674.8 jit_solution(6952938187700625283)
XLA Ops:
  0.7 113.6 %attn_forward_kernel.2 = (f32[256,1536]{1,0:T(8,128)}, bf16[4,256,1536]{2,1,0:T(8,128)(2,1)}, bf16[1024,1024]{1,0:T(8,128)(2,1)}, bf16[1024,384]{1,0:T(8,128)(2,...) custom-call(f32[256,1536]{1,0:T(8,128)} %refs_1_.3, ...), custom_call_target="tpu_custom_call" | custom-call | flops 20000000000 | bytes 60000000 | tf_op jit(solution)/shard_map/attn_forward_kernel/pallas_call | solution.py:1236
  114.3 81.8 %mlp_forward_kernel.2 = (f32[256,1536]{1,0:T(8,128)}, bf16[4,256,1536]{2,1,0:T(8,128)(2,1)}, bf16[1024,2048]{1,0:T(8,128)(2,1)}, bf16[1024,1024]{1,0:T(8,128)(2,...) custom-call(bf16[192,1024]{1,0:T(8,128)(2,1)} %get-tuple-element.100.refs_0_, ...), custom_call_target="tpu_custom_call" | custom-call | flops 20000000000 | bytes 60000000 | tf_op jit(solution)/shard_map/mlp_forward_kernel/pallas_call | solution.py:1236
  196.1 70.4 %attn_forward_kernel.3 = (f32[256,1536]{1,0:T(8,128)}, bf16[4,256,1536]{2,1,0:T(8,128)(2,1)}, bf16[1024,1024]{1,0:T(8,128)(2,1)}, bf16[1024,384]{1,0:T(8,128)(2,...) custom-call(f32[256,1536]{1,0:T(8,128)} %get-tuple-element.108.refs_, ...), custom_call_target="tpu_custom_call" | custom-call | flops 20000000000 | bytes 60000000 | tf_op jit(solution)/shard_map/attn_forward_kernel/pallas_call | solution.py:1236
  266.4 63.5 %mlp_forward_kernel.3 = (f32[256,1536]{1,0:T(8,128)}, bf16[4,256,1536]{2,1,0:T(8,128)(2,1)}, bf16[1024,2048]{1,0:T(8,128)(2,1)}, bf16[1024,1024]{1,0:T(8,128)(2,1)}, bf16[8,192,1024]{2,1,0:T(8,128)(2,1)}) custom-call(bf16[192,1024]{1,0:T(8,128)(2,1)} %get-tuple-element.98.refs_0_, bf16[192,1024]{1,0:T(8,128)(2,1)} %get-tuple-element.99.refs_8_.refs_1_, ...), custom_call_target="tpu_custom_call" | custom-call | flops 20000000000 | bytes 60000000 | tf_op jit(solution)/shard_map/mlp_forward_kernel/pallas_call | solution.py:1236
  330.0 59.4 %mlp_backward_kernel.2 = (f32[256,1536]{1,0:T(8,128)}, f32[8,1536]{1,0:T(8,128)}, bf16[8,192,2048]{2,1,0:T(8,128)(2,1)}, f32[192,1024]{1,0:T(8,128)}) custom-call(bf16[192,1024]{1,0:T(8,128)(2,1)} %get-tuple-element.98.refs_0_, bf16[192,1024]{1,0:T(8,128)(2,1)} %get-tuple-element.99.refs_8_.refs_1_, bf16[8,192,1024]{2,1,0:T(8,128)(2,1)} %get-tuple-element.114.refs_2_, ...), custom_call_target="tpu_custom_call" | custom-call | flops 20000000000 | bytes 60000000 | tf_op jit(solution)/shard_map/mlp_backward_kernel/pallas_call | solution.py:1236
  389.4 76.9 %attn_backward_kernel.2 = (f32[256,1536]{1,0:T(8,128)}, f32[8,1536]{1,0:T(8,128)}, bf16[8,192,1152]{2,1,0:T(8,128)(2,1)}, f32[192,2048]{1,0:T(8,128)}) custom-call(f32[256,1536]{1,0:T(8,128)} %get-tuple-element.124.refs_0_, f32[256,1536]{1,0:T(8,128)} %get-tuple-element.108.refs_0_.refs_1_, f32[16,1536]{1,0:T(8,128)} %get-tuple-element.106.refs_6_.refs_2_.refs_8_, ...), custom_call_target="tpu_custom_call" | custom-call | flops 20000000000 | bytes 60000000 | tf_op jit(solution)/shard_map/attn_backward_kernel/pallas_call | solution.py:1236
  466.3 83.4 %mlp_backward_kernel.3 = (f32[256,1536]{1,0:T(8,128)}, f32[8,1536]{1,0:T(8,128)}, bf16[8,192,2048]{2,1,0:T(8,128)(2,1)}, f32[192,1024]{1,0:T(8,128)}, f32[192,1152]{1,0:T(8,128)}) custom-call(bf16[192,1024]{1,0:T(8,128)(2,1)} %get-tuple-element.100.refs_0_, bf16[192,1024]{1,0:T(8,128)(2,1)} %get-tuple-element.101.refs_1_, ...), custom_call_target="tpu_custom_call" | custom-call | flops 20000000000 | bytes 60000000 | tf_op jit(solution)/shard_map/mlp_backward_kernel/pallas_call | solution.py:1236
  549.7 116.2 %attn_backward_kernel.3 = (f32[256,1536]{1,0:T(8,128)}, f32[8,1536]{1,0:T(8,128)}, f32[16,256]{1,0:T(8,128)}, f32[192,1152]{1,0:T(8,128)}, f32[192,2048]{1,0:T(8,128)}) custom-call(f32[256,1536]{1,0:T(8,128)} %get-tuple-element.138.refs_0_, f32[256,1536]{1,0:T(8,128)} %refs_1_.3, f32[16,1536]{1,0:T(8,128)} %get-tuple-element.106.refs_6_.refs_2_.refs_8_, ...), custom_call_target="tpu_custom_call" | custom-call | flops 20000000000 | bytes 60000000 | tf_op jit(solution)/shard_map/attn_backward_kernel/pallas_call | solution.py:1236
  665.9 1.4 fusion
  667.3 7.3 %unpack_kernel.1 = (f32[256,1536]{1,0:T(8,128)}, f32[256,1536]{1,0:T(8,128)}, f32[192,384]{1,0:T(8,128)}, f32[192,192]{1,0:T(8,128)}, f32[192,192]{1,0:T(8,128)}...) custom-call(f32[256,1536]{1,0:T(8,128)} %get-tuple-element.117.refs_, ...), custom_call_target="tpu_custom_call" | custom-call | flops 20000000000 | bytes 60000000 | tf_op jit(solution)/shard_map/unpack_kernel/pallas_call | solution.py:1236

commit v7 on v6

--- a/solution.py
+++ b/solution.py
@@ -1612,7 +1612,7 @@
     )
     back_attn2 = attn_backward(
         1, 5, back_mlp2.grad_out, mlp1.result, gains, tables, place, attn2, (attn_pack[1], attn2_blocks),
-        [back_mlp2.wide_out], [1, 0, 0, 1, 0, 1, 0, 0, 0, 1],
+        [back_mlp2.wide_out], [1, 0, 0, 1, 0, 0, 1, 0, 0, 1],
     )
     back_mlp1 = mlp_backward(
         0, 6, back_attn2.grad_out, attn1.middle, gains, mlp1, wide1, down1,

time: 685 us -> 685 us (level)
  no operation moved by 1% of the time
where the time goes in v7:
time: 685 us; the launch traced here: 675 us
  Pallas kernels  672 us (98%)
    pallas_call x9, Pallas kernels, launch(): pl.pallas_call(entry, out_shape=[shape for shape, _ in outs.values()], in...  672 us

profile of v7, /device:TPU:28, one launch (start us, length us, event | category | flops | bytes accessed | tf_op | source)
XLA Modules:
  0.0 674.8 jit_solution(9856170933589977059)
XLA Ops:
  0.7 113.6 %attn_forward_kernel.2 = (f32[256,1536]{1,0:T(8,128)}, bf16[4,256,1536]{2,1,0:T(8,128)(2,1)}, bf16[1024,1024]{1,0:T(8,128)(2,1)}, bf16[1024,384]{1,0:T(8,128)(2,...) custom-call(f32[256,1536]{1,0:T(8,128)} %refs_1_.3, ...), custom_call_target="tpu_custom_call" | custom-call | flops 20000000000 | bytes 60000000 | tf_op jit(solution)/shard_map/attn_forward_kernel/pallas_call | solution.py:1236
  114.3 81.8 %mlp_forward_kernel.2 = (f32[256,1536]{1,0:T(8,128)}, bf16[4,256,1536]{2,1,0:T(8,128)(2,1)}, bf16[1024,2048]{1,0:T(8,128)(2,1)}, bf16[1024,1024]{1,0:T(8,128)(2,...) custom-call(bf16[192,1024]{1,0:T(8,128)(2,1)} %get-tuple-element.100.refs_0_, ...), custom_call_target="tpu_custom_call" | custom-call | flops 20000000000 | bytes 60000000 | tf_op jit(solution)/shard_map/mlp_forward_kernel/pallas_call | solution.py:1236
  196.1 70.4 %attn_forward_kernel.3 = (f32[256,1536]{1,0:T(8,128)}, bf16[4,256,1536]{2,1,0:T(8,128)(2,1)}, bf16[1024,1024]{1,0:T(8,128)(2,1)}, bf16[1024,384]{1,0:T(8,128)(2,...) custom-call(f32[256,1536]{1,0:T(8,128)} %get-tuple-element.108.refs_, ...), custom_call_target="tpu_custom_call" | custom-call | flops 20000000000 | bytes 60000000 | tf_op jit(solution)/shard_map/attn_forward_kernel/pallas_call | solution.py:1236
  266.4 63.5 %mlp_forward_kernel.3 = (f32[256,1536]{1,0:T(8,128)}, bf16[4,256,1536]{2,1,0:T(8,128)(2,1)}, bf16[1024,2048]{1,0:T(8,128)(2,1)}, bf16[1024,1024]{1,0:T(8,128)(2,1)}, bf16[8,192,1024]{2,1,0:T(8,128)(2,1)}) custom-call(bf16[192,1024]{1,0:T(8,128)(2,1)} %get-tuple-element.98.refs_0_, bf16[192,1024]{1,0:T(8,128)(2,1)} %get-tuple-element.99.refs_8_.refs_1_, ...), custom_call_target="tpu_custom_call" | custom-call | flops 20000000000 | bytes 60000000 | tf_op jit(solution)/shard_map/mlp_forward_kernel/pallas_call | solution.py:1236
  330.0 59.4 %mlp_backward_kernel.2 = (f32[256,1536]{1,0:T(8,128)}, f32[8,1536]{1,0:T(8,128)}, bf16[8,192,2048]{2,1,0:T(8,128)(2,1)}, f32[192,1024]{1,0:T(8,128)}) custom-call(bf16[192,1024]{1,0:T(8,128)(2,1)} %get-tuple-element.98.refs_0_, bf16[192,1024]{1,0:T(8,128)(2,1)} %get-tuple-element.99.refs_8_.refs_1_, bf16[8,192,1024]{2,1,0:T(8,128)(2,1)} %get-tuple-element.114.refs_2_, ...), custom_call_target="tpu_custom_call" | custom-call | flops 20000000000 | bytes 60000000 | tf_op jit(solution)/shard_map/mlp_backward_kernel/pallas_call | solution.py:1236
  389.4 76.8 %attn_backward_kernel.2 = (f32[256,1536]{1,0:T(8,128)}, f32[8,1536]{1,0:T(8,128)}, bf16[8,192,1152]{2,1,0:T(8,128)(2,1)}, f32[192,2048]{1,0:T(8,128)}) custom-call(f32[256,1536]{1,0:T(8,128)} %get-tuple-element.124.refs_0_, f32[256,1536]{1,0:T(8,128)} %get-tuple-element.108.refs_0_.refs_1_, f32[16,1536]{1,0:T(8,128)} %get-tuple-element.106.refs_6_.refs_2_.refs_8_, ...), custom_call_target="tpu_custom_call" | custom-call | flops 20000000000 | bytes 60000000 | tf_op jit(solution)/shard_map/attn_backward_kernel/pallas_call | solution.py:1236
  466.2 83.5 %mlp_backward_kernel.3 = (f32[256,1536]{1,0:T(8,128)}, f32[8,1536]{1,0:T(8,128)}, bf16[8,192,2048]{2,1,0:T(8,128)(2,1)}, f32[192,1024]{1,0:T(8,128)}, f32[192,1152]{1,0:T(8,128)}) custom-call(bf16[192,1024]{1,0:T(8,128)(2,1)} %get-tuple-element.100.refs_0_, bf16[192,1024]{1,0:T(8,128)(2,1)} %get-tuple-element.101.refs_1_, ...), custom_call_target="tpu_custom_call" | custom-call | flops 20000000000 | bytes 60000000 | tf_op jit(solution)/shard_map/mlp_backward_kernel/pallas_call | solution.py:1236
  549.7 116.2 %attn_backward_kernel.3 = (f32[256,1536]{1,0:T(8,128)}, f32[8,1536]{1,0:T(8,128)}, f32[16,256]{1,0:T(8,128)}, f32[192,1152]{1,0:T(8,128)}, f32[192,2048]{1,0:T(8,128)}) custom-call(f32[256,1536]{1,0:T(8,128)} %get-tuple-element.138.refs_0_, f32[256,1536]{1,0:T(8,128)} %refs_1_.3, f32[16,1536]{1,0:T(8,128)} %get-tuple-element.106.refs_6_.refs_2_.refs_8_, ...), custom_call_target="tpu_custom_call" | custom-call | flops 20000000000 | bytes 60000000 | tf_op jit(solution)/shard_map/attn_backward_kernel/pallas_call | solution.py:1236
  665.9 1.4 fusion
  667.3 7.3 %unpack_kernel.1 = (f32[256,1536]{1,0:T(8,128)}, f32[256,1536]{1,0:T(8,128)}, f32[192,384]{1,0:T(8,128)}, f32[192,192]{1,0:T(8,128)}, f32[192,192]{1,0:T(8,128)}...) custom-call(f32[256,1536]{1,0:T(8,128)} %get-tuple-element.117.refs_, ...), custom_call_target="tpu_custom_call" | custom-call | flops 20000000000 | bytes 60000000 | tf_op jit(solution)/shard_map/unpack_kernel/pallas_call | solution.py:1236
